TPU v7x, 32 devices: a whole 2x2x4 slice. The times are simulated.
32 devices in a mesh: groups: 2 (over y), tensor: 4 (over z), dp: 2 (over x), query: 2 (over core).
Axes of the slice: x: 2, y: 2, z: 4, core: 2. Of those that a mesh axis runs over, the one named last changes fastest.
Arguments:
- inputs: bfloat16 [8, 512, 8192], P(('groups', 'dp', 'query'), None, 'tensor'), parts along dimension 0, may hold values from -6 to 6
- residual: bfloat16 [8, 512, 8192], P(('groups', 'dp', 'query'), 'tensor'), parts along dimension 0, may hold values from -4 to 4
- out_grad: bfloat16 [8, 512, 8192], P(('groups', 'dp', 'query'), 'tensor'), parts along dimension 0, may hold values from -6 to 6
- norm_gain: bfloat16 [8192], replicated, may hold values from 0.099609375 to 1.8984375
- w_out: bfloat16 [8192, 8192], P('tensor'), may hold values from -0.0625 to 0.0625
- proj_in: bfloat16 [64, 8192], P(None, 'tensor'), may hold values from -0.0625 to 0.0625
- proj_out: bfloat16 [64, 8192], replicated, may hold values from -0.0625 to 0.0625
- queries: bfloat16 [1024, 4096], P('query', 'tensor'), may hold values from -0.0078125 to 0.0078125
- segment_ids: int32 [8, 512], P(('groups', 'dp', 'query')), parts along dimension 0, may hold values from 0 to 3, never falling along the last dimension, each value on 1 to 256 neighbouring positions
Outputs:
- input_grad: bfloat16 [8, 512, 8192], P(('groups', 'dp', 'query'), None, 'tensor'), parts along dimension 0
- scores: float32 [32, 1024], P(('groups', 'dp'), 'query'), parts along dimension 0
There are 2 independent parts, one for each index of `groups`. A program takes and returns all parts, laid end to end along the dimension named above; an argument that names none is the same for every part. Nothing has to cross between parts.
Inputs may be any that keep to these rules, and one draw needn't show every extreme that they name: `segment_ids`: within each row of 512 tokens the example numbers never fall and every example number has at least one token.
All inputs are finite; a program needn't handle non-finite values.
Results may differ from a plain program's by a relative error of at most 0.015.
Values may be sent and summed in bfloat16 or wider, within the bound.
No kernel may reach another device: no remote copies, remote signals or barrier semaphores. Data moves between devices by JAX's collectives and lax.ppermute only.
A program may use at most 128 MiB of HBM per device.

v0:
```python
import functools

import jax
import jax.numpy as jnp
from jax import lax
from jax.experimental import pallas as pl
from jax.experimental.pallas import tpu as pltpu
from jax.sharding import PartitionSpec as P

EX_DEV = 4
EPS = 1e-05
CHUNKS = 2
HALVES = 2
PIECES = 2
SHORT, LONG = 0.2, 5.0
SMALL, LIMIT, LARGE = 6 * 1024 * 1024, 11 * 1024 * 1024, 24 * 1024 * 1024
QUARTERS = 4

F32, BF16 = jnp.float32, jnp.bfloat16
ANY = pl.BlockSpec(memory_space=pl.ANY)
TOKEN = jax.ShapeDtypeStruct((8, 128), F32)
TOKEN_SPEC = pl.BlockSpec((8, 128), lambda *_: (0, 0))


def divisor(total, wanted):
    size = min(total, wanted)
    while total % size:
        size //= 2
    return size


def cost(microseconds):
    return pl.CostEstimate(flops=0, bytes_accessed=int(microseconds * 3.6e6), transcendentals=0)


def in_hbm(x):
    return pltpu.with_memory_space_constraint(x, pltpu.HBM)


def project_rows(values, matrix):
    return lax.dot_general(
        values, matrix, (((1,), (1,)), ((), ())), preferred_element_type=F32
    )


def spread(values, first):
    k = values.shape[1]
    row = lax.broadcasted_iota(jnp.int32, (k, 2 * k), 0)
    col = lax.broadcasted_iota(jnp.int32, (k, 2 * k), 1)
    return jnp.dot(values, jnp.where(col == row + first, 1.0, 0.0).astype(BF16), preferred_element_type=F32)


def forward_extra(by_share, proj_in, chunk, held, after):
    parts, _, rows, depth = by_share.shape
    extra = 2 * proj_in.shape[0]
    at = held.shape[2] // extra - 1

    def kernel(x_ref, p_ref, *refs):
        part = project_rows(x_ref[...].reshape(parts * rows, depth), p_ref[...]).astype(BF16)
        refs[-1][...] = spread(part, 0).astype(BF16).reshape(parts, rows, extra)

    return pl.pallas_call(
        kernel,
        grid=(1,),
        in_specs=[
            pl.BlockSpec((parts, None, rows, depth), lambda i: (0, chunk, 0, 0)),
            pl.BlockSpec(proj_in.shape, lambda i: (0, 0)),
        ]
        + [ANY] * (1 + len(after)),
        out_specs=pl.BlockSpec((parts, rows, extra), lambda i: (0, 0, at)),
        out_shape=jax.ShapeDtypeStruct(held.shape, BF16),
        input_output_aliases={2: 0},
        compiler_params=pltpu.CompilerParams(vmem_limit_bytes=LIMIT),
        cost_estimate=cost(SHORT),
        name="forward_extra",
    )(by_share, proj_in, held, *after)


def forward_piece(by_share, w_out, chunk, halves, half_at, extra, piece, pieces, held, after):
    parts, _, rows, depth = by_share.shape
    half = w_out.shape[1] // halves
    span = half // pieces
    cols = divisor(span, 1024)
    steps = span // cols
    base = half_at * half + piece * span

    def kernel(x_ref, w_ref, *refs):
        out_ref, tok_ref, held_ref, sems = refs[-4:]
        i = pl.program_id(0)

        def copy(j):
            columns = pl.ds(base + j * cols, cols)
            return pltpu.make_async_copy(w_ref.at[:, columns], held_ref.at[j], sems.at[j])

        @pl.when(i == 0)
        def _():
            for j in range(steps):
                copy(j).start()

        for j in range(steps):

            @pl.when(i == j)
            def _():
                copy(j).wait()
                x = x_ref[...].reshape(parts * rows, depth)
                y = jnp.dot(x, held_ref[j], preferred_element_type=F32).astype(BF16)
                out_ref[...] = y.reshape(parts, rows, cols)

        tok_ref[...] = jnp.zeros_like(tok_ref)

    more = ([] if held is None else [held]) + after
    return pl.pallas_call(
        kernel,
        grid=(steps,),
        in_specs=[
            pl.BlockSpec(
                (parts, None, rows, depth), lambda i: (0, chunk, 0, 0), pipeline_mode=pl.Buffered(1)
            )
        ]
        + [ANY] * (1 + len(more)),
        out_specs=[
            pl.BlockSpec((parts, rows, cols), lambda i: (0, 0, piece * steps + i)),
            TOKEN_SPEC,
        ],
        out_shape=[jax.ShapeDtypeStruct((parts, rows, half + extra), BF16), TOKEN],
        scratch_shapes=[pltpu.VMEM((steps, depth, cols), BF16), pltpu.SemaphoreType.DMA((steps,))],
        input_output_aliases={} if held is None else {2: 0},
        compiler_params=pltpu.CompilerParams(vmem_limit_bytes=LARGE),
        cost_estimate=cost(SHORT),
        name="forward_piece",
    )(in_hbm(by_share), in_hbm(w_out), *more)


def load_weights(w_out, piece, pieces, after):
    rows = w_out.shape[0] // pieces
    width = w_out.shape[1]

    def kernel(w_ref, *refs):
        out_ref, sem = refs[-2:]
        copy = pltpu.make_async_copy(w_ref.at[pl.ds(piece * rows, rows)], out_ref, sem)
        copy.start()
        copy.wait()

    return pl.pallas_call(
        kernel,
        in_specs=[ANY] * (1 + len(after)),
        out_specs=pl.BlockSpec(memory_space=pltpu.VMEM),
        out_shape=pltpu.VMEM((rows, width), BF16),
        scratch_shapes=[pltpu.SemaphoreType.DMA],
        compiler_params=pltpu.CompilerParams(vmem_limit_bytes=SMALL),
        cost_estimate=cost(SHORT),
        name="load_weights",
    )(in_hbm(w_out), *after)


def backward_piece(blocks, weights, chunk, chunks, halves, piece, pieces, total, last, held, after):
    parts, rows, _ = blocks[0][1].shape
    some, width = weights[0].shape
    half, span = width // halves, some * len(weights)
    cols = divisor(some, 256)
    n, m = len(blocks), len(weights)

    def kernel(*refs):
        out_ref, tok_ref = refs[-2:]
        for j in range(m):

            def step(i, carry):
                here = pl.ds(pl.multiple_of(i * cols, cols), cols)
                there = pl.ds(pl.multiple_of(j * some + i * cols, cols), cols)
                y = None if total is None else refs[n + m][:, :, there].reshape(parts * rows, cols)
                for b, (at, _) in enumerate(blocks):
                    g = refs[b][...].reshape(parts * rows, half)
                    term = project_rows(g, refs[n + j][here, at * half : (at + 1) * half])
                    y = term if y is None else y + term
                out_ref[:, :, there] = y.astype(out_ref.dtype).reshape(parts, rows, cols)
                return carry

            lax.fori_loop(0, some // cols, step, 0)
        tok_ref[...] = jnp.zeros_like(tok_ref)

    once = pl.Buffered(1)
    here = pl.BlockSpec((parts, rows, span), lambda i: (0, 0, piece))
    if last:
        out_spec = pl.BlockSpec((parts, None, rows, span), lambda i: (0, chunk, 0, piece))
        out_shape = jax.ShapeDtypeStruct((parts, chunks, rows, span * pieces), BF16)
    else:
        out_spec, out_shape = here, jax.ShapeDtypeStruct((parts, rows, span * pieces), F32)
    sums = [] if total is None else [total]
    extra = ([] if held is None else [held]) + after
    return pl.pallas_call(
        kernel,
        grid=(1,),
        in_specs=[pl.BlockSpec((parts, rows, half), lambda i: (0, 0, 0), pipeline_mode=once)] * n
        + [pl.BlockSpec(memory_space=pltpu.VMEM)] * m
        + [pl.BlockSpec((parts, rows, span), lambda i: (0, 0, piece), pipeline_mode=once)] * len(sums)
        + [ANY] * len(extra),
        out_specs=[out_spec, TOKEN_SPEC],
        out_shape=[out_shape, TOKEN],
        input_output_aliases={} if held is None else {n + m + len(sums): 0},
        compiler_params=pltpu.CompilerParams(vmem_limit_bytes=LIMIT),
        cost_estimate=cost(SHORT),
        name="backward_piece",
    )(
        *[g for _, g in blocks],
        *[pltpu.with_memory_space_constraint(w, pltpu.VMEM) for w in weights],
        *sums,
        *extra,
    )


def relay(pos, flow, k, partial, came, held, after):
    rows, width = came.shape
    parts = (partial if held is None else held).shape[0]
    n_in = 1 + (partial is not None) + (held is not None) + len(after)

    def far(pos_ref, steps):
        way = pos_ref[1] if flow == 0 else -pos_ref[1]
        return lax.clamp(0, pos_ref[0] + way * steps, parts - 1)

    def kernel(pos_ref, *refs):
        came_ref, x_ref = refs[0], refs[n_in]
        place = pos_ref[2] if flow == 0 else parts - 1 - pos_ref[2]
        if held is not None:
            store = pltpu.make_async_copy(came_ref, refs[n_in + 1].at[far(pos_ref, -k)], refs[-1])
            pl.when(place >= k)(store.start)
        if partial is not None:

            @pl.when(place < k)
            def _():
                x_ref[...] = (came_ref[...].astype(F32) + refs[1][...].astype(F32)).astype(BF16)

            @pl.when(place >= k)
            def _():
                x_ref[...] = came_ref[...]

        else:
            x_ref[...] = came_ref[...]
        if held is not None:
            pl.when(place >= k)(store.wait)

    line = jax.ShapeDtypeStruct((rows, width), BF16)
    whole = pl.BlockSpec((rows, width), lambda i, w: (0, 0), pipeline_mode=pl.Buffered(1))
    args, specs, out_specs, out_shape, alias = [came], [whole], [whole], [line], {}
    if partial is not None:
        term = pl.BlockSpec(
            (None, rows, width),
            lambda i, w: (far(w, parts - k), 0, 0),
            pipeline_mode=pl.Buffered(1),
        )
        specs.append(term)
        args.append(partial)
    if held is not None:
        alias[1 + len(args)] = 1
        specs.append(ANY)
        args.append(held)
        out_specs.append(ANY)
        out_shape.append(jax.ShapeDtypeStruct(held.shape, BF16))
    outs = pl.pallas_call(
        kernel,
        grid_spec=pltpu.PrefetchScalarGridSpec(
            num_scalar_prefetch=1,
            grid=(1,),
            in_specs=specs + [ANY] * len(after),
            out_specs=out_specs,
            scratch_shapes=[pltpu.SemaphoreType.DMA] if held is not None else [],
        ),
        out_shape=out_shape,
        input_output_aliases=alias,
        compiler_params=pltpu.CompilerParams(vmem_limit_bytes=SMALL),
        cost_estimate=cost(LONG),
        name="relay",
    )(pos, *args, *after)
    return outs[0], (outs[1] if held is not None else None)


def store_last(pos, came, held, after):
    parts = held.shape[0]

    def kernel(pos_ref, a_ref, b_ref, *refs):
        out_ref, sem = refs[-2:]
        rank, way, place = pos_ref[0], pos_ref[1], pos_ref[2]
        ends = (
            (place == parts - 1, a_ref, rank - way * (parts - 1)),
            (place == 0, b_ref, rank + way * (parts - 1)),
        )
        for at_end, came_ref, at in ends:
            copy = pltpu.make_async_copy(came_ref, out_ref.at[lax.clamp(0, at, parts - 1)], sem)

            @pl.when(at_end)
            def _():
                copy.start()
                copy.wait()

    return pl.pallas_call(
        kernel,
        grid_spec=pltpu.PrefetchScalarGridSpec(
            num_scalar_prefetch=1,
            grid=(1,),
            in_specs=[pl.BlockSpec(held.shape[1:], lambda i, w: (0, 0))] * 2 + [ANY] * (1 + len(after)),
            out_specs=ANY,
            scratch_shapes=[pltpu.SemaphoreType.DMA],
        ),
        out_shape=jax.ShapeDtypeStruct(held.shape, BF16),
        input_output_aliases={3: 0},
        compiler_params=pltpu.CompilerParams(vmem_limit_bytes=SMALL),
        cost_estimate=cost(SHORT),
        name="store_last",
    )(pos, *came, held, *after)


def first_block(pos, flow, partial):
    parts, rows, width = partial.shape

    def there(i, w):
        way = w[1] if flow == 0 else -w[1]
        return lax.clamp(0, w[0] + way * (parts - 1), parts - 1), 0, 0

    def kernel(pos_ref, p_ref, out_ref):
        out_ref[...] = p_ref[...]

    return pl.pallas_call(
        kernel,
        grid_spec=pltpu.PrefetchScalarGridSpec(
            num_scalar_prefetch=1,
            grid=(1,),
            in_specs=[pl.BlockSpec((None, rows, width), there)],
            out_specs=pl.BlockSpec((rows, width), lambda i, w: (0, 0)),
        ),
        out_shape=jax.ShapeDtypeStruct((rows, width), BF16),
        compiler_params=pltpu.CompilerParams(vmem_limit_bytes=SMALL),
        cost_estimate=cost(SHORT),
        name="first_block",
    )(pos, partial)


def norm_terms(p_ref, a_ref, b_ref, res_ref, grad_ref, gain_ref, at):
    proj = p_ref[:, at].astype(F32) + a_ref[:, at].astype(F32) + b_ref[:, at].astype(F32)
    z = res_ref[:, at].astype(F32) + proj
    scaled = gain_ref[:, at].astype(F32) * grad_ref[:, at].astype(F32)
    return z, scaled


def norm_specs(ins, half, chunk, at):
    _, rows, wide = ins[0].shape
    once = pl.Buffered(1)
    whole = pl.BlockSpec((rows, wide), lambda i, r: (0, 0), pipeline_mode=once)
    own = pl.BlockSpec((None, rows, half), lambda i, r: (0, chunk, at), pipeline_mode=once)
    mine = pl.BlockSpec((None, rows, wide), lambda i, r: (r[0], 0, 0), pipeline_mode=once)
    return [mine, whole, whole, own, own, pl.BlockSpec((1, half), lambda i, r: (0, at))]


def norm_sums(pos, ins, half, chunk, at, sums, after):
    rows = ins[0].shape[1]
    cols = divisor(half, 1024)

    def kernel(pos_ref, *refs):
        square_ref, cross_ref = refs[-2:]

        def step(i, sums):
            z, scaled = norm_terms(*refs[:6], pl.ds(pl.multiple_of(i * cols, cols), cols))
            square, cross = sums
            for j in range(0, cols, 128):
                zj = z[:, j : j + 128]
                square = square + zj * zj
                cross = cross + zj * scaled[:, j : j + 128]
            return square, cross

        zero = jnp.zeros((rows, 128), F32)
        start = (zero, zero) if sums is None else (refs[6][...], refs[7][...])
        square_ref[...], cross_ref[...] = lax.fori_loop(0, half // cols, step, start)

    stat = pl.BlockSpec((rows, 128), lambda i, r: (0, 0))
    before = [] if sums is None else list(sums)
    return pl.pallas_call(
        kernel,
        grid_spec=pltpu.PrefetchScalarGridSpec(
            num_scalar_prefetch=1,
            grid=(1,),
            in_specs=norm_specs(ins, half, chunk, at) + [stat] * len(before) + [ANY] * len(after),
            out_specs=[stat, stat],
        ),
        out_shape=[jax.ShapeDtypeStruct((rows, 128), F32)] * 2,
        compiler_params=pltpu.CompilerParams(vmem_limit_bytes=LIMIT),
        cost_estimate=cost(LONG),
        name="norm_sums",
    )(pos, *ins, *before, *after)


def norm_out(pos, ins, half, chunk, sums, proj_out, after):
    parts, rows, wide = ins[0][1][0].shape
    cols = divisor(half, 1024)
    n, width = len(ins), ins[0][1][3].shape[2]
    with_b = proj_out

    def kernel(pos_ref, *refs):
        square_ref, cross_ref = refs[6 * n], refs[6 * n + 1]
        if with_b is None:
            out_ref, held_ref, sem = refs[-3:]
        else:
            out_ref, held_ref, rest_ref, sem = refs[-4:]
        inv = lax.rsqrt(jnp.sum(square_ref[...], axis=-1, keepdims=True) / width + EPS)
        slope = inv * inv * inv * (jnp.sum(cross_ref[...], axis=-1, keepdims=True) / width)
        for j in range(n):
            to_ref = out_ref if j == 0 else rest_ref.at[j - 1]

            def step(i, carry):
                here = pl.ds(pl.multiple_of(i * cols, cols), cols)
                z, scaled = norm_terms(*refs[6 * j : 6 * j + 6], here)
                to_ref[:, here] = (inv * scaled - z * slope).astype(BF16)
                return carry

            lax.fori_loop(0, half // cols, step, 0)
        if with_b is not None:
            p_ref = refs[6 * n + 2]
            b = project_rows(out_ref[:, :half], p_ref[:, :half])
            for j in range(1, n):
                b = b + project_rows(rest_ref[j - 1], p_ref[:, j * half : (j + 1) * half])
            a = sum(refs[j][:, half:].astype(F32) for j in range(3))
            out_ref[:, half:] = (a + spread(b.astype(BF16), b.shape[1])).astype(BF16)
        else:
            out_ref[:, half:] = jnp.zeros((rows, wide - half), BF16)
        own = pltpu.make_async_copy(out_ref, held_ref.at[pos_ref[0]], sem)
        own.start()
        own.wait()

    stat = pl.BlockSpec((rows, 128), lambda i, r: (0, 0))
    specs, args = [], []
    for at, one in ins:
        specs += norm_specs(one, half, chunk, at)
        args += one
    specs, args = specs + [stat, stat], args + list(sums)
    scratch = [pltpu.SemaphoreType.DMA]
    if with_b is not None:
        specs.append(pl.BlockSpec(proj_out.shape, lambda i, r: (0, 0)))
        args.append(proj_out)
        scratch = [pltpu.VMEM((max(1, n - 1), rows, half), BF16)] + scratch
    return pl.pallas_call(
        kernel,
        grid_spec=pltpu.PrefetchScalarGridSpec(
            num_scalar_prefetch=1,
            grid=(1,),
            in_specs=specs + [ANY] * len(after),
            out_specs=[pl.BlockSpec((rows, wide), lambda i, r: (0, 0)), ANY],
            scratch_shapes=scratch,
        ),
        out_shape=[
            jax.ShapeDtypeStruct((rows, wide), BF16),
            jax.ShapeDtypeStruct((parts, rows, wide), BF16),
        ],
        compiler_params=pltpu.CompilerParams(vmem_limit_bytes=LIMIT),
        cost_estimate=cost(SHORT),
        name="norm_out",
    )(pos, *args, *after)


def tie(value, after):
    def kernel(value_ref, *refs):
        refs[-1][...] = value_ref[...]

    whole = pl.BlockSpec(value.shape, lambda i: (0,) * value.ndim)
    return pl.pallas_call(
        kernel,
        grid=(1,),
        in_specs=[whole] + [ANY] * len(after),
        out_specs=whole,
        out_shape=jax.ShapeDtypeStruct(value.shape, value.dtype),
        compiler_params=pltpu.CompilerParams(vmem_limit_bytes=SMALL),
        cost_estimate=cost(SHORT),
        name="tie",
    )(value, *after)


def touch(x):
    def kernel(x_ref, out_ref):
        out_ref[...] = jnp.zeros_like(out_ref)

    return pl.pallas_call(
        kernel,
        grid=(1,),
        in_specs=[ANY],
        out_specs=TOKEN_SPEC,
        out_shape=TOKEN,
        compiler_params=pltpu.CompilerParams(vmem_limit_bytes=SMALL),
        cost_estimate=cost(SHORT),
        name="touch",
    )(x)


def from_others(value, axis, size):
    return [value] + [
        lax.ppermute(value, axis, [(d, (d + shift) % size) for d in range(size)])
        for shift in range(1, size)
    ]


def sketch_slice(pos, gathered, segment_ids, kp, after):
    parts, rows, wide = gathered[0].shape
    extra, mine = 2 * kp, kp // parts
    chunks, tokens = len(gathered), segment_ids.shape[1]

    def kernel(pos_ref, *refs):
        out_ref, sum_ref = refs[-2:]
        example = lax.broadcasted_iota(jnp.int32, (8, tokens), 0)
        by_row = jnp.where(refs[chunks][...] == example, 1.0, 0.0).astype(BF16)
        same = lax.broadcasted_iota(jnp.int32, (tokens, tokens), 0) == lax.broadcasted_iota(
            jnp.int32, (tokens, tokens), 1
        )
        weights = project_rows(jnp.where(same, 1.0, 0.0).astype(BF16), by_row)
        weights = weights.reshape(parts, chunks, rows, 8)
        for e in range(EX_DEV):
            total = None
            for c in range(chunks):
                both = refs[c][...].reshape(parts * rows, extra)
                weight = weights[:, c].reshape(parts * rows, 8)[:, e : e + 1]
                part = (both.astype(F32) * weight).astype(BF16)
                term = lax.dot_general(
                    part, both, (((0,), (0,)), ((), ())), preferred_element_type=F32
                )
                total = term if total is None else total + term
            sum_ref[e] = total
        low = lax.broadcasted_iota(jnp.int32, (1, extra), 1) < kp
        for r in range(parts):

            @pl.when(pos_ref[0] == r)
            def _():
                for e in range(EX_DEV):
                    for i in range(mine // 2):
                        at = kp + r * mine + 2 * i
                        left, right = sum_ref[e, at : at + 1, :], sum_ref[e, at + 1 : at + 2, :]
                        out_ref[e : e + 1, i * extra : (i + 1) * extra] = jnp.where(
                            low, left, pltpu.roll(right, kp, 1)
                        )

    return pl.pallas_call(
        kernel,
        grid_spec=pltpu.PrefetchScalarGridSpec(
            num_scalar_prefetch=1,
            grid=(1,),
            in_specs=[pl.BlockSpec((parts, rows, extra), lambda i, w: (0, 0, wide // extra - 1))] * chunks
            + [pl.BlockSpec(segment_ids.shape, lambda i, w: (0, 0))]
            + [ANY] * len(after),
            out_specs=pl.BlockSpec((EX_DEV, mine * kp), lambda i, w: (0, 0)),
            scratch_shapes=[pltpu.VMEM((EX_DEV, extra, extra), F32)],
        ),
        out_shape=jax.ShapeDtypeStruct((EX_DEV, mine * kp), F32),
        compiler_params=pltpu.CompilerParams(vmem_limit_bytes=LIMIT),
        cost_estimate=cost(SHORT),
        name="sketch_slice",
    )(pos, *gathered, segment_ids, *after)


def score_terms(pos, sketches, queries, after):
    size = len(sketches)
    n, depth = queries.shape

    def kernel(pos_ref, *refs):
        out_ref, all_ref = refs[-2:]
        for back in range(size):
            all_ref[lax.rem(pos_ref[3] - back + size, size)] = refs[back][...]
        for d in range(size):
            rest, total = all_ref[d], None
            for _ in range(3):
                part = rest.astype(BF16)
                rest = rest - part.astype(F32)
                term = project_rows(part, refs[size][...])
                total = term if total is None else total + term
            out_ref[d * EX_DEV : (d + 1) * EX_DEV, :] = total

    return pl.pallas_call(
        kernel,
        grid_spec=pltpu.PrefetchScalarGridSpec(
            num_scalar_prefetch=1,
            grid=(1,),
            in_specs=[pl.BlockSpec((EX_DEV, depth), lambda i, w: (0, 0))] * size
            + [pl.BlockSpec((n, depth), lambda i, w: (0, 0))]
            + [ANY] * len(after),
            out_specs=pl.BlockSpec((size * EX_DEV, n), lambda i, w: (0, 0)),
            scratch_shapes=[pltpu.VMEM((size, EX_DEV, depth), F32)],
        ),
        out_shape=jax.ShapeDtypeStruct((size * EX_DEV, n), F32),
        compiler_params=pltpu.CompilerParams(vmem_limit_bytes=LIMIT),
        cost_estimate=cost(SHORT),
        name="score_terms",
    )(pos, *sketches, queries, *after)


def score_sum(pos, terms, after):
    size = len(terms)
    shape = terms[0].shape

    def kernel(pos_ref, *refs):
        out_ref, all_ref = refs[-2:]
        for back in range(size):
            all_ref[lax.rem(pos_ref[0] - back + size, size)] = refs[back][...]
        total = all_ref[0]
        for d in range(1, size):
            total = total + all_ref[d]
        out_ref[...] = total

    whole = pl.BlockSpec(shape, lambda i, w: (0, 0))
    return pl.pallas_call(
        kernel,
        grid_spec=pltpu.PrefetchScalarGridSpec(
            num_scalar_prefetch=1,
            grid=(1,),
            in_specs=[whole] * size + [ANY] * len(after),
            out_specs=whole,
            scratch_shapes=[pltpu.VMEM((size,) + shape, F32)],
        ),
        out_shape=jax.ShapeDtypeStruct(shape, F32),
        compiler_params=pltpu.CompilerParams(vmem_limit_bytes=SMALL),
        cost_estimate=cost(SHORT),
        name="score_sum",
    )(pos, *terms, *after)


def body(inputs, residual, out_grad, norm_gain, w_out, proj_in, proj_out, queries, segment_ids):
    parts = lax.axis_size("tensor")
    rank = lax.axis_index("tensor")
    queriers = lax.axis_size("query")
    q_rank = lax.axis_index("query")
    tokens = inputs.shape[1]
    share = tokens // parts
    chunks = max(1, min(CHUNKS, share // 16))
    rows = share // chunks
    by_share = inputs.reshape(parts, chunks, rows, inputs.shape[2])
    gain = norm_gain.reshape(1, -1)
    half = w_out.shape[1] // HALVES
    kp = proj_out.shape[0]

    up = 1 - 2 * lax.rem(q_rank, 2)
    pos = jnp.stack([rank, up, jnp.where(up == 1, rank, parts - 1 - rank), q_rank]).astype(jnp.int32)

    def pairs(flow, low, high):
        out = []
        for q in range(queriers):
            way = 1 if (q % 2 == 0) == (flow == 0) else -1
            for t in range(parts):
                spot = t if way == 1 else parts - 1 - t
                if low <= spot <= min(high, parts - 2):
                    out.append((t * queriers + q, (t + way) * queriers + q))
        return out

    work, marks, resident = [], [], []
    partials, totals, result = {}, {}, [None]

    def forward(c, h, piece, pieces, after):
        partials[c, h], mark = forward_piece(
            by_share,
            w_out,
            c,
            HALVES,
            h,
            2 * kp,
            piece,
            pieces,
            partials.get((c, h)),
            after,
        )
        if h == 0 and piece == pieces - 1:
            partials[c, h] = forward_extra(by_share, proj_in, c, partials[c, h], [mark])
        return mark

    def backward(c, blocks, total, last, piece, pieces, after):
        held = result[0] if last else totals.get(c)
        some = resident[piece * QUARTERS // pieces : (piece + 1) * QUARTERS // pieces]
        done, mark = backward_piece(
            blocks, some, c, chunks, HALVES, piece, pieces, total, last, held, after
        )
        if last:
            result[0] = done
        else:
            totals[c] = done
        return mark

    def do_one(after, touching=False):
        if work:
            marks[:] = [work.pop(0)[1](after)]
        elif touching:
            marks[:] = [touch(after[0])]

    def finish(key, after):
        while any(k == key for k, _ in work):
            do_one(list(marks) + after)

    def load(count, after):
        for _ in range(count):
            resident.append(load_weights(w_out, len(resident), QUARTERS, after))
            after = [resident[-1]]
        marks[:] = after

    def add_forward(c, h, pieces):
        for piece in range(pieces):
            work.append(((c, h), functools.partial(forward, c, h, piece, pieces)))

    add_forward(0, 0, 1)
    finish((0, 0), [])
    gathered = []
    for slot in range(chunks + 1):
        rs, ag = slot < chunks, slot > 0
        came, held, sent, before = {}, {}, {}, None
        if ag:
            if slot == chunks:
                residual, out_grad, proj_out = in_hbm(residual), in_hbm(out_grad), in_hbm(proj_out)
            ins = [
                [partials[slot - 1, h], arrived[h, 0], arrived[h, 1], residual, out_grad, gain]
                for h in range(HALVES)
            ]
            sums = None
            for h in range(HALVES):
                sums = norm_sums(pos, ins[h], half, slot - 1, h, sums, list(marks))
            grad = [None] * HALVES
            grad[0], held[0] = norm_out(
                pos, list(enumerate(ins)), half, slot - 1, sums, proj_out, []
            )
        for k in range(parts):
            gather_now, reduce_now = ag and k <= parts - 2, rs and k >= 1
            if not gather_now and not reduce_now:
                continue
            for h in range(HALVES):
                if k == 0 and h > 0:
                    if rs and slot > 1:
                        add_forward(slot, h, PIECES)
                    do_one([sent[h - 1, 1]])
                    grad[h], held[h] = norm_out(
                        pos, [(h, ins[h])], half, slot - 1, sums, None, list(marks)
                    )
                if reduce_now:
                    if slot == 0 and k == 1 and h > 0:
                        add_forward(0, h, 1)
                        do_one([sent[h - 1, 1]])
                    finish((slot, h), [sent[h - 1, 1]] if h > 0 else [])
                for flow in range(2):
                    if k == 0:
                        x = before = grad[h]
                    elif (h, flow) not in came:
                        x = first_block(pos, flow, partials[slot, h])
                    else:
                        x, held[h] = relay(
                            pos,
                            flow,
                            k,
                            partials[slot, h] if reduce_now else None,
                            came[h, flow],
                            held.get(h),
                            list(marks) + ([] if before is None else [before]),
                        )
                        before = x
                    came[h, flow] = lax.ppermute(
                        x,
                        ("tensor", "query"),
                        pairs(flow, 0 if reduce_now else k, parts - 2 if gather_now else k - 1),
                    )
                    sent[h, flow] = x
                    if slot == chunks - 1 and flow == 1 and slot > 0:
                        if (k, h) == (parts - 2, HALVES - 1):
                            load(1, [x])
                            continue
                        if (k, h) == (parts - 1, HALVES - 1):
                            load(QUARTERS - len(resident), [x])
                            continue
                    if slot == 0 and k == 2 and (h, flow) == (HALVES - 1, 1) and chunks > 1 and HALVES > 1:
                        add_forward(1, 1, 2 * PIECES)
                        do_one([x])
                        continue
                    if slot == 0 and k == parts - 1 and (h, flow) == (0, 1):
                        do_one([x])
                        continue
                    if slot == 0 and k == parts - 1 and (h, flow) == (HALVES - 1, 1) and chunks > 1:
                        work.insert(0, ((1, 0), functools.partial(forward, 1, 0, 0, 1)))
                    if slot == 0 and work and work[0][0] == (1, 1):
                        continue
                    if k > 0 and (slot > 0 or k > 1) and not (slot == 1 and work and k == 1 and flow == 0):
                        if slot == chunks and flow == 0:
                            marks[:] = [touch(x)]
                        else:
                            do_one([x], slot == chunks)
                if k == 0 and slot == chunks and h == HALVES - 1:
                    marks[:] = [touch(sent[h, 1])]
        if ag:
            if slot + 1 < chunks:
                add_forward(slot + 1, 0, PIECES)
            if rs:
                blocks = [(h, held[h]) for h in range(HALVES)]
                for piece in range(PIECES):
                    work.append(
                        (
                            ("b", slot - 1),
                            functools.partial(backward, slot - 1, blocks, None, True, piece, PIECES),
                        )
                    )
            else:
                while work:
                    do_one(list(marks))
                marks[:] = [touch(came[0, 0])]
                held[0] = store_last(pos, (came[0, 0], came[0, 1]), held[0], list(marks))
            gathered.append(held[0])
        arrived = came
    last = chunks - 1
    sketch = sketch_slice(pos, gathered, segment_ids, kp, [])
    marks[:] = [backward(last, [(0, held[0])], None, HALVES == 1, 0, 1, [sketch])]
    for h in range(1, HALVES):
        marks[:] = [tie(marks[0], [came[h, 0]])]
        held[h] = store_last(pos, (came[h, 0], came[h, 1]), held[h], list(marks))
    terms = score_terms(pos, from_others(sketch, "query", queriers), queries, list(marks))
    for h in range(1, HALVES):
        marks[:] = [backward(last, [(h, held[h])], totals.get(last), h == HALVES - 1, 0, 1, [terms])]
    scores = score_sum(pos, from_others(terms, "tensor", parts), list(marks))
    return (result[0].reshape(1, tokens, -1), scores)


def solution(mesh):
    return jax.shard_map(
        body,
        mesh=mesh,
        in_specs=(
            P(("groups", "dp", "query"), None, "tensor"),
            P(("groups", "dp", "query"), "tensor", None),
            P(("groups", "dp", "query"), "tensor", None),
            P(),
            P("tensor", None),
            P(None, "tensor"),
            P(),
            P("query", "tensor"),
            P(("groups", "dp", "query"), None),
        ),
        out_specs=(P(("groups", "dp", "query"), None, "tensor"), P(("groups", "dp"), "query")),
        check_vma=False,
    )
```

profile of v0, /device:TPU:0, one launch (start us, length us, event | category | flops | bytes accessed | tf_op | source)
XLA Modules:
  0.0 296.6 jit_solution(1515340519862746985)
XLA Ops:
  0.7 9.0 %forward_piece.7 = (bf16[4,64,4224]{2,1,0:T(8,128)(2,1)S(1)}, f32[8,128]{1,0:T(8,128)S(1)}) custom-call(bf16[4,2,64,2048]{3,2,1,0:T(8,128)(2,1)} %bitcast.6, bf16[2048,8192]{1,0:T(8,128)(2,1)} %w_ref.21), custom_call_target="tpu_custom_call" | custom-call | bytes 720000 | tf_op jit(solution)/shard_map/forward_piece/pallas_call | solution.py:112
  10.9 5.0 %collective-permute-start.3 = (bf16[64,4224]{1,0:T(8,128)(2,1)S(1)}, bf16[64,4224]{1,0:T(8,128)(2,1)S(1)}, u32[]{:S(2)}, u32[]{:S(2)}) collective-permute-start(bf16[64,4224]{1,0:T(8,128)(2,1)S(1)} %first_block.7), channel_id=1, source_target_pairs={{0,4},{13,9},{2,6},{15,11},{16,20},{29,25},{18,22},{31,27}} | collective-permute-start | bytes 1622024 | tf_op jit(solution)/shard_map/ppermute | solution.py:749
  17.2 8.8 %forward_piece.8 = (bf16[4,64,4224]{2,1,0:T(8,128)(2,1)S(1)}, f32[8,128]{1,0:T(8,128)S(1)}) custom-call(bf16[4,2,64,2048]{3,2,1,0:T(8,128)(2,1)} %bitcast.7, bf16[2048,8192]{1,0:T(8,128)(2,1)} %w_ref.21, bf16[64,4224]{1,0:T(8,128)(2,1)S(1)} %first_block.4.refs_0_), custom_call_target="tpu_custom_call" | custom-call | bytes 720000 | tf_op jit(solution)/shard_map/forward_piece/pallas_call | solution.py:112
  34.8 5.6 %collective-permute-done.1.refs_0_ = bf16[64,4224]{1,0:T(8,128)(2,1)S(1)} collective-permute-done((bf16[64,4224]{1,0:T(8,128)(2,1)S(1)}, bf16[64,4224]{1,0:T(8,128)(2,1)S(1)}, u32[]{:S(2)}, u32[]{:S(2)}) %collective-permute-start.1) | collective-permute-done | bytes 540704 | tf_op jit(solution)/shard_map/ppermute | solution.py:749
  46.8 4.7 %forward_piece.9 = (bf16[4,64,4224]{2,1,0:T(8,128)(2,1)S(1)}, f32[8,128]{1,0:T(8,128)S(1)}) custom-call(bf16[4,2,64,2048]{3,2,1,0:T(8,128)(2,1)} %bitcast.8, bf16[2048,8192]{1,0:T(8,128)(2,1)} %w_ref.21, bf16[64,4224]{1,0:T(8,128)(2,1)S(1)} %relay.31.refs_0_.refs_3_), custom_call_target="tpu_custom_call" | custom-call | bytes 720000 | tf_op jit(solution)/shard_map/forward_piece/pallas_call | solution.py:112
  59.0 4.7 %forward_piece.10 = (bf16[4,64,4224]{2,1,0:T(8,128)(2,1)S(1)}, f32[8,128]{1,0:T(8,128)S(1)}) custom-call(bf16[4,2,64,2048]{3,2,1,0:T(8,128)(2,1)} %bitcast.9, bf16[2048,8192]{1,0:T(8,128)(2,1)} %w_ref.21, bf16[4,64,4224]{2,1,0:T(8,128)(2,1)S(1)} %get-tuple-element.84.refs_0_, bf16[64,4224]{1,0:T(8,128)(2,1)S(1)} %relay.33.refs_1_.refs_3_), custom_call_target="tpu_custom_call", output_to_operand_aliasing={{0}: (2, {})} | custom-call | bytes 720000 | tf_op jit(solution)/shard_map/forward_piece/pallas_call | solution.py:112
  66.6 5.3 %collective-permute-start.9 = (bf16[64,4224]{1,0:T(8,128)(2,1)S(1)}, bf16[64,4224]{1,0:T(8,128)(2,1)S(1)}, u32[]{:S(2)}, u32[]{:S(2)}) collective-permute-start(bf16[64,4224]{1,0:T(8,128)(2,1)S(1)} %relay.34.refs_3_), channel_id=1, source_target_pairs={{0,4},{4,8},{8,12},{5,1},{9,5},{13,9},{2,6},{6,10},{10,14},{7,3},{... | collective-permute-start | bytes 1622024 | tf_op jit(solution)/shard_map/ppermute | solution.py:749
  72.0 9.1 %forward_piece.11 = (bf16[4,64,4224]{2,1,0:T(8,128)(2,1)S(1)}, f32[8,128]{1,0:T(8,128)S(1)}) custom-call(bf16[4,2,64,2048]{3,2,1,0:T(8,128)(2,1)} %bitcast.10, bf16[2048,8192]{1,0:T(8,128)(2,1)} %w_ref.21, bf16[64,4224]{1,0:T(8,128)(2,1)S(1)} %relay.35.refs_0_), custom_call_target="tpu_custom_call" | custom-call | bytes 720000 | tf_op jit(solution)/shard_map/forward_piece/pallas_call | solution.py:112
  95.9 4.7 %forward_piece.12 = (bf16[4,64,4224]{2,1,0:T(8,128)(2,1)S(1)}, f32[8,128]{1,0:T(8,128)S(1)}) custom-call(bf16[4,2,64,2048]{3,2,1,0:T(8,128)(2,1)} %bitcast.11, bf16[2048,8192]{1,0:T(8,128)(2,1)} %w_ref.21, bf16[4,64,4224]{2,1,0:T(8,128)(2,1)S(1)} %get-tuple-element.86.refs_0_, ...), custom_call_target="tpu_custom_call", output_to_operand_aliasing={{0}: (2, {})} | custom-call | bytes 720000 | tf_op jit(solution)/shard_map/forward_piece/pallas_call | solution.py:112
  101.8 4.6 %collective-permute-start.14 = (bf16[64,4224]{1,0:T(8,128)(2,1)S(1)}, bf16[64,4224]{1,0:T(8,128)(2,1)S(1)}, u32[]{:S(2)}, u32[]{:S(2)}) collective-permute-start(bf16[64,4224]{1,0:T(8,128)(2,1)S(1)} %get-tuple-element.98.refs_4_), channel_id=1, source_target_pairs={{0,4},{4,8},{8,12},{5,1},{9,5},{13,9},{2,6},{6,10},{10,14},{7,3},{... | collective-permute-start | bytes 1622024 | tf_op jit(solution)/shard_map/ppermute | solution.py:749
  109.0 4.6 %collective-permute-start.18 = (bf16[64,4224]{1,0:T(8,128)(2,1)S(1)}, bf16[64,4224]{1,0:T(8,128)(2,1)S(1)}, u32[]{:S(2)}, u32[]{:S(2)}) collective-permute-start(bf16[64,4224]{1,0:T(8,128)(2,1)S(1)} %get-tuple-element.100.refs_4_), channel_id=1, source_target_pairs={{0,4},{4,8},{8,12},{5,1},{9,5},{13,9},{2,6},{6,10},{10,14},{7,3},{... | collective-permute-start | bytes 1622024 | tf_op jit(solution)/shard_map/ppermute | solution.py:749
  115.5 4.7 %forward_piece.13 = (bf16[4,64,4224]{2,1,0:T(8,128)(2,1)S(1)}, f32[8,128]{1,0:T(8,128)S(1)}) custom-call(bf16[4,2,64,2048]{3,2,1,0:T(8,128)(2,1)} %bitcast.12, bf16[2048,8192]{1,0:T(8,128)(2,1)} %w_ref.21, bf16[4,64,4224]{2,1,0:T(8,128)(2,1)S(1)} %get-tuple-element.94.refs_0_, ...), custom_call_target="tpu_custom_call", output_to_operand_aliasing={{0}: (2, {})} | custom-call | bytes 720000 | tf_op jit(solution)/shard_map/forward_piece/pallas_call | solution.py:112
  121.0 4.5 %collective-permute-start.15 = (bf16[64,4224]{1,0:T(8,128)(2,1)S(1)}, bf16[64,4224]{1,0:T(8,128)(2,1)S(1)}, u32[]{:S(2)}, u32[]{:S(2)}) collective-permute-start(bf16[64,4224]{1,0:T(8,128)(2,1)S(1)} %get-tuple-element.105.refs_4_), channel_id=1, source_target_pairs={{0,4},{4,8},{8,12},{5,1},{9,5},{13,9},{2,6},{6,10},{10,14},{7,3},{... | collective-permute-start | bytes 1622024 | tf_op jit(solution)/shard_map/ppermute | solution.py:749
  137.3 4.5 %collective-permute-done.15.refs_0_ = bf16[64,4224]{1,0:T(8,128)(2,1)S(1)} collective-permute-done((bf16[64,4224]{1,0:T(8,128)(2,1)S(1)}, bf16[64,4224]{1,0:T(8,128)(2,1)S(1)}, u32[]{:S(2)}, u32[]{:S(2)}) %collective-permute-start.15) | collective-permute-done | bytes 540704 | tf_op jit(solution)/shard_map/ppermute | solution.py:749
  160.4 4.5 %collective-permute-done.19.refs_0_ = bf16[64,4224]{1,0:T(8,128)(2,1)S(1)} collective-permute-done((bf16[64,4224]{1,0:T(8,128)(2,1)S(1)}, bf16[64,4224]{1,0:T(8,128)(2,1)S(1)}, u32[]{:S(2)}, u32[]{:S(2)}) %collective-permute-start.19) | collective-permute-done | bytes 540704 | tf_op jit(solution)/shard_map/ppermute | solution.py:749
  173.2 14.8 %collective-permute-start.23 = (bf16[64,4224]{1,0:T(8,128)(2,1)S(1)}, bf16[64,4224]{1,0:T(8,128)(2,1)S(1)}, u32[]{:S(2)}, u32[]{:S(2)}) collective-permute-start(bf16[64,4224]{1,0:T(8,128)(2,1)S(1)} %get-tuple-element.121.refs_4_), channel_id=1, source_target_pairs={{0,4},{4,8},{8,12},{5,1},{9,5},{13,9},{2,6},{6,10},{10,14},{7,3},{... | collective-permute-start | bytes 1622024 | tf_op jit(solution)/shard_map/ppermute | solution.py:749
  210.9 6.2 %backward_piece.4 = (bf16[4,2,64,2048]{3,2,1,0:T(8,128)(2,1)}, f32[8,128]{1,0:T(8,128)S(1)}) custom-call(bf16[4,64,4224]{2,1,0:T(8,128)(2,1)S(1)} %copy-done.3, bf16[4,64,4224]{2,1,0:T(8,128)(2,1)S(1)} %copy-done.7, bf16[512,8192]{1,0:T(8,128)(2,1)S(1)} %load_weights.4.refs_3_.refs_2_.refs_1_, bf16[512,8192]{1,0:T(8,128)(2,1)S(1)} %load_weights.5.refs_0_.refs_3_.refs_2_, ...), custom_call_target="tpu_custom_call" | custom-call | bytes 720000 | tf_op jit(solution)/shard_map/backward_piece/pallas_call | solution.py:190
  219.5 4.6 %collective-permute-start.28 = (bf16[64,4224]{1,0:T(8,128)(2,1)S(1)}, bf16[64,4224]{1,0:T(8,128)(2,1)S(1)}, u32[]{:S(2)}, u32[]{:S(2)}) collective-permute-start(bf16[64,4224]{1,0:T(8,128)(2,1)S(1)} %get-tuple-element.132.x_ref.refs_3_), channel_id=1, source_target_pairs={{0,4},{4,8},{8,12},{5,1},{9,5},{13,9},{2,6},{6,10},{10,14},{7,3},{... | collective-permute-start | bytes 1622024 | tf_op jit(solution)/shard_map/ppermute | solution.py:749
  228.7 6.2 %backward_piece.5 = (bf16[4,2,64,2048]{3,2,1,0:T(8,128)(2,1)}, f32[8,128]{1,0:T(8,128)S(1)}) custom-call(bf16[4,64,4224]{2,1,0:T(8,128)(2,1)S(1)} %copy-done.3, bf16[4,64,4224]{2,1,0:T(8,128)(2,1)S(1)} %copy-done.7, bf16[512,8192]{1,0:T(8,128)(2,1)S(1)} %load_weights.6.refs_0_.refs_2_.refs_3_, ...), custom_call_target="tpu_custom_call", output_to_operand_aliasing={{0}: (4, {})} | custom-call | bytes 720000 | tf_op jit(solution)/shard_map/backward_piece/pallas_call | solution.py:190
  242.8 6.9 %collective-permute-done.33.refs_0_ = bf16[64,4224]{1,0:T(8,128)(2,1)S(1)} collective-permute-done((bf16[64,4224]{1,0:T(8,128)(2,1)S(1)}, bf16[64,4224]{1,0:T(8,128)(2,1)S(1)}, u32[]{:S(2)}, u32[]{:S(2)}) %collective-permute-start.33) | collective-permute-done | bytes 540704 | tf_op jit(solution)/shard_map/ppermute | solution.py:749
  253.0 8.3 %collective-permute-done.36.refs_0_ = bf16[64,4224]{1,0:T(8,128)(2,1)S(1)} collective-permute-done((bf16[64,4224]{1,0:T(8,128)(2,1)S(1)}, bf16[64,4224]{1,0:T(8,128)(2,1)S(1)}, u32[]{:S(2)}, u32[]{:S(2)}) %collective-permute-start.36) | collective-permute-done | bytes 540704 | tf_op jit(solution)/shard_map/ppermute | solution.py:749
  263.3 9.6 %collective-permute-done.39.b_ref = bf16[64,4224]{1,0:T(8,128)(2,1)S(1)} collective-permute-done((bf16[64,4224]{1,0:T(8,128)(2,1)S(1)}, bf16[64,4224]{1,0:T(8,128)(2,1)S(1)}, u32[]{:S(2)}, u32[]{:S(2)}) %collective-permute-start.39) | collective-permute-done | bytes 540704 | tf_op jit(solution)/shard_map/ppermute | solution.py:749
  275.4 6.1 %backward_piece.6 = (f32[4,64,2048]{2,1,0:T(8,128)S(1)}, f32[8,128]{1,0:T(8,128)S(1)}) custom-call(bf16[4,64,4224]{2,1,0:T(8,128)(2,1)S(1)} %store_last.2.refs_1_.refs_0_, bf16[512,8192]{1,0:T(8,128)(2,1)S(1)} %load_weights.4.refs_3_.refs_2_.refs_1_, bf16[512,8192]{1,0:T(8,128)(2,1)S(1)} %load_weights.5.refs_0_.refs_3_.refs_2_, ...), custom_call_target="tpu_custom_call" | custom-call | bytes 720000 | tf_op jit(solution)/shard_map/backward_piece/pallas_call | solution.py:190
  288.2 7.1 %backward_piece.7 = (bf16[4,2,64,2048]{3,2,1,0:T(8,128)(2,1)}, f32[8,128]{1,0:T(8,128)S(1)}) custom-call(bf16[4,64,4224]{2,1,0:T(8,128)(2,1)S(1)} %store_last.3.refs_0_, bf16[512,8192]{1,0:T(8,128)(2,1)S(1)} %load_weights.4.refs_3_.refs_2_.refs_1_, bf16[512,8192]{1,0:T(8,128)(2,1)S(1)} %load_weights.5.refs_0_.refs_3_.refs_2_, ...), custom_call_target="tpu_custom_call", output_to_operand_aliasing={{0}: (6, {})} | custom-call | bytes 720000 | tf_op jit(solution)/shard_map/backward_piece/pallas_call | solution.py:190
  (163 shorter events, 140.6 us)
Async XLA Ops:
  29.9 22.0 %collective-permute-start.5 = (bf16[64,4224]{1,0:T(8,128)(2,1)S(1)}, bf16[64,4224]{1,0:T(8,128)(2,1)S(1)}, u32[]{:S(2)}, u32[]{:S(2)}) collective-permute-start(bf16[64,4224]{1,0:T(8,128)(2,1)S(1)} %relay.28.refs_3_), channel_id=1, source_target_pairs={{0,4},{4,8},{9,5},{13,9},{2,6},{6,10},{11,7},{15,11},{16,20},{20,2... | collective-permute-start | bytes 1622024 | tf_op jit(solution)/shard_map/ppermute | solution.py:749
  34.1 23.0 %collective-permute-start.4 = (bf16[64,4224]{1,0:T(8,128)(2,1)S(1)}, bf16[64,4224]{1,0:T(8,128)(2,1)S(1)}, u32[]{:S(2)}, u32[]{:S(2)}) collective-permute-start(bf16[64,4224]{1,0:T(8,128)(2,1)S(1)} %relay.29.refs_3_), channel_id=1, source_target_pairs={{8,4},{12,8},{1,5},{5,9},{10,6},{14,10},{3,7},{7,11},{24,20},{28,2... | collective-permute-start | bytes 1622024 | tf_op jit(solution)/shard_map/ppermute | solution.py:749
  41.1 22.6 %collective-permute-start.8 = (bf16[64,4224]{1,0:T(8,128)(2,1)S(1)}, bf16[64,4224]{1,0:T(8,128)(2,1)S(1)}, u32[]{:S(2)}, u32[]{:S(2)}) collective-permute-start(bf16[64,4224]{1,0:T(8,128)(2,1)S(1)} %relay.30.refs_3_), channel_id=1, source_target_pairs={{0,4},{4,8},{9,5},{13,9},{2,6},{6,10},{11,7},{15,11},{16,20},{20,2... | collective-permute-start | bytes 1622024 | tf_op jit(solution)/shard_map/ppermute | solution.py:749
  52.7 28.5 %collective-permute-start.6 = (bf16[64,4224]{1,0:T(8,128)(2,1)S(1)}, bf16[64,4224]{1,0:T(8,128)(2,1)S(1)}, u32[]{:S(2)}, u32[]{:S(2)}) collective-permute-start(bf16[64,4224]{1,0:T(8,128)(2,1)S(1)} %relay.32.refs_3_), channel_id=1, source_target_pairs={{0,4},{4,8},{8,12},{5,1},{9,5},{13,9},{2,6},{6,10},{10,14},{7,3},{... | collective-permute-start | bytes 1622024 | tf_op jit(solution)/shard_map/ppermute | solution.py:749
  57.7 23.4 %collective-permute-start.7 = (bf16[64,4224]{1,0:T(8,128)(2,1)S(1)}, bf16[64,4224]{1,0:T(8,128)(2,1)S(1)}, u32[]{:S(2)}, u32[]{:S(2)}) collective-permute-start(bf16[64,4224]{1,0:T(8,128)(2,1)S(1)} %relay.33.refs_1_.refs_3_), channel_id=1, source_target_pairs={{4,0},{8,4},{12,8},{1,5},{5,9},{9,13},{6,2},{10,6},{14,10},{3,7},{... | collective-permute-start | bytes 1622024 | tf_op jit(solution)/shard_map/ppermute | solution.py:749
  66.6 20.1 %collective-permute-start.9 = (bf16[64,4224]{1,0:T(8,128)(2,1)S(1)}, bf16[64,4224]{1,0:T(8,128)(2,1)S(1)}, u32[]{:S(2)}, u32[]{:S(2)}) collective-permute-start(bf16[64,4224]{1,0:T(8,128)(2,1)S(1)} %relay.34.refs_3_), channel_id=1, source_target_pairs={{0,4},{4,8},{8,12},{5,1},{9,5},{13,9},{2,6},{6,10},{10,14},{7,3},{... | collective-permute-start | bytes 1622024 | tf_op jit(solution)/shard_map/ppermute | solution.py:749
  109.0 21.2 %collective-permute-start.18 = (bf16[64,4224]{1,0:T(8,128)(2,1)S(1)}, bf16[64,4224]{1,0:T(8,128)(2,1)S(1)}, u32[]{:S(2)}, u32[]{:S(2)}) collective-permute-start(bf16[64,4224]{1,0:T(8,128)(2,1)S(1)} %get-tuple-element.100.refs_4_), channel_id=1, source_target_pairs={{0,4},{4,8},{8,12},{5,1},{9,5},{13,9},{2,6},{6,10},{10,14},{7,3},{... | collective-permute-start | bytes 1622024 | tf_op jit(solution)/shard_map/ppermute | solution.py:749
  114.2 21.1 %collective-permute-start.17 = (bf16[64,4224]{1,0:T(8,128)(2,1)S(1)}, bf16[64,4224]{1,0:T(8,128)(2,1)S(1)}, u32[]{:S(2)}, u32[]{:S(2)}) collective-permute-start(bf16[64,4224]{1,0:T(8,128)(2,1)S(1)} %get-tuple-element.101.refs_1_.refs_4_), channel_id=1, source_target_pairs={{4,0},{8,4},{12,8},{1,5},{5,9},{9,13},{6,2},{10,6},{14,10},{3,7},{... | collective-permute-start | bytes 1622024 | tf_op jit(solution)/shard_map/ppermute | solution.py:749
  121.0 20.8 %collective-permute-start.15 = (bf16[64,4224]{1,0:T(8,128)(2,1)S(1)}, bf16[64,4224]{1,0:T(8,128)(2,1)S(1)}, u32[]{:S(2)}, u32[]{:S(2)}) collective-permute-start(bf16[64,4224]{1,0:T(8,128)(2,1)S(1)} %get-tuple-element.105.refs_4_), channel_id=1, source_target_pairs={{0,4},{4,8},{8,12},{5,1},{9,5},{13,9},{2,6},{6,10},{10,14},{7,3},{... | collective-permute-start | bytes 1622024 | tf_op jit(solution)/shard_map/ppermute | solution.py:749
  126.2 20.7 %collective-permute-start.20 = (bf16[64,4224]{1,0:T(8,128)(2,1)S(1)}, bf16[64,4224]{1,0:T(8,128)(2,1)S(1)}, u32[]{:S(2)}, u32[]{:S(2)}) collective-permute-start(bf16[64,4224]{1,0:T(8,128)(2,1)S(1)} %get-tuple-element.109.refs_4_), channel_id=1, source_target_pairs={{4,0},{8,4},{12,8},{1,5},{5,9},{9,13},{6,2},{10,6},{14,10},{3,7},{... | collective-permute-start | bytes 1622024 | tf_op jit(solution)/shard_map/ppermute | solution.py:749
  130.9 22.5 %collective-permute-start.22 = (bf16[64,4224]{1,0:T(8,128)(2,1)S(1)}, bf16[64,4224]{1,0:T(8,128)(2,1)S(1)}, u32[]{:S(2)}, u32[]{:S(2)}) collective-permute-start(bf16[64,4224]{1,0:T(8,128)(2,1)S(1)} %get-tuple-element.111.refs_4_), channel_id=1, source_target_pairs={{0,4},{4,8},{8,12},{5,1},{9,5},{13,9},{2,6},{6,10},{10,14},{7,3},{... | collective-permute-start | bytes 1622024 | tf_op jit(solution)/shard_map/ppermute | solution.py:749
  136.0 22.5 %collective-permute-start.21 = (bf16[64,4224]{1,0:T(8,128)(2,1)S(1)}, bf16[64,4224]{1,0:T(8,128)(2,1)S(1)}, u32[]{:S(2)}, u32[]{:S(2)}) collective-permute-start(bf16[64,4224]{1,0:T(8,128)(2,1)S(1)} %get-tuple-element.112.refs_4_), channel_id=1, source_target_pairs={{4,0},{8,4},{12,8},{1,5},{5,9},{9,13},{6,2},{10,6},{14,10},{3,7},{... | collective-permute-start | bytes 1622024 | tf_op jit(solution)/shard_map/ppermute | solution.py:749
  142.4 22.5 %collective-permute-start.19 = (bf16[64,4224]{1,0:T(8,128)(2,1)S(1)}, bf16[64,4224]{1,0:T(8,128)(2,1)S(1)}, u32[]{:S(2)}, u32[]{:S(2)}) collective-permute-start(bf16[64,4224]{1,0:T(8,128)(2,1)S(1)} %get-tuple-element.113.refs_4_), channel_id=1, source_target_pairs={{0,4},{4,8},{8,12},{5,1},{9,5},{13,9},{2,6},{6,10},{10,14},{7,3},{... | collective-permute-start | bytes 1622024 | tf_op jit(solution)/shard_map/ppermute | solution.py:749
  147.5 22.3 %collective-permute-start.24 = (bf16[64,4224]{1,0:T(8,128)(2,1)S(1)}, bf16[64,4224]{1,0:T(8,128)(2,1)S(1)}, u32[]{:S(2)}, u32[]{:S(2)}) collective-permute-start(bf16[64,4224]{1,0:T(8,128)(2,1)S(1)} %get-tuple-element.116.refs_0_.refs_4_), channel_id=1, source_target_pairs={{4,0},{8,4},{12,8},{1,5},{5,9},{9,13},{6,2},{10,6},{14,10},{3,7},{... | collective-permute-start | bytes 1622024 | tf_op jit(solution)/shard_map/ppermute | solution.py:749
  154.0 44.1 %collective-permute-start.26 = (bf16[64,4224]{1,0:T(8,128)(2,1)S(1)}, bf16[64,4224]{1,0:T(8,128)(2,1)S(1)}, u32[]{:S(2)}, u32[]{:S(2)}) collective-permute-start(bf16[64,4224]{1,0:T(8,128)(2,1)S(1)} %get-tuple-element.119.refs_4_), channel_id=1, source_target_pairs={{0,4},{4,8},{8,12},{5,1},{9,5},{13,9},{2,6},{6,10},{10,14},{7,3},{... | collective-permute-start | bytes 1622024 | tf_op jit(solution)/shard_map/ppermute | solution.py:749
  159.1 39.0 %collective-permute-start.27 = (bf16[64,4224]{1,0:T(8,128)(2,1)S(1)}, bf16[64,4224]{1,0:T(8,128)(2,1)S(1)}, u32[]{:S(2)}, u32[]{:S(2)}) collective-permute-start(bf16[64,4224]{1,0:T(8,128)(2,1)S(1)} %get-tuple-element.120.refs_4_), channel_id=1, source_target_pairs={{4,0},{8,4},{12,8},{1,5},{5,9},{9,13},{6,2},{10,6},{14,10},{3,7},{... | collective-permute-start | bytes 1622024 | tf_op jit(solution)/shard_map/ppermute | solution.py:749
  171.9 28.6 %collective-permute-start.25 = (bf16[64,4224]{1,0:T(8,128)(2,1)S(1)}, bf16[64,4224]{1,0:T(8,128)(2,1)S(1)}, u32[]{:S(2)}, u32[]{:S(2)}) collective-permute-start(bf16[64,4224]{1,0:T(8,128)(2,1)S(1)} %get-tuple-element.123.refs_0_), channel_id=1, source_target_pairs={{4,0},{8,4},{12,8},{1,5},{5,9},{9,13},{6,2},{10,6},{14,10},{3,7},{... | collective-permute-start | bytes 1622024 | tf_op jit(solution)/shard_map/ppermute | solution.py:749
  173.2 27.3 %collective-permute-start.23 = (bf16[64,4224]{1,0:T(8,128)(2,1)S(1)}, bf16[64,4224]{1,0:T(8,128)(2,1)S(1)}, u32[]{:S(2)}, u32[]{:S(2)}) collective-permute-start(bf16[64,4224]{1,0:T(8,128)(2,1)S(1)} %get-tuple-element.121.refs_4_), channel_id=1, source_target_pairs={{0,4},{4,8},{8,12},{5,1},{9,5},{13,9},{2,6},{6,10},{10,14},{7,3},{... | collective-permute-start | bytes 1622024 | tf_op jit(solution)/shard_map/ppermute | solution.py:749
  227.4 22.3 %collective-permute-start.33 = (bf16[64,4224]{1,0:T(8,128)(2,1)S(1)}, bf16[64,4224]{1,0:T(8,128)(2,1)S(1)}, u32[]{:S(2)}, u32[]{:S(2)}) collective-permute-start(bf16[64,4224]{1,0:T(8,128)(2,1)S(1)} %get-tuple-element.138.refs_5_.refs_3_), channel_id=1, source_target_pairs={{4,0},{8,4},{5,9},{9,13},{6,2},{10,6},{7,11},{11,15},{20,16},{24,2... | collective-permute-start | bytes 1622024 | tf_op jit(solution)/shard_map/ppermute | solution.py:749
  240.1 21.2 %collective-permute-start.36 = (bf16[64,4224]{1,0:T(8,128)(2,1)S(1)}, bf16[64,4224]{1,0:T(8,128)(2,1)S(1)}, u32[]{:S(2)}, u32[]{:S(2)}) collective-permute-start(bf16[64,4224]{1,0:T(8,128)(2,1)S(1)} %get-tuple-element.144.x_ref.refs_3_), channel_id=1, source_target_pairs={{4,0},{8,4},{5,9},{9,13},{6,2},{10,6},{7,11},{11,15},{20,16},{24,2... | collective-permute-start | bytes 1622024 | tf_op jit(solution)/shard_map/ppermute | solution.py:749
  242.1 21.2 %collective-permute-start.38 = (bf16[64,4224]{1,0:T(8,128)(2,1)S(1)}, bf16[64,4224]{1,0:T(8,128)(2,1)S(1)}, u32[]{:S(2)}, u32[]{:S(2)}) collective-permute-start(bf16[64,4224]{1,0:T(8,128)(2,1)S(1)} %get-tuple-element.146.x_ref.refs_3_), channel_id=1, source_target_pairs={{8,12},{5,1},{10,14},{7,3},{24,28},{21,17},{26,30},{23,19}} | collective-permute-start | bytes 1622024 | tf_op jit(solution)/shard_map/ppermute | solution.py:749
  250.4 22.5 %collective-permute-start.39 = (bf16[64,4224]{1,0:T(8,128)(2,1)S(1)}, bf16[64,4224]{1,0:T(8,128)(2,1)S(1)}, u32[]{:S(2)}, u32[]{:S(2)}) collective-permute-start(bf16[64,4224]{1,0:T(8,128)(2,1)S(1)} %get-tuple-element.147.x_ref.refs_3_), channel_id=1, source_target_pairs={{4,0},{9,13},{6,2},{11,15},{20,16},{25,29},{22,18},{27,31}} | collective-permute-start | bytes 1622024 | tf_op jit(solution)/shard_map/ppermute | solution.py:749
  252.3 29.1 %collective-permute-start.35 = (bf16[64,4224]{1,0:T(8,128)(2,1)S(1)}, bf16[64,4224]{1,0:T(8,128)(2,1)S(1)}, u32[]{:S(2)}, u32[]{:S(2)}) collective-permute-start(bf16[64,4224]{1,0:T(8,128)(2,1)S(1)} %get-tuple-element.148.x_ref.refs_3_), channel_id=1, source_target_pairs={{8,12},{5,1},{10,14},{7,3},{24,28},{21,17},{26,30},{23,19}} | collective-permute-start | bytes 1622024 | tf_op jit(solution)/shard_map/ppermute | solution.py:749
  262.0 25.6 %collective-permute-start.37 = (bf16[64,4224]{1,0:T(8,128)(2,1)S(1)}, bf16[64,4224]{1,0:T(8,128)(2,1)S(1)}, u32[]{:S(2)}, u32[]{:S(2)}) collective-permute-start(bf16[64,4224]{1,0:T(8,128)(2,1)S(1)} %get-tuple-element.150), channel_id=1, source_target_pairs={{4,0},{9,13},{6,2},{11,15},{20,16},{25,29},{22,18},{27,31}} | collective-permute-start | bytes 1622024 | tf_op jit(solution)/shard_map/ppermute | solution.py:749
  (33 other events, 395.9 us)
where the time goes:
time: 302 us; the launch traced here: 297 us
  Pallas kernels  130 us (43%)
  starting transfers between devices  108 us (36%)
  waiting for transfers between devices  55.6 us (18%)
    ppermute x40, starting transfers between devices, body(): lax.ppermute(x, ('tensor', 'query'), pairs(flow, 0 if reduce_now else k,...  104 us
    ppermute x40, waiting for transfers between devices, body(): lax.ppermute(x, ('tensor', 'query'), pairs(flow, 0 if reduce_now else k,...  55.6 us
    pallas_call x7, Pallas kernels, forward_piece(): pl.pallas_call(kernel, grid=(steps,), in_specs=[pl.BlockSpec((parts, None...  45.7 us
    pallas_call x4, Pallas kernels, backward_piece(): pl.pallas_call(kernel, grid=(1,), in_specs=[pl.BlockSpec((parts, rows, ha...  25.5 us
    pallas_call x28, Pallas kernels, relay(): pl.pallas_call(kernel, grid_spec=pltpu.PrefetchScalarGridSpec(num_scalar_...  18.2 us
    pallas_call x4, Pallas kernels, load_weights(): pl.pallas_call(kernel, in_specs=[ANY] * (1 + len(after)), out_specs=pl.Bl...  13.6 us
    pallas_call x4, Pallas kernels, norm_out(): pl.pallas_call(kernel, grid_spec=pltpu.PrefetchScalarGridSpec(num_scalar_...  10.1 us
    pallas_call x4, Pallas kernels, norm_sums(): pl.pallas_call(kernel, grid_spec=pltpu.PrefetchScalarGridSpec(num_scalar_...  6.9 us
  transfers between devices with their start and end apart: 44, of which 12 were waited for; matrix products, arithmetic and copies ran while one was open for 0% of the time, Pallas kernels for 37%

commit v1 on v0

--- a/solution.py
+++ b/solution.py
@@ -13,7 +13,7 @@
 HALVES = 2
 PIECES = 2
 SHORT, LONG = 0.2, 5.0
-SMALL, LIMIT, LARGE = 6 * 1024 * 1024, 11 * 1024 * 1024, 24 * 1024 * 1024
+SMALL, LIMIT, LARGE = 5 * 1024 * 1024, 9 * 1024 * 1024, 24 * 1024 * 1024
 QUARTERS = 4
 
 F32, BF16 = jnp.float32, jnp.bfloat16
@@ -80,7 +80,7 @@
     parts, _, rows, depth = by_share.shape
     half = w_out.shape[1] // halves
     span = half // pieces
-    cols = divisor(span, 1024)
+    cols = divisor(span, max(256, span // 4))
     steps = span // cols
     base = half_at * half + piece * span
 
@@ -89,7 +89,7 @@
         i = pl.program_id(0)
 
         def copy(j):
-            columns = pl.ds(base + j * cols, cols)
+            columns = pl.ds(pl.multiple_of(base + j * cols, cols), cols)
             return pltpu.make_async_copy(w_ref.at[:, columns], held_ref.at[j], sems.at[j])
 
         @pl.when(i == 0)
@@ -97,15 +97,10 @@
             for j in range(steps):
                 copy(j).start()
 
-        for j in range(steps):
-
-            @pl.when(i == j)
-            def _():
-                copy(j).wait()
-                x = x_ref[...].reshape(parts * rows, depth)
-                y = jnp.dot(x, held_ref[j], preferred_element_type=F32).astype(BF16)
-                out_ref[...] = y.reshape(parts, rows, cols)
-
+        copy(i).wait()
+        x = x_ref[...].reshape(parts * rows, depth)
+        y = jnp.dot(x, held_ref[i], preferred_element_type=F32).astype(BF16)
+        out_ref[...] = y.reshape(parts, rows, cols)
         tok_ref[...] = jnp.zeros_like(tok_ref)
 
     more = ([] if held is None else [held]) + after
@@ -128,7 +123,7 @@
         compiler_params=pltpu.CompilerParams(vmem_limit_bytes=LARGE),
         cost_estimate=cost(SHORT),
         name="forward_piece",
-    )(in_hbm(by_share), in_hbm(w_out), *more)
+    )(in_hbm(by_share) if chunk == 0 and half_at == 0 else by_share, in_hbm(w_out), *more)
 
 
 def load_weights(w_out, piece, pieces, after):
@@ -151,6 +146,36 @@
         cost_estimate=cost(SHORT),
         name="load_weights",
     )(in_hbm(w_out), *after)
+
+
+def load_rows(residual, out_grad, chunk, rows, after):
+    width = residual.shape[2]
+
+    def kernel(*refs):
+        out_refs, sems = refs[-3:-1], refs[-1]
+        copies = [
+            pltpu.make_async_copy(refs[j].at[0, pl.ds(chunk * rows, rows)], out_refs[j], sems.at[j])
+            for j in range(2)
+        ]
+        for copy in copies:
+            copy.start()
+        for copy in copies:
+            copy.wait()
+
+    return pl.pallas_call(
+        kernel,
+        in_specs=[ANY] * (2 + len(after)),
+        out_specs=[pl.BlockSpec(memory_space=pltpu.VMEM)] * 2,
+        out_shape=[pltpu.VMEM((rows, width), BF16)] * 2,
+        scratch_shapes=[pltpu.SemaphoreType.DMA((2,))],
+        compiler_params=pltpu.CompilerParams(vmem_limit_bytes=SMALL),
+        cost_estimate=cost(SHORT),
+        name="load_rows",
+    )(in_hbm(residual), in_hbm(out_grad), *after)
+
+
+def in_vmem(x):
+    return pltpu.with_memory_space_constraint(x, pltpu.VMEM)
 
 
 def backward_piece(blocks, weights, chunk, chunks, halves, piece, pieces, total, last, held, after):
@@ -202,7 +227,7 @@
         name="backward_piece",
     )(
         *[g for _, g in blocks],
-        *[pltpu.with_memory_space_constraint(w, pltpu.VMEM) for w in weights],
+        *[in_vmem(w) for w in weights],
         *sums,
         *extra,
     )
@@ -344,7 +369,7 @@
     _, rows, wide = ins[0].shape
     once = pl.Buffered(1)
     whole = pl.BlockSpec((rows, wide), lambda i, r: (0, 0), pipeline_mode=once)
-    own = pl.BlockSpec((None, rows, half), lambda i, r: (0, chunk, at), pipeline_mode=once)
+    own = pl.BlockSpec((rows, half), lambda i, r: (0, at), pipeline_mode=once)
     mine = pl.BlockSpec((None, rows, wide), lambda i, r: (r[0], 0, 0), pipeline_mode=once)
     return [mine, whole, whole, own, own, pl.BlockSpec((1, half), lambda i, r: (0, at))]
 
@@ -389,7 +414,7 @@
 def norm_out(pos, ins, half, chunk, sums, proj_out, after):
     parts, rows, wide = ins[0][1][0].shape
     cols = divisor(half, 1024)
-    n, width = len(ins), ins[0][1][3].shape[2]
+    n, width = len(ins), ins[0][1][3].shape[1]
     with_b = proj_out
 
     def kernel(pos_ref, *refs):
@@ -431,7 +456,9 @@
     specs, args = specs + [stat, stat], args + list(sums)
     scratch = [pltpu.SemaphoreType.DMA]
     if with_b is not None:
-        specs.append(pl.BlockSpec(proj_out.shape, lambda i, r: (0, 0)))
+        specs.append(
+            pl.BlockSpec(proj_out.shape, lambda i, r: (0, 0), pipeline_mode=pl.Buffered(1))
+        )
         args.append(proj_out)
         scratch = [pltpu.VMEM((max(1, n - 1), rows, half), BF16)] + scratch
     return pl.pallas_call(
@@ -701,9 +728,10 @@
         came, held, sent, before = {}, {}, {}, None
         if ag:
             if slot == chunks:
-                residual, out_grad, proj_out = in_hbm(residual), in_hbm(out_grad), in_hbm(proj_out)
+                proj_out = in_hbm(proj_out)
+            res, grd = in_vmem(own_rows[0]), in_vmem(own_rows[1])
             ins = [
-                [partials[slot - 1, h], arrived[h, 0], arrived[h, 1], residual, out_grad, gain]
+                [partials[slot - 1, h], arrived[h, 0], arrived[h, 1], res, grd, gain]
                 for h in range(HALVES)
             ]
             sums = None
@@ -752,6 +780,9 @@
                         pairs(flow, 0 if reduce_now else k, parts - 2 if gather_now else k - 1),
                     )
                     sent[h, flow] = x
+                    if rs and (k, h, flow) == (parts - 1, HALVES - 1, 1):
+                        own_rows = load_rows(residual, out_grad, slot, rows, [x])
+                        x = own_rows[0]
                     if slot == chunks - 1 and flow == 1 and slot > 0:
                         if (k, h) == (parts - 2, HALVES - 1):
                             load(1, [x])

time: 302 us -> 287 us (0.950); the launches traced: 297 us -> 285 us
  starting transfers between devices: 108 us -> 97.7 us
  Pallas kernels: 130 us -> 124 us
  waiting for transfers between devices: 55.6 us -> 61.5 us
    ppermute x40, starting transfers between devices: 104 us -> 93.8 us  [body(): lax.ppermute(x, ('tensor', 'query'), pairs(flow, 0 if reduce_now else k,...]
    pallas_call x7, Pallas kernels: 45.7 us -> 37.4 us  [forward_piece(): pl.pallas_call(kernel, grid=(steps,), in_specs=[pl.BlockSpec((parts, None...]
    ppermute x40, waiting for transfers between devices: 55.6 us -> 61.5 us  [body(): lax.ppermute(x, ('tensor', 'query'), pairs(flow, 0 if reduce_now else k,...]
    pallas_call x0 -> x2, Pallas kernels: none -> 3.12 us  [load_rows(): pl.pallas_call(kernel, in_specs=[ANY] * (2 + len(after)), out_specs=[pl.B...]
    pallas_call x4, Pallas kernels: 13.6 us -> 16.6 us  [load_weights(): pl.pallas_call(kernel, in_specs=[ANY] * (1 + len(after)), out_specs=pl.Bl...]
  transfers between devices with their start and end apart: 44 -> 44, of which waited for: 12 -> 16; matrix products, arithmetic and copies ran while one was open for 0% -> 0% of each run, Pallas kernels for 37% -> 37%
where the time goes in v1:
time: 287 us; the launch traced here: 285 us
  Pallas kernels  124 us (43%)
  starting transfers between devices  97.7 us (34%)
  waiting for transfers between devices  61.5 us (21%)
    ppermute x40, starting transfers between devices, body(): lax.ppermute(x, ('tensor', 'query'), pairs(flow, 0 if reduce_now else k,...  93.8 us
    ppermute x40, waiting for transfers between devices, body(): lax.ppermute(x, ('tensor', 'query'), pairs(flow, 0 if reduce_now else k,...  61.5 us
    pallas_call x7, Pallas kernels, forward_piece(): pl.pallas_call(kernel, grid=(steps,), in_specs=[pl.BlockSpec((parts, None...  37.4 us
    pallas_call x4, Pallas kernels, backward_piece(): pl.pallas_call(kernel, grid=(1,), in_specs=[pl.BlockSpec((parts, rows, ha...  25.5 us
    pallas_call x28, Pallas kernels, relay(): pl.pallas_call(kernel, grid_spec=pltpu.PrefetchScalarGridSpec(num_scalar_...  18.4 us
    pallas_call x4, Pallas kernels, load_weights(): pl.pallas_call(kernel, in_specs=[ANY] * (1 + len(after)), out_specs=pl.Bl...  16.6 us
    pallas_call x4, Pallas kernels, norm_out(): pl.pallas_call(kernel, grid_spec=pltpu.PrefetchScalarGridSpec(num_scalar_...  8.41 us
  transfers between devices with their start and end apart: 44, of which 16 were waited for; matrix products, arithmetic and copies ran while one was open for 0% of the time, Pallas kernels for 37%

profile of v1, /device:TPU:0, one launch (start us, length us, event | category | flops | bytes accessed | tf_op | source)
XLA Modules:
  0.0 285.5 jit_solution(14994766107776836912)
XLA Ops:
  0.7 8.9 %forward_piece.7 = (bf16[4,64,4224]{2,1,0:T(8,128)(2,1)S(1)}, f32[8,128]{1,0:T(8,128)S(1)}) custom-call(bf16[4,2,64,2048]{3,2,1,0:T(8,128)(2,1)} %bitcast.8, bf16[2048,8192]{1,0:T(8,128)(2,1)} %w_ref.21), custom_call_target="tpu_custom_call" | custom-call | bytes 720000 | tf_op jit(solution)/shard_map/forward_piece/pallas_call | solution.py:107
  10.9 5.0 %collective-permute-start.3 = (bf16[64,4224]{1,0:T(8,128)(2,1)S(1)}, bf16[64,4224]{1,0:T(8,128)(2,1)S(1)}, u32[]{:S(2)}, u32[]{:S(2)}) collective-permute-start(bf16[64,4224]{1,0:T(8,128)(2,1)S(1)} %first_block.7), channel_id=1, source_target_pairs={{0,4},{13,9},{2,6},{15,11},{16,20},{29,25},{18,22},{31,27}} | collective-permute-start | bytes 1622024 | tf_op jit(solution)/shard_map/ppermute | solution.py:777
  17.1 7.6 %forward_piece.8 = (bf16[4,64,4224]{2,1,0:T(8,128)(2,1)S(1)}, f32[8,128]{1,0:T(8,128)S(1)}) custom-call(bf16[4,2,64,2048]{3,2,1,0:T(8,128)(2,1)S(1)} %bitcast.10, bf16[2048,8192]{1,0:T(8,128)(2,1)} %w_ref.21, bf16[64,4224]{1,0:T(8,128)(2,1)S(1)} %first_block.4.refs_0_), custom_call_target="tpu_custom_call" | custom-call | bytes 720000 | tf_op jit(solution)/shard_map/forward_piece/pallas_call | solution.py:107
  34.7 5.2 %collective-permute-done.1.refs_0_ = bf16[64,4224]{1,0:T(8,128)(2,1)S(1)} collective-permute-done((bf16[64,4224]{1,0:T(8,128)(2,1)S(1)}, bf16[64,4224]{1,0:T(8,128)(2,1)S(1)}, u32[]{:S(2)}, u32[]{:S(2)}) %collective-permute-start.1) | collective-permute-done | bytes 540704 | tf_op jit(solution)/shard_map/ppermute | solution.py:777
  40.6 4.4 %collective-permute-start.9 = (bf16[64,4224]{1,0:T(8,128)(2,1)S(1)}, bf16[64,4224]{1,0:T(8,128)(2,1)S(1)}, u32[]{:S(2)}, u32[]{:S(2)}) collective-permute-start(bf16[64,4224]{1,0:T(8,128)(2,1)S(1)} %relay.30.refs_3_), channel_id=1, source_target_pairs={{0,4},{4,8},{9,5},{13,9},{2,6},{6,10},{11,7},{15,11},{16,20},{20,2... | collective-permute-start | bytes 1622024 | tf_op jit(solution)/shard_map/ppermute | solution.py:777
  52.2 4.4 %collective-permute-start.6 = (bf16[64,4224]{1,0:T(8,128)(2,1)S(1)}, bf16[64,4224]{1,0:T(8,128)(2,1)S(1)}, u32[]{:S(2)}, u32[]{:S(2)}) collective-permute-start(bf16[64,4224]{1,0:T(8,128)(2,1)S(1)} %relay.32.refs_3_), channel_id=1, source_target_pairs={{0,4},{4,8},{8,12},{5,1},{9,5},{13,9},{2,6},{6,10},{10,14},{7,3},{... | collective-permute-start | bytes 1622024 | tf_op jit(solution)/shard_map/ppermute | solution.py:777
  65.7 5.2 %collective-permute-start.10 = (bf16[64,4224]{1,0:T(8,128)(2,1)S(1)}, bf16[64,4224]{1,0:T(8,128)(2,1)S(1)}, u32[]{:S(2)}, u32[]{:S(2)}) collective-permute-start(bf16[64,4224]{1,0:T(8,128)(2,1)S(1)} %relay.34.refs_3_), channel_id=1, source_target_pairs={{0,4},{4,8},{8,12},{5,1},{9,5},{13,9},{2,6},{6,10},{10,14},{7,3},{... | collective-permute-start | bytes 1622024 | tf_op jit(solution)/shard_map/ppermute | solution.py:777
  72.4 7.6 %forward_piece.11 = (bf16[4,64,4224]{2,1,0:T(8,128)(2,1)S(1)}, f32[8,128]{1,0:T(8,128)S(1)}) custom-call(bf16[4,2,64,2048]{3,2,1,0:T(8,128)(2,1)S(1)} %bitcast.13, bf16[2048,8192]{1,0:T(8,128)(2,1)} %w_ref.21, bf16[64,8192]{1,0:T(8,128)(2,1)S(1)} %get-tuple-element.92.refs_0_.refs_3_.refs_9_), custom_call_target="tpu_custom_call" | custom-call | bytes 720000 | tf_op jit(solution)/shard_map/forward_piece/pallas_call | solution.py:107
  81.3 5.0 %collective-permute-done.10.refs_1_.refs_7_ = bf16[64,4224]{1,0:T(8,128)(2,1)S(1)} collective-permute-done((bf16[64,4224]{1,0:T(8,128)(2,1)S(1)}, bf16[64,4224]{1,0:T(8,128)(2,1)S(1)}, u32[]{:S(2)}, u32[]{:S(2)}) %collective-permute-start.10) | collective-permute-done | bytes 540704 | tf_op jit(solution)/shard_map/ppermute | solution.py:777
  99.9 4.6 %collective-permute-start.14 = (bf16[64,4224]{1,0:T(8,128)(2,1)S(1)}, bf16[64,4224]{1,0:T(8,128)(2,1)S(1)}, u32[]{:S(2)}, u32[]{:S(2)}) collective-permute-start(bf16[64,4224]{1,0:T(8,128)(2,1)S(1)} %get-tuple-element.104.refs_4_), channel_id=1, source_target_pairs={{0,4},{4,8},{8,12},{5,1},{9,5},{13,9},{2,6},{6,10},{10,14},{7,3},{... | collective-permute-start | bytes 1622024 | tf_op jit(solution)/shard_map/ppermute | solution.py:777
  107.1 4.5 %collective-permute-start.18 = (bf16[64,4224]{1,0:T(8,128)(2,1)S(1)}, bf16[64,4224]{1,0:T(8,128)(2,1)S(1)}, u32[]{:S(2)}, u32[]{:S(2)}) collective-permute-start(bf16[64,4224]{1,0:T(8,128)(2,1)S(1)} %get-tuple-element.106.refs_4_), channel_id=1, source_target_pairs={{0,4},{4,8},{8,12},{5,1},{9,5},{13,9},{2,6},{6,10},{10,14},{7,3},{... | collective-permute-start | bytes 1622024 | tf_op jit(solution)/shard_map/ppermute | solution.py:777
  135.9 4.5 %collective-permute-done.15.refs_0_ = bf16[64,4224]{1,0:T(8,128)(2,1)S(1)} collective-permute-done((bf16[64,4224]{1,0:T(8,128)(2,1)S(1)}, bf16[64,4224]{1,0:T(8,128)(2,1)S(1)}, u32[]{:S(2)}, u32[]{:S(2)}) %collective-permute-start.15) | collective-permute-done | bytes 540704 | tf_op jit(solution)/shard_map/ppermute | solution.py:777
  152.7 4.4 %collective-permute-start.26 = (bf16[64,4224]{1,0:T(8,128)(2,1)S(1)}, bf16[64,4224]{1,0:T(8,128)(2,1)S(1)}, u32[]{:S(2)}, u32[]{:S(2)}) collective-permute-start(bf16[64,4224]{1,0:T(8,128)(2,1)S(1)} %get-tuple-element.125.refs_4_), channel_id=1, source_target_pairs={{0,4},{4,8},{8,12},{5,1},{9,5},{13,9},{2,6},{6,10},{10,14},{7,3},{... | collective-permute-start | bytes 1622024 | tf_op jit(solution)/shard_map/ppermute | solution.py:777
  159.1 4.5 %collective-permute-done.19.refs_0_ = bf16[64,4224]{1,0:T(8,128)(2,1)S(1)} collective-permute-done((bf16[64,4224]{1,0:T(8,128)(2,1)S(1)}, bf16[64,4224]{1,0:T(8,128)(2,1)S(1)}, u32[]{:S(2)}, u32[]{:S(2)}) %collective-permute-start.19) | collective-permute-done | bytes 540704 | tf_op jit(solution)/shard_map/ppermute | solution.py:777
  169.9 4.6 %collective-permute-start.23 = (bf16[64,4224]{1,0:T(8,128)(2,1)S(1)}, bf16[64,4224]{1,0:T(8,128)(2,1)S(1)}, u32[]{:S(2)}, u32[]{:S(2)}) collective-permute-start(bf16[64,4224]{1,0:T(8,128)(2,1)S(1)} %get-tuple-element.127.refs_4_), channel_id=1, source_target_pairs={{0,4},{4,8},{8,12},{5,1},{9,5},{13,9},{2,6},{6,10},{10,14},{7,3},{... | collective-permute-start | bytes 1622024 | tf_op jit(solution)/shard_map/ppermute | solution.py:777
  182.9 6.4 %load_weights.7.refs_6_.refs_8_.refs_3_.refs_4_ = bf16[512,8192]{1,0:T(8,128)(2,1)S(1)} custom-call(bf16[2048,8192]{1,0:T(8,128)(2,1)} %w_ref.21, bf16[512,8192]{1,0:T(8,128)(2,1)S(1)} %load_weights.6.refs_0_.refs_2_.refs_3_), custom_call_target="tpu_custom_call" | custom-call | bytes 720000 | tf_op jit(solution)/shard_map/load_weights/pallas_call | solution.py:139
  199.4 6.2 %backward_piece.4 = (bf16[4,2,64,2048]{3,2,1,0:T(8,128)(2,1)}, f32[8,128]{1,0:T(8,128)S(1)}) custom-call(bf16[4,64,4224]{2,1,0:T(8,128)(2,1)S(1)} %get-tuple-element.136.refs_0_, bf16[4,64,4224]{2,1,0:T(8,128)(2,1)S(1)} %get-tuple-element.137.refs_1_, bf16[512,8192]{1,0:T(8,128)(2,1)S(1)} %load_weights.4.refs_3_.refs_2_.refs_1_, ...), custom_call_target="tpu_custom_call" | custom-call | bytes 720000 | tf_op jit(solution)/shard_map/backward_piece/pallas_call | solution.py:215
  206.8 4.6 %collective-permute-start.28 = (bf16[64,4224]{1,0:T(8,128)(2,1)S(1)}, bf16[64,4224]{1,0:T(8,128)(2,1)S(1)}, u32[]{:S(2)}, u32[]{:S(2)}) collective-permute-start(bf16[64,4224]{1,0:T(8,128)(2,1)S(1)} %get-tuple-element.140.x_ref.refs_3_), channel_id=1, source_target_pairs={{0,4},{4,8},{8,12},{5,1},{9,5},{13,9},{2,6},{6,10},{10,14},{7,3},{... | collective-permute-start | bytes 1622024 | tf_op jit(solution)/shard_map/ppermute | solution.py:777
  216.0 6.2 %backward_piece.5 = (bf16[4,2,64,2048]{3,2,1,0:T(8,128)(2,1)}, f32[8,128]{1,0:T(8,128)S(1)}) custom-call(bf16[4,64,4224]{2,1,0:T(8,128)(2,1)S(1)} %get-tuple-element.136.refs_0_, bf16[4,64,4224]{2,1,0:T(8,128)(2,1)S(1)} %get-tuple-element.137.refs_1_, bf16[512,8192]{1,0:T(8,128)(2,1)S(1)} %bitcast.7, ...), custom_call_target="tpu_custom_call", output_to_operand_aliasing={{0}: (4, {})} | custom-call | bytes 720000 | tf_op jit(solution)/shard_map/backward_piece/pallas_call | solution.py:215
  231.6 6.9 %collective-permute-done.33.refs_0_ = bf16[64,4224]{1,0:T(8,128)(2,1)S(1)} collective-permute-done((bf16[64,4224]{1,0:T(8,128)(2,1)S(1)}, bf16[64,4224]{1,0:T(8,128)(2,1)S(1)}, u32[]{:S(2)}, u32[]{:S(2)}) %collective-permute-start.33) | collective-permute-done | bytes 540704 | tf_op jit(solution)/shard_map/ppermute | solution.py:777
  241.8 8.3 %collective-permute-done.36.refs_0_ = bf16[64,4224]{1,0:T(8,128)(2,1)S(1)} collective-permute-done((bf16[64,4224]{1,0:T(8,128)(2,1)S(1)}, bf16[64,4224]{1,0:T(8,128)(2,1)S(1)}, u32[]{:S(2)}, u32[]{:S(2)}) %collective-permute-start.36) | collective-permute-done | bytes 540704 | tf_op jit(solution)/shard_map/ppermute | solution.py:777
  252.1 9.6 %collective-permute-done.39.b_ref = bf16[64,4224]{1,0:T(8,128)(2,1)S(1)} collective-permute-done((bf16[64,4224]{1,0:T(8,128)(2,1)S(1)}, bf16[64,4224]{1,0:T(8,128)(2,1)S(1)}, u32[]{:S(2)}, u32[]{:S(2)}) %collective-permute-start.39) | collective-permute-done | bytes 540704 | tf_op jit(solution)/shard_map/ppermute | solution.py:777
  264.4 6.1 %backward_piece.6 = (f32[4,64,2048]{2,1,0:T(8,128)S(1)}, f32[8,128]{1,0:T(8,128)S(1)}) custom-call(bf16[4,64,4224]{2,1,0:T(8,128)(2,1)S(1)} %store_last.2.refs_1_.refs_0_, bf16[512,8192]{1,0:T(8,128)(2,1)S(1)} %load_weights.4.refs_3_.refs_2_.refs_1_, bf16[512,8192]{1,0:T(8,128)(2,1)S(1)} %load_weights.5.refs_0_.refs_3_.refs_2_, ...), custom_call_target="tpu_custom_call" | custom-call | bytes 720000 | tf_op jit(solution)/shard_map/backward_piece/pallas_call | solution.py:215
  277.2 7.1 %backward_piece.7 = (bf16[4,2,64,2048]{3,2,1,0:T(8,128)(2,1)}, f32[8,128]{1,0:T(8,128)S(1)}) custom-call(bf16[4,64,4224]{2,1,0:T(8,128)(2,1)S(1)} %store_last.3.refs_0_, bf16[512,8192]{1,0:T(8,128)(2,1)S(1)} %load_weights.4.refs_3_.refs_2_.refs_1_, bf16[512,8192]{1,0:T(8,128)(2,1)S(1)} %load_weights.5.refs_0_.refs_3_.refs_2_, ...), custom_call_target="tpu_custom_call", output_to_operand_aliasing={{0}: (6, {})} | custom-call | bytes 720000 | tf_op jit(solution)/shard_map/backward_piece/pallas_call | solution.py:215
  (158 shorter events, 142.0 us)
Async XLA Ops:
  29.0 22.5 %collective-permute-start.5 = (bf16[64,4224]{1,0:T(8,128)(2,1)S(1)}, bf16[64,4224]{1,0:T(8,128)(2,1)S(1)}, u32[]{:S(2)}, u32[]{:S(2)}) collective-permute-start(bf16[64,4224]{1,0:T(8,128)(2,1)S(1)} %relay.28.refs_3_), channel_id=1, source_target_pairs={{0,4},{4,8},{9,5},{13,9},{2,6},{6,10},{11,7},{15,11},{16,20},{20,2... | collective-permute-start | bytes 1622024 | tf_op jit(solution)/shard_map/ppermute | solution.py:777
  34.0 22.6 %collective-permute-start.4 = (bf16[64,4224]{1,0:T(8,128)(2,1)S(1)}, bf16[64,4224]{1,0:T(8,128)(2,1)S(1)}, u32[]{:S(2)}, u32[]{:S(2)}) collective-permute-start(bf16[64,4224]{1,0:T(8,128)(2,1)S(1)} %relay.29.refs_3_), channel_id=1, source_target_pairs={{8,4},{12,8},{1,5},{5,9},{10,6},{14,10},{3,7},{7,11},{24,20},{28,2... | collective-permute-start | bytes 1622024 | tf_op jit(solution)/shard_map/ppermute | solution.py:777
  40.6 22.5 %collective-permute-start.9 = (bf16[64,4224]{1,0:T(8,128)(2,1)S(1)}, bf16[64,4224]{1,0:T(8,128)(2,1)S(1)}, u32[]{:S(2)}, u32[]{:S(2)}) collective-permute-start(bf16[64,4224]{1,0:T(8,128)(2,1)S(1)} %relay.30.refs_3_), channel_id=1, source_target_pairs={{0,4},{4,8},{9,5},{13,9},{2,6},{6,10},{11,7},{15,11},{16,20},{20,2... | collective-permute-start | bytes 1622024 | tf_op jit(solution)/shard_map/ppermute | solution.py:777
  52.2 27.9 %collective-permute-start.6 = (bf16[64,4224]{1,0:T(8,128)(2,1)S(1)}, bf16[64,4224]{1,0:T(8,128)(2,1)S(1)}, u32[]{:S(2)}, u32[]{:S(2)}) collective-permute-start(bf16[64,4224]{1,0:T(8,128)(2,1)S(1)} %relay.32.refs_3_), channel_id=1, source_target_pairs={{0,4},{4,8},{8,12},{5,1},{9,5},{13,9},{2,6},{6,10},{10,14},{7,3},{... | collective-permute-start | bytes 1622024 | tf_op jit(solution)/shard_map/ppermute | solution.py:777
  57.2 22.9 %collective-permute-start.7 = (bf16[64,4224]{1,0:T(8,128)(2,1)S(1)}, bf16[64,4224]{1,0:T(8,128)(2,1)S(1)}, u32[]{:S(2)}, u32[]{:S(2)}) collective-permute-start(bf16[64,4224]{1,0:T(8,128)(2,1)S(1)} %relay.33.refs_1_.refs_3_), channel_id=1, source_target_pairs={{4,0},{8,4},{12,8},{1,5},{5,9},{9,13},{6,2},{10,6},{14,10},{3,7},{... | collective-permute-start | bytes 1622024 | tf_op jit(solution)/shard_map/ppermute | solution.py:777
  65.7 20.6 %collective-permute-start.10 = (bf16[64,4224]{1,0:T(8,128)(2,1)S(1)}, bf16[64,4224]{1,0:T(8,128)(2,1)S(1)}, u32[]{:S(2)}, u32[]{:S(2)}) collective-permute-start(bf16[64,4224]{1,0:T(8,128)(2,1)S(1)} %relay.34.refs_3_), channel_id=1, source_target_pairs={{0,4},{4,8},{8,12},{5,1},{9,5},{13,9},{2,6},{6,10},{10,14},{7,3},{... | collective-permute-start | bytes 1622024 | tf_op jit(solution)/shard_map/ppermute | solution.py:777
  107.1 21.7 %collective-permute-start.18 = (bf16[64,4224]{1,0:T(8,128)(2,1)S(1)}, bf16[64,4224]{1,0:T(8,128)(2,1)S(1)}, u32[]{:S(2)}, u32[]{:S(2)}) collective-permute-start(bf16[64,4224]{1,0:T(8,128)(2,1)S(1)} %get-tuple-element.106.refs_4_), channel_id=1, source_target_pairs={{0,4},{4,8},{8,12},{5,1},{9,5},{13,9},{2,6},{6,10},{10,14},{7,3},{... | collective-permute-start | bytes 1622024 | tf_op jit(solution)/shard_map/ppermute | solution.py:777
  112.3 21.6 %collective-permute-start.17 = (bf16[64,4224]{1,0:T(8,128)(2,1)S(1)}, bf16[64,4224]{1,0:T(8,128)(2,1)S(1)}, u32[]{:S(2)}, u32[]{:S(2)}) collective-permute-start(bf16[64,4224]{1,0:T(8,128)(2,1)S(1)} %get-tuple-element.107.refs_1_.refs_4_), channel_id=1, source_target_pairs={{4,0},{8,4},{12,8},{1,5},{5,9},{9,13},{6,2},{10,6},{14,10},{3,7},{... | collective-permute-start | bytes 1622024 | tf_op jit(solution)/shard_map/ppermute | solution.py:777
  118.1 22.3 %collective-permute-start.15 = (bf16[64,4224]{1,0:T(8,128)(2,1)S(1)}, bf16[64,4224]{1,0:T(8,128)(2,1)S(1)}, u32[]{:S(2)}, u32[]{:S(2)}) collective-permute-start(bf16[64,4224]{1,0:T(8,128)(2,1)S(1)} %get-tuple-element.111.refs_4_), channel_id=1, source_target_pairs={{0,4},{4,8},{8,12},{5,1},{9,5},{13,9},{2,6},{6,10},{10,14},{7,3},{... | collective-permute-start | bytes 1622024 | tf_op jit(solution)/shard_map/ppermute | solution.py:777
  123.2 22.4 %collective-permute-start.20 = (bf16[64,4224]{1,0:T(8,128)(2,1)S(1)}, bf16[64,4224]{1,0:T(8,128)(2,1)S(1)}, u32[]{:S(2)}, u32[]{:S(2)}) collective-permute-start(bf16[64,4224]{1,0:T(8,128)(2,1)S(1)} %get-tuple-element.115.refs_4_), channel_id=1, source_target_pairs={{4,0},{8,4},{12,8},{1,5},{5,9},{9,13},{6,2},{10,6},{14,10},{3,7},{... | collective-permute-start | bytes 1622024 | tf_op jit(solution)/shard_map/ppermute | solution.py:777
  129.5 22.5 %collective-permute-start.22 = (bf16[64,4224]{1,0:T(8,128)(2,1)S(1)}, bf16[64,4224]{1,0:T(8,128)(2,1)S(1)}, u32[]{:S(2)}, u32[]{:S(2)}) collective-permute-start(bf16[64,4224]{1,0:T(8,128)(2,1)S(1)} %get-tuple-element.117.refs_4_), channel_id=1, source_target_pairs={{0,4},{4,8},{8,12},{5,1},{9,5},{13,9},{2,6},{6,10},{10,14},{7,3},{... | collective-permute-start | bytes 1622024 | tf_op jit(solution)/shard_map/ppermute | solution.py:777
  134.6 22.5 %collective-permute-start.21 = (bf16[64,4224]{1,0:T(8,128)(2,1)S(1)}, bf16[64,4224]{1,0:T(8,128)(2,1)S(1)}, u32[]{:S(2)}, u32[]{:S(2)}) collective-permute-start(bf16[64,4224]{1,0:T(8,128)(2,1)S(1)} %get-tuple-element.118.refs_4_), channel_id=1, source_target_pairs={{4,0},{8,4},{12,8},{1,5},{5,9},{9,13},{6,2},{10,6},{14,10},{3,7},{... | collective-permute-start | bytes 1622024 | tf_op jit(solution)/shard_map/ppermute | solution.py:777
  141.1 22.5 %collective-permute-start.19 = (bf16[64,4224]{1,0:T(8,128)(2,1)S(1)}, bf16[64,4224]{1,0:T(8,128)(2,1)S(1)}, u32[]{:S(2)}, u32[]{:S(2)}) collective-permute-start(bf16[64,4224]{1,0:T(8,128)(2,1)S(1)} %get-tuple-element.119.refs_4_), channel_id=1, source_target_pairs={{0,4},{4,8},{8,12},{5,1},{9,5},{13,9},{2,6},{6,10},{10,14},{7,3},{... | collective-permute-start | bytes 1622024 | tf_op jit(solution)/shard_map/ppermute | solution.py:777
  146.2 21.7 %collective-permute-start.24 = (bf16[64,4224]{1,0:T(8,128)(2,1)S(1)}, bf16[64,4224]{1,0:T(8,128)(2,1)S(1)}, u32[]{:S(2)}, u32[]{:S(2)}) collective-permute-start(bf16[64,4224]{1,0:T(8,128)(2,1)S(1)} %get-tuple-element.122.refs_0_.refs_4_), channel_id=1, source_target_pairs={{4,0},{8,4},{12,8},{1,5},{5,9},{9,13},{6,2},{10,6},{14,10},{3,7},{... | collective-permute-start | bytes 1622024 | tf_op jit(solution)/shard_map/ppermute | solution.py:777
  152.7 36.7 %collective-permute-start.26 = (bf16[64,4224]{1,0:T(8,128)(2,1)S(1)}, bf16[64,4224]{1,0:T(8,128)(2,1)S(1)}, u32[]{:S(2)}, u32[]{:S(2)}) collective-permute-start(bf16[64,4224]{1,0:T(8,128)(2,1)S(1)} %get-tuple-element.125.refs_4_), channel_id=1, source_target_pairs={{0,4},{4,8},{8,12},{5,1},{9,5},{13,9},{2,6},{6,10},{10,14},{7,3},{... | collective-permute-start | bytes 1622024 | tf_op jit(solution)/shard_map/ppermute | solution.py:777
  157.8 31.6 %collective-permute-start.27 = (bf16[64,4224]{1,0:T(8,128)(2,1)S(1)}, bf16[64,4224]{1,0:T(8,128)(2,1)S(1)}, u32[]{:S(2)}, u32[]{:S(2)}) collective-permute-start(bf16[64,4224]{1,0:T(8,128)(2,1)S(1)} %get-tuple-element.126.refs_4_), channel_id=1, source_target_pairs={{4,0},{8,4},{12,8},{1,5},{5,9},{9,13},{6,2},{10,6},{14,10},{3,7},{... | collective-permute-start | bytes 1622024 | tf_op jit(solution)/shard_map/ppermute | solution.py:777
  168.6 21.9 %collective-permute-start.25 = (bf16[64,4224]{1,0:T(8,128)(2,1)S(1)}, bf16[64,4224]{1,0:T(8,128)(2,1)S(1)}, u32[]{:S(2)}, u32[]{:S(2)}) collective-permute-start(bf16[64,4224]{1,0:T(8,128)(2,1)S(1)} %get-tuple-element.129.refs_2_), channel_id=1, source_target_pairs={{4,0},{8,4},{12,8},{1,5},{5,9},{9,13},{6,2},{10,6},{14,10},{3,7},{... | collective-permute-start | bytes 1622024 | tf_op jit(solution)/shard_map/ppermute | solution.py:777
  169.9 20.6 %collective-permute-start.23 = (bf16[64,4224]{1,0:T(8,128)(2,1)S(1)}, bf16[64,4224]{1,0:T(8,128)(2,1)S(1)}, u32[]{:S(2)}, u32[]{:S(2)}) collective-permute-start(bf16[64,4224]{1,0:T(8,128)(2,1)S(1)} %get-tuple-element.127.refs_4_), channel_id=1, source_target_pairs={{0,4},{4,8},{8,12},{5,1},{9,5},{13,9},{2,6},{6,10},{10,14},{7,3},{... | collective-permute-start | bytes 1622024 | tf_op jit(solution)/shard_map/ppermute | solution.py:777
  214.7 23.9 %collective-permute-start.33 = (bf16[64,4224]{1,0:T(8,128)(2,1)S(1)}, bf16[64,4224]{1,0:T(8,128)(2,1)S(1)}, u32[]{:S(2)}, u32[]{:S(2)}) collective-permute-start(bf16[64,4224]{1,0:T(8,128)(2,1)S(1)} %get-tuple-element.146.refs_5_.refs_3_), channel_id=1, source_target_pairs={{4,0},{8,4},{5,9},{9,13},{6,2},{10,6},{7,11},{11,15},{20,16},{24,2... | collective-permute-start | bytes 1622024 | tf_op jit(solution)/shard_map/ppermute | solution.py:777
  228.9 21.2 %collective-permute-start.36 = (bf16[64,4224]{1,0:T(8,128)(2,1)S(1)}, bf16[64,4224]{1,0:T(8,128)(2,1)S(1)}, u32[]{:S(2)}, u32[]{:S(2)}) collective-permute-start(bf16[64,4224]{1,0:T(8,128)(2,1)S(1)} %get-tuple-element.152.x_ref.refs_3_), channel_id=1, source_target_pairs={{4,0},{8,4},{5,9},{9,13},{6,2},{10,6},{7,11},{11,15},{20,16},{24,2... | collective-permute-start | bytes 1622024 | tf_op jit(solution)/shard_map/ppermute | solution.py:777
  230.9 21.2 %collective-permute-start.38 = (bf16[64,4224]{1,0:T(8,128)(2,1)S(1)}, bf16[64,4224]{1,0:T(8,128)(2,1)S(1)}, u32[]{:S(2)}, u32[]{:S(2)}) collective-permute-start(bf16[64,4224]{1,0:T(8,128)(2,1)S(1)} %get-tuple-element.154.x_ref.refs_3_), channel_id=1, source_target_pairs={{8,12},{5,1},{10,14},{7,3},{24,28},{21,17},{26,30},{23,19}} | collective-permute-start | bytes 1622024 | tf_op jit(solution)/shard_map/ppermute | solution.py:777
  239.2 22.5 %collective-permute-start.39 = (bf16[64,4224]{1,0:T(8,128)(2,1)S(1)}, bf16[64,4224]{1,0:T(8,128)(2,1)S(1)}, u32[]{:S(2)}, u32[]{:S(2)}) collective-permute-start(bf16[64,4224]{1,0:T(8,128)(2,1)S(1)} %get-tuple-element.155.x_ref.refs_3_), channel_id=1, source_target_pairs={{4,0},{9,13},{6,2},{11,15},{20,16},{25,29},{22,18},{27,31}} | collective-permute-start | bytes 1622024 | tf_op jit(solution)/shard_map/ppermute | solution.py:777
  241.1 29.3 %collective-permute-start.35 = (bf16[64,4224]{1,0:T(8,128)(2,1)S(1)}, bf16[64,4224]{1,0:T(8,128)(2,1)S(1)}, u32[]{:S(2)}, u32[]{:S(2)}) collective-permute-start(bf16[64,4224]{1,0:T(8,128)(2,1)S(1)} %get-tuple-element.156.x_ref.refs_3_), channel_id=1, source_target_pairs={{8,12},{5,1},{10,14},{7,3},{24,28},{21,17},{26,30},{23,19}} | collective-permute-start | bytes 1622024 | tf_op jit(solution)/shard_map/ppermute | solution.py:777
  250.8 25.8 %collective-permute-start.37 = (bf16[64,4224]{1,0:T(8,128)(2,1)S(1)}, bf16[64,4224]{1,0:T(8,128)(2,1)S(1)}, u32[]{:S(2)}, u32[]{:S(2)}) collective-permute-start(bf16[64,4224]{1,0:T(8,128)(2,1)S(1)} %get-tuple-element.158), channel_id=1, source_target_pairs={{4,0},{9,13},{6,2},{11,15},{20,16},{25,29},{22,18},{27,31}} | collective-permute-start | bytes 1622024 | tf_op jit(solution)/shard_map/ppermute | solution.py:777
  (29 other events, 391.2 us)

commit v2 on v1

--- a/solution.py
+++ b/solution.py
@@ -727,8 +727,6 @@
         rs, ag = slot < chunks, slot > 0
         came, held, sent, before = {}, {}, {}, None
         if ag:
-            if slot == chunks:
-                proj_out = in_hbm(proj_out)
             res, grd = in_vmem(own_rows[0]), in_vmem(own_rows[1])
             ins = [
                 [partials[slot - 1, h], arrived[h, 0], arrived[h, 1], res, grd, gain]
@@ -802,7 +800,7 @@
                     if slot == 0 and work and work[0][0] == (1, 1):
                         continue
                     if k > 0 and (slot > 0 or k > 1) and not (slot == 1 and work and k == 1 and flow == 0):
-                        if slot == chunks and flow == 0:
+                        if slot == chunks and (h, flow, k) != (HALVES - 1, 1, parts - 2):
                             marks[:] = [touch(x)]
                         else:
                             do_one([x], slot == chunks)
@@ -823,7 +821,7 @@
             else:
                 while work:
                     do_one(list(marks))
-                marks[:] = [touch(came[0, 0])]
+                marks[:] = [tie(marks[0], [came[0, 0]])]
                 held[0] = store_last(pos, (came[0, 0], came[0, 1]), held[0], list(marks))
             gathered.append(held[0])
         arrived = came

time: 287 us -> 286 us (level)
  no operation moved by 1% of the time
where the time goes in v2:
time: 286 us; the launch traced here: 285 us
  Pallas kernels  123 us (43%)
  starting transfers between devices  97.9 us (34%)
  waiting for transfers between devices  62.6 us (22%)
    ppermute x40, starting transfers between devices, body(): lax.ppermute(x, ('tensor', 'query'), pairs(flow, 0 if reduce_now else k,...  94 us
    ppermute x40, waiting for transfers between devices, body(): lax.ppermute(x, ('tensor', 'query'), pairs(flow, 0 if reduce_now else k,...  62.6 us
    pallas_call x7, Pallas kernels, forward_piece(): pl.pallas_call(kernel, grid=(steps,), in_specs=[pl.BlockSpec((parts, None...  37.4 us
    pallas_call x4, Pallas kernels, backward_piece(): pl.pallas_call(kernel, grid=(1,), in_specs=[pl.BlockSpec((parts, rows, ha...  25.5 us
    pallas_call x28, Pallas kernels, relay(): pl.pallas_call(kernel, grid_spec=pltpu.PrefetchScalarGridSpec(num_scalar_...  18.4 us
    pallas_call x4, Pallas kernels, load_weights(): pl.pallas_call(kernel, in_specs=[ANY] * (1 + len(after)), out_specs=pl.Bl...  16.6 us
    pallas_call x4, Pallas kernels, norm_out(): pl.pallas_call(kernel, grid_spec=pltpu.PrefetchScalarGridSpec(num_scalar_...  6.76 us
  transfers between devices with their start and end apart: 44, of which 16 were waited for; matrix products, arithmetic and copies ran while one was open for 0% of the time, Pallas kernels for 37%

profile of v2, /device:TPU:0, one launch (start us, length us, event | category | flops | bytes accessed | tf_op | source)
XLA Modules:
  0.0 285.2 jit_solution(4433170558101221816)
XLA Ops:
  0.7 8.9 %forward_piece.7 = (bf16[4,64,4224]{2,1,0:T(8,128)(2,1)S(1)}, f32[8,128]{1,0:T(8,128)S(1)}) custom-call(bf16[4,2,64,2048]{3,2,1,0:T(8,128)(2,1)} %bitcast.8, bf16[2048,8192]{1,0:T(8,128)(2,1)} %w_ref.21), custom_call_target="tpu_custom_call" | custom-call | bytes 720000 | tf_op jit(solution)/shard_map/forward_piece/pallas_call | solution.py:107
  10.9 5.0 %collective-permute-start.3 = (bf16[64,4224]{1,0:T(8,128)(2,1)S(1)}, bf16[64,4224]{1,0:T(8,128)(2,1)S(1)}, u32[]{:S(2)}, u32[]{:S(2)}) collective-permute-start(bf16[64,4224]{1,0:T(8,128)(2,1)S(1)} %first_block.7), channel_id=1, source_target_pairs={{0,4},{13,9},{2,6},{15,11},{16,20},{29,25},{18,22},{31,27}} | collective-permute-start | bytes 1622024 | tf_op jit(solution)/shard_map/ppermute | solution.py:775
  17.1 7.6 %forward_piece.8 = (bf16[4,64,4224]{2,1,0:T(8,128)(2,1)S(1)}, f32[8,128]{1,0:T(8,128)S(1)}) custom-call(bf16[4,2,64,2048]{3,2,1,0:T(8,128)(2,1)S(1)} %bitcast.10, bf16[2048,8192]{1,0:T(8,128)(2,1)} %w_ref.21, bf16[64,4224]{1,0:T(8,128)(2,1)S(1)} %first_block.4.refs_0_), custom_call_target="tpu_custom_call" | custom-call | bytes 720000 | tf_op jit(solution)/shard_map/forward_piece/pallas_call | solution.py:107
  34.7 5.2 %collective-permute-done.1.refs_0_ = bf16[64,4224]{1,0:T(8,128)(2,1)S(1)} collective-permute-done((bf16[64,4224]{1,0:T(8,128)(2,1)S(1)}, bf16[64,4224]{1,0:T(8,128)(2,1)S(1)}, u32[]{:S(2)}, u32[]{:S(2)}) %collective-permute-start.1) | collective-permute-done | bytes 540704 | tf_op jit(solution)/shard_map/ppermute | solution.py:775
  40.6 4.4 %collective-permute-start.9 = (bf16[64,4224]{1,0:T(8,128)(2,1)S(1)}, bf16[64,4224]{1,0:T(8,128)(2,1)S(1)}, u32[]{:S(2)}, u32[]{:S(2)}) collective-permute-start(bf16[64,4224]{1,0:T(8,128)(2,1)S(1)} %relay.30.refs_3_), channel_id=1, source_target_pairs={{0,4},{4,8},{9,5},{13,9},{2,6},{6,10},{11,7},{15,11},{16,20},{20,2... | collective-permute-start | bytes 1622024 | tf_op jit(solution)/shard_map/ppermute | solution.py:775
  52.2 4.4 %collective-permute-start.6 = (bf16[64,4224]{1,0:T(8,128)(2,1)S(1)}, bf16[64,4224]{1,0:T(8,128)(2,1)S(1)}, u32[]{:S(2)}, u32[]{:S(2)}) collective-permute-start(bf16[64,4224]{1,0:T(8,128)(2,1)S(1)} %relay.32.refs_3_), channel_id=1, source_target_pairs={{0,4},{4,8},{8,12},{5,1},{9,5},{13,9},{2,6},{6,10},{10,14},{7,3},{... | collective-permute-start | bytes 1622024 | tf_op jit(solution)/shard_map/ppermute | solution.py:775
  65.7 5.2 %collective-permute-start.10 = (bf16[64,4224]{1,0:T(8,128)(2,1)S(1)}, bf16[64,4224]{1,0:T(8,128)(2,1)S(1)}, u32[]{:S(2)}, u32[]{:S(2)}) collective-permute-start(bf16[64,4224]{1,0:T(8,128)(2,1)S(1)} %relay.34.refs_3_), channel_id=1, source_target_pairs={{0,4},{4,8},{8,12},{5,1},{9,5},{13,9},{2,6},{6,10},{10,14},{7,3},{... | collective-permute-start | bytes 1622024 | tf_op jit(solution)/shard_map/ppermute | solution.py:775
  72.4 7.6 %forward_piece.11 = (bf16[4,64,4224]{2,1,0:T(8,128)(2,1)S(1)}, f32[8,128]{1,0:T(8,128)S(1)}) custom-call(bf16[4,2,64,2048]{3,2,1,0:T(8,128)(2,1)S(1)} %bitcast.13, bf16[2048,8192]{1,0:T(8,128)(2,1)} %w_ref.21, bf16[64,8192]{1,0:T(8,128)(2,1)S(1)} %get-tuple-element.92.refs_0_.refs_3_.refs_9_), custom_call_target="tpu_custom_call" | custom-call | bytes 720000 | tf_op jit(solution)/shard_map/forward_piece/pallas_call | solution.py:107
  81.3 5.0 %collective-permute-done.10.refs_1_.refs_7_ = bf16[64,4224]{1,0:T(8,128)(2,1)S(1)} collective-permute-done((bf16[64,4224]{1,0:T(8,128)(2,1)S(1)}, bf16[64,4224]{1,0:T(8,128)(2,1)S(1)}, u32[]{:S(2)}, u32[]{:S(2)}) %collective-permute-start.10) | collective-permute-done | bytes 540704 | tf_op jit(solution)/shard_map/ppermute | solution.py:775
  99.9 4.6 %collective-permute-start.14 = (bf16[64,4224]{1,0:T(8,128)(2,1)S(1)}, bf16[64,4224]{1,0:T(8,128)(2,1)S(1)}, u32[]{:S(2)}, u32[]{:S(2)}) collective-permute-start(bf16[64,4224]{1,0:T(8,128)(2,1)S(1)} %get-tuple-element.104.refs_4_), channel_id=1, source_target_pairs={{0,4},{4,8},{8,12},{5,1},{9,5},{13,9},{2,6},{6,10},{10,14},{7,3},{... | collective-permute-start | bytes 1622024 | tf_op jit(solution)/shard_map/ppermute | solution.py:775
  107.1 4.5 %collective-permute-start.18 = (bf16[64,4224]{1,0:T(8,128)(2,1)S(1)}, bf16[64,4224]{1,0:T(8,128)(2,1)S(1)}, u32[]{:S(2)}, u32[]{:S(2)}) collective-permute-start(bf16[64,4224]{1,0:T(8,128)(2,1)S(1)} %get-tuple-element.106.refs_4_), channel_id=1, source_target_pairs={{0,4},{4,8},{8,12},{5,1},{9,5},{13,9},{2,6},{6,10},{10,14},{7,3},{... | collective-permute-start | bytes 1622024 | tf_op jit(solution)/shard_map/ppermute | solution.py:775
  135.9 4.5 %collective-permute-done.15.refs_0_ = bf16[64,4224]{1,0:T(8,128)(2,1)S(1)} collective-permute-done((bf16[64,4224]{1,0:T(8,128)(2,1)S(1)}, bf16[64,4224]{1,0:T(8,128)(2,1)S(1)}, u32[]{:S(2)}, u32[]{:S(2)}) %collective-permute-start.15) | collective-permute-done | bytes 540704 | tf_op jit(solution)/shard_map/ppermute | solution.py:775
  152.7 4.4 %collective-permute-start.26 = (bf16[64,4224]{1,0:T(8,128)(2,1)S(1)}, bf16[64,4224]{1,0:T(8,128)(2,1)S(1)}, u32[]{:S(2)}, u32[]{:S(2)}) collective-permute-start(bf16[64,4224]{1,0:T(8,128)(2,1)S(1)} %get-tuple-element.125.refs_4_), channel_id=1, source_target_pairs={{0,4},{4,8},{8,12},{5,1},{9,5},{13,9},{2,6},{6,10},{10,14},{7,3},{... | collective-permute-start | bytes 1622024 | tf_op jit(solution)/shard_map/ppermute | solution.py:775
  159.1 4.5 %collective-permute-done.19.refs_0_ = bf16[64,4224]{1,0:T(8,128)(2,1)S(1)} collective-permute-done((bf16[64,4224]{1,0:T(8,128)(2,1)S(1)}, bf16[64,4224]{1,0:T(8,128)(2,1)S(1)}, u32[]{:S(2)}, u32[]{:S(2)}) %collective-permute-start.19) | collective-permute-done | bytes 540704 | tf_op jit(solution)/shard_map/ppermute | solution.py:775
  169.9 4.6 %collective-permute-start.23 = (bf16[64,4224]{1,0:T(8,128)(2,1)S(1)}, bf16[64,4224]{1,0:T(8,128)(2,1)S(1)}, u32[]{:S(2)}, u32[]{:S(2)}) collective-permute-start(bf16[64,4224]{1,0:T(8,128)(2,1)S(1)} %get-tuple-element.127.refs_4_), channel_id=1, source_target_pairs={{0,4},{4,8},{8,12},{5,1},{9,5},{13,9},{2,6},{6,10},{10,14},{7,3},{... | collective-permute-start | bytes 1622024 | tf_op jit(solution)/shard_map/ppermute | solution.py:775
  182.9 6.4 %load_weights.7.refs_6_.refs_8_.refs_3_.refs_4_ = bf16[512,8192]{1,0:T(8,128)(2,1)S(1)} custom-call(bf16[2048,8192]{1,0:T(8,128)(2,1)} %w_ref.21, bf16[512,8192]{1,0:T(8,128)(2,1)S(1)} %load_weights.6.refs_0_.refs_2_.refs_3_), custom_call_target="tpu_custom_call" | custom-call | bytes 720000 | tf_op jit(solution)/shard_map/load_weights/pallas_call | solution.py:139
  197.7 6.2 %backward_piece.4 = (bf16[4,2,64,2048]{3,2,1,0:T(8,128)(2,1)}, f32[8,128]{1,0:T(8,128)S(1)}) custom-call(bf16[4,64,4224]{2,1,0:T(8,128)(2,1)S(1)} %get-tuple-element.136.refs_0_, bf16[4,64,4224]{2,1,0:T(8,128)(2,1)S(1)} %get-tuple-element.137.refs_1_, bf16[512,8192]{1,0:T(8,128)(2,1)S(1)} %load_weights.4.refs_3_.refs_2_.refs_1_, ...), custom_call_target="tpu_custom_call" | custom-call | bytes 720000 | tf_op jit(solution)/shard_map/backward_piece/pallas_call | solution.py:215
  205.1 4.6 %collective-permute-start.28 = (bf16[64,4224]{1,0:T(8,128)(2,1)S(1)}, bf16[64,4224]{1,0:T(8,128)(2,1)S(1)}, u32[]{:S(2)}, u32[]{:S(2)}) collective-permute-start(bf16[64,4224]{1,0:T(8,128)(2,1)S(1)} %get-tuple-element.140.x_ref.refs_3_), channel_id=1, source_target_pairs={{0,4},{4,8},{8,12},{5,1},{9,5},{13,9},{2,6},{6,10},{10,14},{7,3},{... | collective-permute-start | bytes 1622024 | tf_op jit(solution)/shard_map/ppermute | solution.py:775
  214.3 7.7 %collective-permute-done.28.refs_0_ = bf16[64,4224]{1,0:T(8,128)(2,1)S(1)} collective-permute-done((bf16[64,4224]{1,0:T(8,128)(2,1)S(1)}, bf16[64,4224]{1,0:T(8,128)(2,1)S(1)}, u32[]{:S(2)}, u32[]{:S(2)}) %collective-permute-start.28) | collective-permute-done | bytes 540704 | tf_op jit(solution)/shard_map/ppermute | solution.py:775
  230.0 8.2 %collective-permute-done.33.refs_0_ = bf16[64,4224]{1,0:T(8,128)(2,1)S(1)} collective-permute-done((bf16[64,4224]{1,0:T(8,128)(2,1)S(1)}, bf16[64,4224]{1,0:T(8,128)(2,1)S(1)}, u32[]{:S(2)}, u32[]{:S(2)}) %collective-permute-start.33) | collective-permute-done | bytes 540704 | tf_op jit(solution)/shard_map/ppermute | solution.py:775
  241.6 8.2 %collective-permute-done.36.refs_0_ = bf16[64,4224]{1,0:T(8,128)(2,1)S(1)} collective-permute-done((bf16[64,4224]{1,0:T(8,128)(2,1)S(1)}, bf16[64,4224]{1,0:T(8,128)(2,1)S(1)}, u32[]{:S(2)}, u32[]{:S(2)}) %collective-permute-start.36) | collective-permute-done | bytes 540704 | tf_op jit(solution)/shard_map/ppermute | solution.py:775
  251.8 6.2 %backward_piece.5 = (bf16[4,2,64,2048]{3,2,1,0:T(8,128)(2,1)}, f32[8,128]{1,0:T(8,128)S(1)}) custom-call(bf16[4,64,4224]{2,1,0:T(8,128)(2,1)S(1)} %get-tuple-element.136.refs_0_, bf16[4,64,4224]{2,1,0:T(8,128)(2,1)S(1)} %get-tuple-element.137.refs_1_, bf16[512,8192]{1,0:T(8,128)(2,1)S(1)} %bitcast.7, ...), custom_call_target="tpu_custom_call", output_to_operand_aliasing={{0}: (4, {})} | custom-call | bytes 720000 | tf_op jit(solution)/shard_map/backward_piece/pallas_call | solution.py:215
  264.1 6.1 %backward_piece.6 = (f32[4,64,2048]{2,1,0:T(8,128)S(1)}, f32[8,128]{1,0:T(8,128)S(1)}) custom-call(bf16[4,64,4224]{2,1,0:T(8,128)(2,1)S(1)} %store_last.2.refs_1_.refs_0_, bf16[512,8192]{1,0:T(8,128)(2,1)S(1)} %load_weights.4.refs_3_.refs_2_.refs_1_, bf16[512,8192]{1,0:T(8,128)(2,1)S(1)} %load_weights.5.refs_0_.refs_3_.refs_2_, ...), custom_call_target="tpu_custom_call" | custom-call | bytes 720000 | tf_op jit(solution)/shard_map/backward_piece/pallas_call | solution.py:215
  276.9 7.1 %backward_piece.7 = (bf16[4,2,64,2048]{3,2,1,0:T(8,128)(2,1)}, f32[8,128]{1,0:T(8,128)S(1)}) custom-call(bf16[4,64,4224]{2,1,0:T(8,128)(2,1)S(1)} %store_last.3.refs_0_, bf16[512,8192]{1,0:T(8,128)(2,1)S(1)} %load_weights.4.refs_3_.refs_2_.refs_1_, bf16[512,8192]{1,0:T(8,128)(2,1)S(1)} %load_weights.5.refs_0_.refs_3_.refs_2_, ...), custom_call_target="tpu_custom_call", output_to_operand_aliasing={{0}: (6, {})} | custom-call | bytes 720000 | tf_op jit(solution)/shard_map/backward_piece/pallas_call | solution.py:215
  (159 shorter events, 142.5 us)
Async XLA Ops:
  29.0 22.5 %collective-permute-start.5 = (bf16[64,4224]{1,0:T(8,128)(2,1)S(1)}, bf16[64,4224]{1,0:T(8,128)(2,1)S(1)}, u32[]{:S(2)}, u32[]{:S(2)}) collective-permute-start(bf16[64,4224]{1,0:T(8,128)(2,1)S(1)} %relay.28.refs_3_), channel_id=1, source_target_pairs={{0,4},{4,8},{9,5},{13,9},{2,6},{6,10},{11,7},{15,11},{16,20},{20,2... | collective-permute-start | bytes 1622024 | tf_op jit(solution)/shard_map/ppermute | solution.py:775
  34.0 22.6 %collective-permute-start.4 = (bf16[64,4224]{1,0:T(8,128)(2,1)S(1)}, bf16[64,4224]{1,0:T(8,128)(2,1)S(1)}, u32[]{:S(2)}, u32[]{:S(2)}) collective-permute-start(bf16[64,4224]{1,0:T(8,128)(2,1)S(1)} %relay.29.refs_3_), channel_id=1, source_target_pairs={{8,4},{12,8},{1,5},{5,9},{10,6},{14,10},{3,7},{7,11},{24,20},{28,2... | collective-permute-start | bytes 1622024 | tf_op jit(solution)/shard_map/ppermute | solution.py:775
  40.6 22.5 %collective-permute-start.9 = (bf16[64,4224]{1,0:T(8,128)(2,1)S(1)}, bf16[64,4224]{1,0:T(8,128)(2,1)S(1)}, u32[]{:S(2)}, u32[]{:S(2)}) collective-permute-start(bf16[64,4224]{1,0:T(8,128)(2,1)S(1)} %relay.30.refs_3_), channel_id=1, source_target_pairs={{0,4},{4,8},{9,5},{13,9},{2,6},{6,10},{11,7},{15,11},{16,20},{20,2... | collective-permute-start | bytes 1622024 | tf_op jit(solution)/shard_map/ppermute | solution.py:775
  52.2 27.9 %collective-permute-start.6 = (bf16[64,4224]{1,0:T(8,128)(2,1)S(1)}, bf16[64,4224]{1,0:T(8,128)(2,1)S(1)}, u32[]{:S(2)}, u32[]{:S(2)}) collective-permute-start(bf16[64,4224]{1,0:T(8,128)(2,1)S(1)} %relay.32.refs_3_), channel_id=1, source_target_pairs={{0,4},{4,8},{8,12},{5,1},{9,5},{13,9},{2,6},{6,10},{10,14},{7,3},{... | collective-permute-start | bytes 1622024 | tf_op jit(solution)/shard_map/ppermute | solution.py:775
  57.2 22.9 %collective-permute-start.7 = (bf16[64,4224]{1,0:T(8,128)(2,1)S(1)}, bf16[64,4224]{1,0:T(8,128)(2,1)S(1)}, u32[]{:S(2)}, u32[]{:S(2)}) collective-permute-start(bf16[64,4224]{1,0:T(8,128)(2,1)S(1)} %relay.33.refs_1_.refs_3_), channel_id=1, source_target_pairs={{4,0},{8,4},{12,8},{1,5},{5,9},{9,13},{6,2},{10,6},{14,10},{3,7},{... | collective-permute-start | bytes 1622024 | tf_op jit(solution)/shard_map/ppermute | solution.py:775
  65.7 20.6 %collective-permute-start.10 = (bf16[64,4224]{1,0:T(8,128)(2,1)S(1)}, bf16[64,4224]{1,0:T(8,128)(2,1)S(1)}, u32[]{:S(2)}, u32[]{:S(2)}) collective-permute-start(bf16[64,4224]{1,0:T(8,128)(2,1)S(1)} %relay.34.refs_3_), channel_id=1, source_target_pairs={{0,4},{4,8},{8,12},{5,1},{9,5},{13,9},{2,6},{6,10},{10,14},{7,3},{... | collective-permute-start | bytes 1622024 | tf_op jit(solution)/shard_map/ppermute | solution.py:775
  107.1 21.7 %collective-permute-start.18 = (bf16[64,4224]{1,0:T(8,128)(2,1)S(1)}, bf16[64,4224]{1,0:T(8,128)(2,1)S(1)}, u32[]{:S(2)}, u32[]{:S(2)}) collective-permute-start(bf16[64,4224]{1,0:T(8,128)(2,1)S(1)} %get-tuple-element.106.refs_4_), channel_id=1, source_target_pairs={{0,4},{4,8},{8,12},{5,1},{9,5},{13,9},{2,6},{6,10},{10,14},{7,3},{... | collective-permute-start | bytes 1622024 | tf_op jit(solution)/shard_map/ppermute | solution.py:775
  112.3 21.6 %collective-permute-start.17 = (bf16[64,4224]{1,0:T(8,128)(2,1)S(1)}, bf16[64,4224]{1,0:T(8,128)(2,1)S(1)}, u32[]{:S(2)}, u32[]{:S(2)}) collective-permute-start(bf16[64,4224]{1,0:T(8,128)(2,1)S(1)} %get-tuple-element.107.refs_1_.refs_4_), channel_id=1, source_target_pairs={{4,0},{8,4},{12,8},{1,5},{5,9},{9,13},{6,2},{10,6},{14,10},{3,7},{... | collective-permute-start | bytes 1622024 | tf_op jit(solution)/shard_map/ppermute | solution.py:775
  118.1 22.3 %collective-permute-start.15 = (bf16[64,4224]{1,0:T(8,128)(2,1)S(1)}, bf16[64,4224]{1,0:T(8,128)(2,1)S(1)}, u32[]{:S(2)}, u32[]{:S(2)}) collective-permute-start(bf16[64,4224]{1,0:T(8,128)(2,1)S(1)} %get-tuple-element.111.refs_4_), channel_id=1, source_target_pairs={{0,4},{4,8},{8,12},{5,1},{9,5},{13,9},{2,6},{6,10},{10,14},{7,3},{... | collective-permute-start | bytes 1622024 | tf_op jit(solution)/shard_map/ppermute | solution.py:775
  123.2 22.4 %collective-permute-start.20 = (bf16[64,4224]{1,0:T(8,128)(2,1)S(1)}, bf16[64,4224]{1,0:T(8,128)(2,1)S(1)}, u32[]{:S(2)}, u32[]{:S(2)}) collective-permute-start(bf16[64,4224]{1,0:T(8,128)(2,1)S(1)} %get-tuple-element.115.refs_4_), channel_id=1, source_target_pairs={{4,0},{8,4},{12,8},{1,5},{5,9},{9,13},{6,2},{10,6},{14,10},{3,7},{... | collective-permute-start | bytes 1622024 | tf_op jit(solution)/shard_map/ppermute | solution.py:775
  129.5 22.5 %collective-permute-start.22 = (bf16[64,4224]{1,0:T(8,128)(2,1)S(1)}, bf16[64,4224]{1,0:T(8,128)(2,1)S(1)}, u32[]{:S(2)}, u32[]{:S(2)}) collective-permute-start(bf16[64,4224]{1,0:T(8,128)(2,1)S(1)} %get-tuple-element.117.refs_4_), channel_id=1, source_target_pairs={{0,4},{4,8},{8,12},{5,1},{9,5},{13,9},{2,6},{6,10},{10,14},{7,3},{... | collective-permute-start | bytes 1622024 | tf_op jit(solution)/shard_map/ppermute | solution.py:775
  134.6 22.5 %collective-permute-start.21 = (bf16[64,4224]{1,0:T(8,128)(2,1)S(1)}, bf16[64,4224]{1,0:T(8,128)(2,1)S(1)}, u32[]{:S(2)}, u32[]{:S(2)}) collective-permute-start(bf16[64,4224]{1,0:T(8,128)(2,1)S(1)} %get-tuple-element.118.refs_4_), channel_id=1, source_target_pairs={{4,0},{8,4},{12,8},{1,5},{5,9},{9,13},{6,2},{10,6},{14,10},{3,7},{... | collective-permute-start | bytes 1622024 | tf_op jit(solution)/shard_map/ppermute | solution.py:775
  141.1 22.5 %collective-permute-start.19 = (bf16[64,4224]{1,0:T(8,128)(2,1)S(1)}, bf16[64,4224]{1,0:T(8,128)(2,1)S(1)}, u32[]{:S(2)}, u32[]{:S(2)}) collective-permute-start(bf16[64,4224]{1,0:T(8,128)(2,1)S(1)} %get-tuple-element.119.refs_4_), channel_id=1, source_target_pairs={{0,4},{4,8},{8,12},{5,1},{9,5},{13,9},{2,6},{6,10},{10,14},{7,3},{... | collective-permute-start | bytes 1622024 | tf_op jit(solution)/shard_map/ppermute | solution.py:775
  146.2 21.7 %collective-permute-start.24 = (bf16[64,4224]{1,0:T(8,128)(2,1)S(1)}, bf16[64,4224]{1,0:T(8,128)(2,1)S(1)}, u32[]{:S(2)}, u32[]{:S(2)}) collective-permute-start(bf16[64,4224]{1,0:T(8,128)(2,1)S(1)} %get-tuple-element.122.refs_0_.refs_4_), channel_id=1, source_target_pairs={{4,0},{8,4},{12,8},{1,5},{5,9},{9,13},{6,2},{10,6},{14,10},{3,7},{... | collective-permute-start | bytes 1622024 | tf_op jit(solution)/shard_map/ppermute | solution.py:775
  152.7 36.7 %collective-permute-start.26 = (bf16[64,4224]{1,0:T(8,128)(2,1)S(1)}, bf16[64,4224]{1,0:T(8,128)(2,1)S(1)}, u32[]{:S(2)}, u32[]{:S(2)}) collective-permute-start(bf16[64,4224]{1,0:T(8,128)(2,1)S(1)} %get-tuple-element.125.refs_4_), channel_id=1, source_target_pairs={{0,4},{4,8},{8,12},{5,1},{9,5},{13,9},{2,6},{6,10},{10,14},{7,3},{... | collective-permute-start | bytes 1622024 | tf_op jit(solution)/shard_map/ppermute | solution.py:775
  157.8 31.6 %collective-permute-start.27 = (bf16[64,4224]{1,0:T(8,128)(2,1)S(1)}, bf16[64,4224]{1,0:T(8,128)(2,1)S(1)}, u32[]{:S(2)}, u32[]{:S(2)}) collective-permute-start(bf16[64,4224]{1,0:T(8,128)(2,1)S(1)} %get-tuple-element.126.refs_4_), channel_id=1, source_target_pairs={{4,0},{8,4},{12,8},{1,5},{5,9},{9,13},{6,2},{10,6},{14,10},{3,7},{... | collective-permute-start | bytes 1622024 | tf_op jit(solution)/shard_map/ppermute | solution.py:775
  168.6 21.9 %collective-permute-start.25 = (bf16[64,4224]{1,0:T(8,128)(2,1)S(1)}, bf16[64,4224]{1,0:T(8,128)(2,1)S(1)}, u32[]{:S(2)}, u32[]{:S(2)}) collective-permute-start(bf16[64,4224]{1,0:T(8,128)(2,1)S(1)} %get-tuple-element.129.refs_2_), channel_id=1, source_target_pairs={{4,0},{8,4},{12,8},{1,5},{5,9},{9,13},{6,2},{10,6},{14,10},{3,7},{... | collective-permute-start | bytes 1622024 | tf_op jit(solution)/shard_map/ppermute | solution.py:775
  169.9 20.6 %collective-permute-start.23 = (bf16[64,4224]{1,0:T(8,128)(2,1)S(1)}, bf16[64,4224]{1,0:T(8,128)(2,1)S(1)}, u32[]{:S(2)}, u32[]{:S(2)}) collective-permute-start(bf16[64,4224]{1,0:T(8,128)(2,1)S(1)} %get-tuple-element.127.refs_4_), channel_id=1, source_target_pairs={{0,4},{4,8},{8,12},{5,1},{9,5},{13,9},{2,6},{6,10},{10,14},{7,3},{... | collective-permute-start | bytes 1622024 | tf_op jit(solution)/shard_map/ppermute | solution.py:775
  213.0 25.2 %collective-permute-start.33 = (bf16[64,4224]{1,0:T(8,128)(2,1)S(1)}, bf16[64,4224]{1,0:T(8,128)(2,1)S(1)}, u32[]{:S(2)}, u32[]{:S(2)}) collective-permute-start(bf16[64,4224]{1,0:T(8,128)(2,1)S(1)} %get-tuple-element.145.x_ref.refs_3_), channel_id=1, source_target_pairs={{4,0},{8,4},{5,9},{9,13},{6,2},{10,6},{7,11},{11,15},{20,16},{24,2... | collective-permute-start | bytes 1622024 | tf_op jit(solution)/shard_map/ppermute | solution.py:775
  227.3 22.5 %collective-permute-start.36 = (bf16[64,4224]{1,0:T(8,128)(2,1)S(1)}, bf16[64,4224]{1,0:T(8,128)(2,1)S(1)}, u32[]{:S(2)}, u32[]{:S(2)}) collective-permute-start(bf16[64,4224]{1,0:T(8,128)(2,1)S(1)} %get-tuple-element.150.x_ref.refs_3_), channel_id=1, source_target_pairs={{4,0},{8,4},{5,9},{9,13},{6,2},{10,6},{7,11},{11,15},{20,16},{24,2... | collective-permute-start | bytes 1622024 | tf_op jit(solution)/shard_map/ppermute | solution.py:775
  229.3 28.6 %collective-permute-start.38 = (bf16[64,4224]{1,0:T(8,128)(2,1)S(1)}, bf16[64,4224]{1,0:T(8,128)(2,1)S(1)}, u32[]{:S(2)}, u32[]{:S(2)}) collective-permute-start(bf16[64,4224]{1,0:T(8,128)(2,1)S(1)} %get-tuple-element.152.x_ref.refs_3_), channel_id=1, source_target_pairs={{8,12},{5,1},{10,14},{7,3},{24,28},{21,17},{26,30},{23,19}} | collective-permute-start | bytes 1622024 | tf_op jit(solution)/shard_map/ppermute | solution.py:775
  238.9 22.5 %collective-permute-start.39 = (bf16[64,4224]{1,0:T(8,128)(2,1)S(1)}, bf16[64,4224]{1,0:T(8,128)(2,1)S(1)}, u32[]{:S(2)}, u32[]{:S(2)}) collective-permute-start(bf16[64,4224]{1,0:T(8,128)(2,1)S(1)} %get-tuple-element.153.x_ref.refs_3_), channel_id=1, source_target_pairs={{4,0},{9,13},{6,2},{11,15},{20,16},{25,29},{22,18},{27,31}} | collective-permute-start | bytes 1622024 | tf_op jit(solution)/shard_map/ppermute | solution.py:775
  240.9 29.2 %collective-permute-start.35 = (bf16[64,4224]{1,0:T(8,128)(2,1)S(1)}, bf16[64,4224]{1,0:T(8,128)(2,1)S(1)}, u32[]{:S(2)}, u32[]{:S(2)}) collective-permute-start(bf16[64,4224]{1,0:T(8,128)(2,1)S(1)} %get-tuple-element.154.x_ref.refs_3_), channel_id=1, source_target_pairs={{8,12},{5,1},{10,14},{7,3},{24,28},{21,17},{26,30},{23,19}} | collective-permute-start | bytes 1622024 | tf_op jit(solution)/shard_map/ppermute | solution.py:775
  250.4 25.8 %collective-permute-start.37 = (bf16[64,4224]{1,0:T(8,128)(2,1)S(1)}, bf16[64,4224]{1,0:T(8,128)(2,1)S(1)}, u32[]{:S(2)}, u32[]{:S(2)}) collective-permute-start(bf16[64,4224]{1,0:T(8,128)(2,1)S(1)} %get-tuple-element.156.refs_5_), channel_id=1, source_target_pairs={{4,0},{9,13},{6,2},{11,15},{20,16},{25,29},{22,18},{27,31}} | collective-permute-start | bytes 1622024 | tf_op jit(solution)/shard_map/ppermute | solution.py:775
  (29 other events, 391.8 us)

commit v3 on v2

--- a/solution.py
+++ b/solution.py
@@ -440,7 +440,7 @@
             b = project_rows(out_ref[:, :half], p_ref[:, :half])
             for j in range(1, n):
                 b = b + project_rows(rest_ref[j - 1], p_ref[:, j * half : (j + 1) * half])
-            a = sum(refs[j][:, half:].astype(F32) for j in range(3))
+            a = sum(refs[6 * (n - 1) + j][:, half:].astype(F32) for j in range(3))
             out_ref[:, half:] = (a + spread(b.astype(BF16), b.shape[1])).astype(BF16)
         else:
             out_ref[:, half:] = jnp.zeros((rows, wide - half), BF16)
@@ -581,17 +581,19 @@
     n, depth = queries.shape
 
     def kernel(pos_ref, *refs):
-        out_ref, all_ref = refs[-2:]
+        out_ref, all_ref, parts_ref = refs[-3:]
         for back in range(size):
             all_ref[lax.rem(pos_ref[3] - back + size, size)] = refs[back][...]
         for d in range(size):
-            rest, total = all_ref[d], None
-            for _ in range(3):
-                part = rest.astype(BF16)
-                rest = rest - part.astype(F32)
-                term = project_rows(part, refs[size][...])
-                total = term if total is None else total + term
-            out_ref[d * EX_DEV : (d + 1) * EX_DEV, :] = total
+            rest = all_ref[d]
+            for t in range(3):
+                part = rest.astype(BF16).astype(F32)
+                rest = rest - part
+                at = (t * size + d) * EX_DEV
+                parts_ref[at : at + EX_DEV, :] = part
+        terms = project_rows(parts_ref[...].astype(BF16), refs[size][...])
+        n_out = size * EX_DEV
+        out_ref[...] = terms[:n_out] + terms[n_out : 2 * n_out] + terms[2 * n_out :]
 
     return pl.pallas_call(
         kernel,
@@ -602,7 +604,10 @@
             + [pl.BlockSpec((n, depth), lambda i, w: (0, 0))]
             + [ANY] * len(after),
             out_specs=pl.BlockSpec((size * EX_DEV, n), lambda i, w: (0, 0)),
-            scratch_shapes=[pltpu.VMEM((size, EX_DEV, depth), F32)],
+            scratch_shapes=[
+                pltpu.VMEM((size, EX_DEV, depth), F32),
+                pltpu.VMEM((3 * size * EX_DEV, depth), F32),
+            ],
         ),
         out_shape=jax.ShapeDtypeStruct((size * EX_DEV, n), F32),
         compiler_params=pltpu.CompilerParams(vmem_limit_bytes=LIMIT),
@@ -684,7 +689,7 @@
             partials.get((c, h)),
             after,
         )
-        if h == 0 and piece == pieces - 1:
+        if h == HALVES - 1 and piece == pieces - 1:
             partials[c, h] = forward_extra(by_share, proj_in, c, partials[c, h], [mark])
         return mark
 

time: 286 us -> 285 us (level)
  transfers between devices with their start and end apart: 44 -> 44, of which waited for: 16 -> 15; matrix products, arithmetic and copies ran while one was open for 0% -> 0% of each run, Pallas kernels for 37% -> 37%
where the time goes in v3:
time: 285 us; the launch traced here: 284 us
  Pallas kernels  122 us (43%)
  starting transfers between devices  97.6 us (34%)
  waiting for transfers between devices  62.4 us (22%)
    ppermute x40, starting transfers between devices, body(): lax.ppermute(x, ('tensor', 'query'), pairs(flow, 0 if reduce_now else k,...  93.7 us
    ppermute x40, waiting for transfers between devices, body(): lax.ppermute(x, ('tensor', 'query'), pairs(flow, 0 if reduce_now else k,...  62.4 us
    pallas_call x7, Pallas kernels, forward_piece(): pl.pallas_call(kernel, grid=(steps,), in_specs=[pl.BlockSpec((parts, None...  37.9 us
    pallas_call x4, Pallas kernels, backward_piece(): pl.pallas_call(kernel, grid=(1,), in_specs=[pl.BlockSpec((parts, rows, ha...  25.5 us
    pallas_call x28, Pallas kernels, relay(): pl.pallas_call(kernel, grid_spec=pltpu.PrefetchScalarGridSpec(num_scalar_...  18.4 us
    pallas_call x4, Pallas kernels, load_weights(): pl.pallas_call(kernel, in_specs=[ANY] * (1 + len(after)), out_specs=pl.Bl...  16.6 us
    pallas_call x4, Pallas kernels, norm_out(): pl.pallas_call(kernel, grid_spec=pltpu.PrefetchScalarGridSpec(num_scalar_...  6.77 us
  transfers between devices with their start and end apart: 44, of which 15 were waited for; matrix products, arithmetic and copies ran while one was open for 0% of the time, Pallas kernels for 37%

profile of v3, /device:TPU:0, one launch (start us, length us, event | category | flops | bytes accessed | tf_op | source)
XLA Modules:
  0.0 283.9 jit_solution(688392694579647019)
XLA Ops:
  0.6 9.4 %forward_piece.7 = (bf16[4,64,4224]{2,1,0:T(8,128)(2,1)S(1)}, f32[8,128]{1,0:T(8,128)}) custom-call(bf16[4,2,64,2048]{3,2,1,0:T(8,128)(2,1)} %bitcast.8, bf16[2048,8192]{1,0:T(8,128)(2,1)} %w_ref.21), custom_call_target="tpu_custom_call" | custom-call | bytes 720000 | tf_op jit(solution)/shard_map/forward_piece/pallas_call | solution.py:107
  10.7 5.1 %collective-permute-start.3 = (bf16[64,4224]{1,0:T(8,128)(2,1)S(1)}, bf16[64,4224]{1,0:T(8,128)(2,1)S(1)}, u32[]{:S(2)}, u32[]{:S(2)}) collective-permute-start(bf16[64,4224]{1,0:T(8,128)(2,1)S(1)} %first_block.7), channel_id=1, source_target_pairs={{0,4},{13,9},{2,6},{15,11},{16,20},{29,25},{18,22},{31,27}} | collective-permute-start | bytes 1622024 | tf_op jit(solution)/shard_map/ppermute | solution.py:780
  17.2 7.6 %forward_piece.8 = (bf16[4,64,4224]{2,1,0:T(8,128)(2,1)S(1)}, f32[8,128]{1,0:T(8,128)S(1)}) custom-call(bf16[4,2,64,2048]{3,2,1,0:T(8,128)(2,1)S(1)} %bitcast.9, bf16[2048,8192]{1,0:T(8,128)(2,1)} %w_ref.21, bf16[64,4224]{1,0:T(8,128)(2,1)S(1)} %first_block.4.refs_0_), custom_call_target="tpu_custom_call" | custom-call | bytes 720000 | tf_op jit(solution)/shard_map/forward_piece/pallas_call | solution.py:107
  34.5 5.3 %collective-permute-done.1.refs_0_ = bf16[64,4224]{1,0:T(8,128)(2,1)S(1)} collective-permute-done((bf16[64,4224]{1,0:T(8,128)(2,1)S(1)}, bf16[64,4224]{1,0:T(8,128)(2,1)S(1)}, u32[]{:S(2)}, u32[]{:S(2)}) %collective-permute-start.1) | collective-permute-done | bytes 540704 | tf_op jit(solution)/shard_map/ppermute | solution.py:780
  40.5 4.4 %collective-permute-start.9 = (bf16[64,4224]{1,0:T(8,128)(2,1)S(1)}, bf16[64,4224]{1,0:T(8,128)(2,1)S(1)}, u32[]{:S(2)}, u32[]{:S(2)}) collective-permute-start(bf16[64,4224]{1,0:T(8,128)(2,1)S(1)} %relay.30.refs_3_), channel_id=1, source_target_pairs={{0,4},{4,8},{9,5},{13,9},{2,6},{6,10},{11,7},{15,11},{16,20},{20,2... | collective-permute-start | bytes 1622024 | tf_op jit(solution)/shard_map/ppermute | solution.py:780
  65.6 5.2 %collective-permute-start.10 = (bf16[64,4224]{1,0:T(8,128)(2,1)S(1)}, bf16[64,4224]{1,0:T(8,128)(2,1)S(1)}, u32[]{:S(2)}, u32[]{:S(2)}) collective-permute-start(bf16[64,4224]{1,0:T(8,128)(2,1)S(1)} %relay.34.refs_3_), channel_id=1, source_target_pairs={{0,4},{4,8},{8,12},{5,1},{9,5},{13,9},{2,6},{6,10},{10,14},{7,3},{... | collective-permute-start | bytes 1622024 | tf_op jit(solution)/shard_map/ppermute | solution.py:780
  72.4 7.6 %forward_piece.11 = (bf16[4,64,4224]{2,1,0:T(8,128)(2,1)S(1)}, f32[8,128]{1,0:T(8,128)S(1)}) custom-call(bf16[4,2,64,2048]{3,2,1,0:T(8,128)(2,1)S(1)} %bitcast.13, bf16[2048,8192]{1,0:T(8,128)(2,1)} %w_ref.21, bf16[64,8192]{1,0:T(8,128)(2,1)S(1)} %get-tuple-element.90.refs_0_.refs_3_.refs_9_), custom_call_target="tpu_custom_call" | custom-call | bytes 720000 | tf_op jit(solution)/shard_map/forward_piece/pallas_call | solution.py:107
  81.2 5.0 %collective-permute-done.10.refs_1_.refs_7_ = bf16[64,4224]{1,0:T(8,128)(2,1)S(1)} collective-permute-done((bf16[64,4224]{1,0:T(8,128)(2,1)S(1)}, bf16[64,4224]{1,0:T(8,128)(2,1)S(1)}, u32[]{:S(2)}, u32[]{:S(2)}) %collective-permute-start.10) | collective-permute-done | bytes 540704 | tf_op jit(solution)/shard_map/ppermute | solution.py:780
  89.6 4.4 %collective-permute-start.13 = (bf16[64,4224]{1,0:T(8,128)(2,1)S(1)}, bf16[64,4224]{1,0:T(8,128)(2,1)S(1)}, u32[]{:S(2)}, u32[]{:S(2)}) collective-permute-start(bf16[64,4224]{1,0:T(8,128)(2,1)S(1)} %get-tuple-element.97.refs_1_), channel_id=1, source_target_pairs={{0,4},{4,8},{8,12},{5,1},{9,5},{13,9},{2,6},{6,10},{10,14},{7,3},{... | collective-permute-start | bytes 1622024 | tf_op jit(solution)/shard_map/ppermute | solution.py:780
  99.9 4.6 %collective-permute-start.14 = (bf16[64,4224]{1,0:T(8,128)(2,1)S(1)}, bf16[64,4224]{1,0:T(8,128)(2,1)S(1)}, u32[]{:S(2)}, u32[]{:S(2)}) collective-permute-start(bf16[64,4224]{1,0:T(8,128)(2,1)S(1)} %get-tuple-element.102.refs_4_), channel_id=1, source_target_pairs={{0,4},{4,8},{8,12},{5,1},{9,5},{13,9},{2,6},{6,10},{10,14},{7,3},{... | collective-permute-start | bytes 1622024 | tf_op jit(solution)/shard_map/ppermute | solution.py:780
  106.5 4.5 %collective-permute-start.18 = (bf16[64,4224]{1,0:T(8,128)(2,1)S(1)}, bf16[64,4224]{1,0:T(8,128)(2,1)S(1)}, u32[]{:S(2)}, u32[]{:S(2)}) collective-permute-start(bf16[64,4224]{1,0:T(8,128)(2,1)S(1)} %get-tuple-element.104.refs_4_), channel_id=1, source_target_pairs={{0,4},{4,8},{8,12},{5,1},{9,5},{13,9},{2,6},{6,10},{10,14},{7,3},{... | collective-permute-start | bytes 1622024 | tf_op jit(solution)/shard_map/ppermute | solution.py:780
  135.9 4.5 %collective-permute-done.15.refs_0_ = bf16[64,4224]{1,0:T(8,128)(2,1)S(1)} collective-permute-done((bf16[64,4224]{1,0:T(8,128)(2,1)S(1)}, bf16[64,4224]{1,0:T(8,128)(2,1)S(1)}, u32[]{:S(2)}, u32[]{:S(2)}) %collective-permute-start.15) | collective-permute-done | bytes 540704 | tf_op jit(solution)/shard_map/ppermute | solution.py:780
  141.1 4.4 %collective-permute-start.19 = (bf16[64,4224]{1,0:T(8,128)(2,1)S(1)}, bf16[64,4224]{1,0:T(8,128)(2,1)S(1)}, u32[]{:S(2)}, u32[]{:S(2)}) collective-permute-start(bf16[64,4224]{1,0:T(8,128)(2,1)S(1)} %get-tuple-element.117.refs_4_), channel_id=1, source_target_pairs={{0,4},{4,8},{8,12},{5,1},{9,5},{13,9},{2,6},{6,10},{10,14},{7,3},{... | collective-permute-start | bytes 1622024 | tf_op jit(solution)/shard_map/ppermute | solution.py:780
  159.1 4.5 %collective-permute-done.19.refs_0_ = bf16[64,4224]{1,0:T(8,128)(2,1)S(1)} collective-permute-done((bf16[64,4224]{1,0:T(8,128)(2,1)S(1)}, bf16[64,4224]{1,0:T(8,128)(2,1)S(1)}, u32[]{:S(2)}, u32[]{:S(2)}) %collective-permute-start.19) | collective-permute-done | bytes 540704 | tf_op jit(solution)/shard_map/ppermute | solution.py:780
  169.9 4.6 %collective-permute-start.23 = (bf16[64,4224]{1,0:T(8,128)(2,1)S(1)}, bf16[64,4224]{1,0:T(8,128)(2,1)S(1)}, u32[]{:S(2)}, u32[]{:S(2)}) collective-permute-start(bf16[64,4224]{1,0:T(8,128)(2,1)S(1)} %get-tuple-element.125.refs_4_), channel_id=1, source_target_pairs={{0,4},{4,8},{8,12},{5,1},{9,5},{13,9},{2,6},{6,10},{10,14},{7,3},{... | collective-permute-start | bytes 1622024 | tf_op jit(solution)/shard_map/ppermute | solution.py:780
  182.9 6.4 %load_weights.7.refs_6_.refs_8_.refs_3_.refs_4_ = bf16[512,8192]{1,0:T(8,128)(2,1)S(1)} custom-call(bf16[2048,8192]{1,0:T(8,128)(2,1)} %w_ref.21, bf16[512,8192]{1,0:T(8,128)(2,1)S(1)} %load_weights.6.refs_0_.refs_2_.refs_3_), custom_call_target="tpu_custom_call" | custom-call | bytes 720000 | tf_op jit(solution)/shard_map/load_weights/pallas_call | solution.py:139
  197.7 6.2 %backward_piece.4 = (bf16[4,2,64,2048]{3,2,1,0:T(8,128)(2,1)}, f32[8,128]{1,0:T(8,128)S(1)}) custom-call(bf16[4,64,4224]{2,1,0:T(8,128)(2,1)S(1)} %get-tuple-element.134.refs_0_, bf16[4,64,4224]{2,1,0:T(8,128)(2,1)S(1)} %get-tuple-element.135.refs_1_, bf16[512,8192]{1,0:T(8,128)(2,1)S(1)} %load_weights.4.refs_3_.refs_2_.refs_1_, ...), custom_call_target="tpu_custom_call" | custom-call | bytes 720000 | tf_op jit(solution)/shard_map/backward_piece/pallas_call | solution.py:215
  205.1 4.6 %collective-permute-start.28 = (bf16[64,4224]{1,0:T(8,128)(2,1)S(1)}, bf16[64,4224]{1,0:T(8,128)(2,1)S(1)}, u32[]{:S(2)}, u32[]{:S(2)}) collective-permute-start(bf16[64,4224]{1,0:T(8,128)(2,1)S(1)} %get-tuple-element.138.x_ref.refs_3_), channel_id=1, source_target_pairs={{0,4},{4,8},{8,12},{5,1},{9,5},{13,9},{2,6},{6,10},{10,14},{7,3},{... | collective-permute-start | bytes 1622024 | tf_op jit(solution)/shard_map/ppermute | solution.py:780
  214.3 7.7 %collective-permute-done.28.refs_0_ = bf16[64,4224]{1,0:T(8,128)(2,1)S(1)} collective-permute-done((bf16[64,4224]{1,0:T(8,128)(2,1)S(1)}, bf16[64,4224]{1,0:T(8,128)(2,1)S(1)}, u32[]{:S(2)}, u32[]{:S(2)}) %collective-permute-start.28) | collective-permute-done | bytes 540704 | tf_op jit(solution)/shard_map/ppermute | solution.py:780
  230.0 8.2 %collective-permute-done.33.refs_0_ = bf16[64,4224]{1,0:T(8,128)(2,1)S(1)} collective-permute-done((bf16[64,4224]{1,0:T(8,128)(2,1)S(1)}, bf16[64,4224]{1,0:T(8,128)(2,1)S(1)}, u32[]{:S(2)}, u32[]{:S(2)}) %collective-permute-start.33) | collective-permute-done | bytes 540704 | tf_op jit(solution)/shard_map/ppermute | solution.py:780
  241.6 8.2 %collective-permute-done.36.refs_0_ = bf16[64,4224]{1,0:T(8,128)(2,1)S(1)} collective-permute-done((bf16[64,4224]{1,0:T(8,128)(2,1)S(1)}, bf16[64,4224]{1,0:T(8,128)(2,1)S(1)}, u32[]{:S(2)}, u32[]{:S(2)}) %collective-permute-start.36) | collective-permute-done | bytes 540704 | tf_op jit(solution)/shard_map/ppermute | solution.py:780
  251.8 6.2 %backward_piece.5 = (bf16[4,2,64,2048]{3,2,1,0:T(8,128)(2,1)}, f32[8,128]{1,0:T(8,128)S(1)}) custom-call(bf16[4,64,4224]{2,1,0:T(8,128)(2,1)S(1)} %get-tuple-element.134.refs_0_, bf16[4,64,4224]{2,1,0:T(8,128)(2,1)S(1)} %get-tuple-element.135.refs_1_, bf16[512,8192]{1,0:T(8,128)(2,1)S(1)} %bitcast.7, ...), custom_call_target="tpu_custom_call", output_to_operand_aliasing={{0}: (4, {})} | custom-call | bytes 720000 | tf_op jit(solution)/shard_map/backward_piece/pallas_call | solution.py:215
  264.0 6.1 %backward_piece.6 = (f32[4,64,2048]{2,1,0:T(8,128)S(1)}, f32[8,128]{1,0:T(8,128)S(1)}) custom-call(bf16[4,64,4224]{2,1,0:T(8,128)(2,1)S(1)} %store_last.2.refs_1_.refs_0_, bf16[512,8192]{1,0:T(8,128)(2,1)S(1)} %load_weights.4.refs_3_.refs_2_.refs_1_, bf16[512,8192]{1,0:T(8,128)(2,1)S(1)} %load_weights.5.refs_0_.refs_3_.refs_2_, ...), custom_call_target="tpu_custom_call" | custom-call | bytes 720000 | tf_op jit(solution)/shard_map/backward_piece/pallas_call | solution.py:215
  275.6 7.1 %backward_piece.7 = (bf16[4,2,64,2048]{3,2,1,0:T(8,128)(2,1)}, f32[8,128]{1,0:T(8,128)S(1)}) custom-call(bf16[4,64,4224]{2,1,0:T(8,128)(2,1)S(1)} %store_last.3.refs_0_, bf16[512,8192]{1,0:T(8,128)(2,1)S(1)} %load_weights.4.refs_3_.refs_2_.refs_1_, bf16[512,8192]{1,0:T(8,128)(2,1)S(1)} %load_weights.5.refs_0_.refs_3_.refs_2_, ...), custom_call_target="tpu_custom_call", output_to_operand_aliasing={{0}: (6, {})} | custom-call | bytes 720000 | tf_op jit(solution)/shard_map/backward_piece/pallas_call | solution.py:215
  (159 shorter events, 140.5 us)
Async XLA Ops:
  29.4 22.0 %collective-permute-start.5 = (bf16[64,4224]{1,0:T(8,128)(2,1)S(1)}, bf16[64,4224]{1,0:T(8,128)(2,1)S(1)}, u32[]{:S(2)}, u32[]{:S(2)}) collective-permute-start(bf16[64,4224]{1,0:T(8,128)(2,1)S(1)} %relay.28.refs_3_), channel_id=1, source_target_pairs={{0,4},{4,8},{9,5},{13,9},{2,6},{6,10},{11,7},{15,11},{16,20},{20,2... | collective-permute-start | bytes 1622024 | tf_op jit(solution)/shard_map/ppermute | solution.py:780
  33.8 22.7 %collective-permute-start.4 = (bf16[64,4224]{1,0:T(8,128)(2,1)S(1)}, bf16[64,4224]{1,0:T(8,128)(2,1)S(1)}, u32[]{:S(2)}, u32[]{:S(2)}) collective-permute-start(bf16[64,4224]{1,0:T(8,128)(2,1)S(1)} %relay.29.refs_3_), channel_id=1, source_target_pairs={{8,4},{12,8},{1,5},{5,9},{10,6},{14,10},{3,7},{7,11},{24,20},{28,2... | collective-permute-start | bytes 1622024 | tf_op jit(solution)/shard_map/ppermute | solution.py:780
  40.5 22.5 %collective-permute-start.9 = (bf16[64,4224]{1,0:T(8,128)(2,1)S(1)}, bf16[64,4224]{1,0:T(8,128)(2,1)S(1)}, u32[]{:S(2)}, u32[]{:S(2)}) collective-permute-start(bf16[64,4224]{1,0:T(8,128)(2,1)S(1)} %relay.30.refs_3_), channel_id=1, source_target_pairs={{0,4},{4,8},{9,5},{13,9},{2,6},{6,10},{11,7},{15,11},{16,20},{20,2... | collective-permute-start | bytes 1622024 | tf_op jit(solution)/shard_map/ppermute | solution.py:780
  52.1 27.9 %collective-permute-start.6 = (bf16[64,4224]{1,0:T(8,128)(2,1)S(1)}, bf16[64,4224]{1,0:T(8,128)(2,1)S(1)}, u32[]{:S(2)}, u32[]{:S(2)}) collective-permute-start(bf16[64,4224]{1,0:T(8,128)(2,1)S(1)} %relay.32.refs_3_), channel_id=1, source_target_pairs={{0,4},{4,8},{8,12},{5,1},{9,5},{13,9},{2,6},{6,10},{10,14},{7,3},{... | collective-permute-start | bytes 1622024 | tf_op jit(solution)/shard_map/ppermute | solution.py:780
  57.2 22.9 %collective-permute-start.7 = (bf16[64,4224]{1,0:T(8,128)(2,1)S(1)}, bf16[64,4224]{1,0:T(8,128)(2,1)S(1)}, u32[]{:S(2)}, u32[]{:S(2)}) collective-permute-start(bf16[64,4224]{1,0:T(8,128)(2,1)S(1)} %relay.33.refs_1_.refs_3_), channel_id=1, source_target_pairs={{4,0},{8,4},{12,8},{1,5},{5,9},{9,13},{6,2},{10,6},{14,10},{3,7},{... | collective-permute-start | bytes 1622024 | tf_op jit(solution)/shard_map/ppermute | solution.py:780
  65.6 20.6 %collective-permute-start.10 = (bf16[64,4224]{1,0:T(8,128)(2,1)S(1)}, bf16[64,4224]{1,0:T(8,128)(2,1)S(1)}, u32[]{:S(2)}, u32[]{:S(2)}) collective-permute-start(bf16[64,4224]{1,0:T(8,128)(2,1)S(1)} %relay.34.refs_3_), channel_id=1, source_target_pairs={{0,4},{4,8},{8,12},{5,1},{9,5},{13,9},{2,6},{6,10},{10,14},{7,3},{... | collective-permute-start | bytes 1622024 | tf_op jit(solution)/shard_map/ppermute | solution.py:780
  106.5 22.3 %collective-permute-start.18 = (bf16[64,4224]{1,0:T(8,128)(2,1)S(1)}, bf16[64,4224]{1,0:T(8,128)(2,1)S(1)}, u32[]{:S(2)}, u32[]{:S(2)}) collective-permute-start(bf16[64,4224]{1,0:T(8,128)(2,1)S(1)} %get-tuple-element.104.refs_4_), channel_id=1, source_target_pairs={{0,4},{4,8},{8,12},{5,1},{9,5},{13,9},{2,6},{6,10},{10,14},{7,3},{... | collective-permute-start | bytes 1622024 | tf_op jit(solution)/shard_map/ppermute | solution.py:780
  111.7 22.2 %collective-permute-start.17 = (bf16[64,4224]{1,0:T(8,128)(2,1)S(1)}, bf16[64,4224]{1,0:T(8,128)(2,1)S(1)}, u32[]{:S(2)}, u32[]{:S(2)}) collective-permute-start(bf16[64,4224]{1,0:T(8,128)(2,1)S(1)} %get-tuple-element.105.refs_1_.refs_4_), channel_id=1, source_target_pairs={{4,0},{8,4},{12,8},{1,5},{5,9},{9,13},{6,2},{10,6},{14,10},{3,7},{... | collective-permute-start | bytes 1622024 | tf_op jit(solution)/shard_map/ppermute | solution.py:780
  118.1 22.3 %collective-permute-start.15 = (bf16[64,4224]{1,0:T(8,128)(2,1)S(1)}, bf16[64,4224]{1,0:T(8,128)(2,1)S(1)}, u32[]{:S(2)}, u32[]{:S(2)}) collective-permute-start(bf16[64,4224]{1,0:T(8,128)(2,1)S(1)} %get-tuple-element.109.refs_4_), channel_id=1, source_target_pairs={{0,4},{4,8},{8,12},{5,1},{9,5},{13,9},{2,6},{6,10},{10,14},{7,3},{... | collective-permute-start | bytes 1622024 | tf_op jit(solution)/shard_map/ppermute | solution.py:780
  123.1 22.4 %collective-permute-start.20 = (bf16[64,4224]{1,0:T(8,128)(2,1)S(1)}, bf16[64,4224]{1,0:T(8,128)(2,1)S(1)}, u32[]{:S(2)}, u32[]{:S(2)}) collective-permute-start(bf16[64,4224]{1,0:T(8,128)(2,1)S(1)} %get-tuple-element.113.refs_4_), channel_id=1, source_target_pairs={{4,0},{8,4},{12,8},{1,5},{5,9},{9,13},{6,2},{10,6},{14,10},{3,7},{... | collective-permute-start | bytes 1622024 | tf_op jit(solution)/shard_map/ppermute | solution.py:780
  129.5 22.5 %collective-permute-start.22 = (bf16[64,4224]{1,0:T(8,128)(2,1)S(1)}, bf16[64,4224]{1,0:T(8,128)(2,1)S(1)}, u32[]{:S(2)}, u32[]{:S(2)}) collective-permute-start(bf16[64,4224]{1,0:T(8,128)(2,1)S(1)} %get-tuple-element.115.refs_4_), channel_id=1, source_target_pairs={{0,4},{4,8},{8,12},{5,1},{9,5},{13,9},{2,6},{6,10},{10,14},{7,3},{... | collective-permute-start | bytes 1622024 | tf_op jit(solution)/shard_map/ppermute | solution.py:780
  134.6 22.5 %collective-permute-start.21 = (bf16[64,4224]{1,0:T(8,128)(2,1)S(1)}, bf16[64,4224]{1,0:T(8,128)(2,1)S(1)}, u32[]{:S(2)}, u32[]{:S(2)}) collective-permute-start(bf16[64,4224]{1,0:T(8,128)(2,1)S(1)} %get-tuple-element.116.refs_4_), channel_id=1, source_target_pairs={{4,0},{8,4},{12,8},{1,5},{5,9},{9,13},{6,2},{10,6},{14,10},{3,7},{... | collective-permute-start | bytes 1622024 | tf_op jit(solution)/shard_map/ppermute | solution.py:780
  141.1 22.5 %collective-permute-start.19 = (bf16[64,4224]{1,0:T(8,128)(2,1)S(1)}, bf16[64,4224]{1,0:T(8,128)(2,1)S(1)}, u32[]{:S(2)}, u32[]{:S(2)}) collective-permute-start(bf16[64,4224]{1,0:T(8,128)(2,1)S(1)} %get-tuple-element.117.refs_4_), channel_id=1, source_target_pairs={{0,4},{4,8},{8,12},{5,1},{9,5},{13,9},{2,6},{6,10},{10,14},{7,3},{... | collective-permute-start | bytes 1622024 | tf_op jit(solution)/shard_map/ppermute | solution.py:780
  146.2 21.7 %collective-permute-start.24 = (bf16[64,4224]{1,0:T(8,128)(2,1)S(1)}, bf16[64,4224]{1,0:T(8,128)(2,1)S(1)}, u32[]{:S(2)}, u32[]{:S(2)}) collective-permute-start(bf16[64,4224]{1,0:T(8,128)(2,1)S(1)} %get-tuple-element.120.refs_0_.refs_4_), channel_id=1, source_target_pairs={{4,0},{8,4},{12,8},{1,5},{5,9},{9,13},{6,2},{10,6},{14,10},{3,7},{... | collective-permute-start | bytes 1622024 | tf_op jit(solution)/shard_map/ppermute | solution.py:780
  152.6 36.7 %collective-permute-start.26 = (bf16[64,4224]{1,0:T(8,128)(2,1)S(1)}, bf16[64,4224]{1,0:T(8,128)(2,1)S(1)}, u32[]{:S(2)}, u32[]{:S(2)}) collective-permute-start(bf16[64,4224]{1,0:T(8,128)(2,1)S(1)} %get-tuple-element.123.refs_4_), channel_id=1, source_target_pairs={{0,4},{4,8},{8,12},{5,1},{9,5},{13,9},{2,6},{6,10},{10,14},{7,3},{... | collective-permute-start | bytes 1622024 | tf_op jit(solution)/shard_map/ppermute | solution.py:780
  157.8 31.5 %collective-permute-start.27 = (bf16[64,4224]{1,0:T(8,128)(2,1)S(1)}, bf16[64,4224]{1,0:T(8,128)(2,1)S(1)}, u32[]{:S(2)}, u32[]{:S(2)}) collective-permute-start(bf16[64,4224]{1,0:T(8,128)(2,1)S(1)} %get-tuple-element.124.refs_4_), channel_id=1, source_target_pairs={{4,0},{8,4},{12,8},{1,5},{5,9},{9,13},{6,2},{10,6},{14,10},{3,7},{... | collective-permute-start | bytes 1622024 | tf_op jit(solution)/shard_map/ppermute | solution.py:780
  168.6 21.9 %collective-permute-start.25 = (bf16[64,4224]{1,0:T(8,128)(2,1)S(1)}, bf16[64,4224]{1,0:T(8,128)(2,1)S(1)}, u32[]{:S(2)}, u32[]{:S(2)}) collective-permute-start(bf16[64,4224]{1,0:T(8,128)(2,1)S(1)} %get-tuple-element.127.refs_2_), channel_id=1, source_target_pairs={{4,0},{8,4},{12,8},{1,5},{5,9},{9,13},{6,2},{10,6},{14,10},{3,7},{... | collective-permute-start | bytes 1622024 | tf_op jit(solution)/shard_map/ppermute | solution.py:780
  169.9 20.6 %collective-permute-start.23 = (bf16[64,4224]{1,0:T(8,128)(2,1)S(1)}, bf16[64,4224]{1,0:T(8,128)(2,1)S(1)}, u32[]{:S(2)}, u32[]{:S(2)}) collective-permute-start(bf16[64,4224]{1,0:T(8,128)(2,1)S(1)} %get-tuple-element.125.refs_4_), channel_id=1, source_target_pairs={{0,4},{4,8},{8,12},{5,1},{9,5},{13,9},{2,6},{6,10},{10,14},{7,3},{... | collective-permute-start | bytes 1622024 | tf_op jit(solution)/shard_map/ppermute | solution.py:780
  213.0 25.2 %collective-permute-start.33 = (bf16[64,4224]{1,0:T(8,128)(2,1)S(1)}, bf16[64,4224]{1,0:T(8,128)(2,1)S(1)}, u32[]{:S(2)}, u32[]{:S(2)}) collective-permute-start(bf16[64,4224]{1,0:T(8,128)(2,1)S(1)} %get-tuple-element.143.x_ref.refs_3_), channel_id=1, source_target_pairs={{4,0},{8,4},{5,9},{9,13},{6,2},{10,6},{7,11},{11,15},{20,16},{24,2... | collective-permute-start | bytes 1622024 | tf_op jit(solution)/shard_map/ppermute | solution.py:780
  227.3 22.5 %collective-permute-start.36 = (bf16[64,4224]{1,0:T(8,128)(2,1)S(1)}, bf16[64,4224]{1,0:T(8,128)(2,1)S(1)}, u32[]{:S(2)}, u32[]{:S(2)}) collective-permute-start(bf16[64,4224]{1,0:T(8,128)(2,1)S(1)} %get-tuple-element.148.x_ref.refs_3_), channel_id=1, source_target_pairs={{4,0},{8,4},{5,9},{9,13},{6,2},{10,6},{7,11},{11,15},{20,16},{24,2... | collective-permute-start | bytes 1622024 | tf_op jit(solution)/shard_map/ppermute | solution.py:780
  229.3 28.6 %collective-permute-start.38 = (bf16[64,4224]{1,0:T(8,128)(2,1)S(1)}, bf16[64,4224]{1,0:T(8,128)(2,1)S(1)}, u32[]{:S(2)}, u32[]{:S(2)}) collective-permute-start(bf16[64,4224]{1,0:T(8,128)(2,1)S(1)} %get-tuple-element.150.x_ref.refs_3_), channel_id=1, source_target_pairs={{8,12},{5,1},{10,14},{7,3},{24,28},{21,17},{26,30},{23,19}} | collective-permute-start | bytes 1622024 | tf_op jit(solution)/shard_map/ppermute | solution.py:780
  238.8 22.5 %collective-permute-start.39 = (bf16[64,4224]{1,0:T(8,128)(2,1)S(1)}, bf16[64,4224]{1,0:T(8,128)(2,1)S(1)}, u32[]{:S(2)}, u32[]{:S(2)}) collective-permute-start(bf16[64,4224]{1,0:T(8,128)(2,1)S(1)} %get-tuple-element.151.x_ref.refs_3_), channel_id=1, source_target_pairs={{4,0},{9,13},{6,2},{11,15},{20,16},{25,29},{22,18},{27,31}} | collective-permute-start | bytes 1622024 | tf_op jit(solution)/shard_map/ppermute | solution.py:780
  240.9 29.2 %collective-permute-start.35 = (bf16[64,4224]{1,0:T(8,128)(2,1)S(1)}, bf16[64,4224]{1,0:T(8,128)(2,1)S(1)}, u32[]{:S(2)}, u32[]{:S(2)}) collective-permute-start(bf16[64,4224]{1,0:T(8,128)(2,1)S(1)} %get-tuple-element.152.x_ref.refs_3_), channel_id=1, source_target_pairs={{8,12},{5,1},{10,14},{7,3},{24,28},{21,17},{26,30},{23,19}} | collective-permute-start | bytes 1622024 | tf_op jit(solution)/shard_map/ppermute | solution.py:780
  250.4 24.5 %collective-permute-start.37 = (bf16[64,4224]{1,0:T(8,128)(2,1)S(1)}, bf16[64,4224]{1,0:T(8,128)(2,1)S(1)}, u32[]{:S(2)}, u32[]{:S(2)}) collective-permute-start(bf16[64,4224]{1,0:T(8,128)(2,1)S(1)} %get-tuple-element.154.refs_5_), channel_id=1, source_target_pairs={{4,0},{9,13},{6,2},{11,15},{20,16},{25,29},{22,18},{27,31}} | collective-permute-start | bytes 1622024 | tf_op jit(solution)/shard_map/ppermute | solution.py:780
  (29 other events, 387.4 us)

commit v4 on v3

--- a/solution.py
+++ b/solution.py
@@ -783,7 +783,7 @@
                         pairs(flow, 0 if reduce_now else k, parts - 2 if gather_now else k - 1),
                     )
                     sent[h, flow] = x
-                    if rs and (k, h, flow) == (parts - 1, HALVES - 1, 1):
+                    if rs and (k, h, flow) == (parts - (1 if slot == 0 else 2), HALVES - 1, 1):
                         own_rows = load_rows(residual, out_grad, slot, rows, [x])
                         x = own_rows[0]
                     if slot == chunks - 1 and flow == 1 and slot > 0:

time: 285 us -> 284 us (level)
  transfers between devices with their start and end apart: 44 -> 44, of which waited for: 15 -> 14; matrix products, arithmetic and copies ran while one was open for 0% -> 0% of each run, Pallas kernels for 37% -> 37%
where the time goes in v4:
time: 284 us; the launch traced here: 283 us
  Pallas kernels  122 us (43%)
  starting transfers between devices  98 us (35%)
  waiting for transfers between devices  60.9 us (21%)
    ppermute x40, starting transfers between devices, body(): lax.ppermute(x, ('tensor', 'query'), pairs(flow, 0 if reduce_now else k,...  94 us
    ppermute x40, waiting for transfers between devices, body(): lax.ppermute(x, ('tensor', 'query'), pairs(flow, 0 if reduce_now else k,...  60.8 us
    pallas_call x7, Pallas kernels, forward_piece(): pl.pallas_call(kernel, grid=(steps,), in_specs=[pl.BlockSpec((parts, None...  37.9 us
    pallas_call x4, Pallas kernels, backward_piece(): pl.pallas_call(kernel, grid=(1,), in_specs=[pl.BlockSpec((parts, rows, ha...  25.5 us
    pallas_call x28, Pallas kernels, relay(): pl.pallas_call(kernel, grid_spec=pltpu.PrefetchScalarGridSpec(num_scalar_...  18.4 us
    pallas_call x4, Pallas kernels, load_weights(): pl.pallas_call(kernel, in_specs=[ANY] * (1 + len(after)), out_specs=pl.Bl...  16.6 us
    pallas_call x4, Pallas kernels, norm_out(): pl.pallas_call(kernel, grid_spec=pltpu.PrefetchScalarGridSpec(num_scalar_...  6.76 us
  transfers between devices with their start and end apart: 44, of which 14 were waited for; matrix products, arithmetic and copies ran while one was open for 0% of the time, Pallas kernels for 37%

profile of v4, /device:TPU:0, one launch (start us, length us, event | category | flops | bytes accessed | tf_op | source)
XLA Modules:
  0.0 282.6 jit_solution(4427133112328762183)
XLA Ops:
  0.6 9.4 %forward_piece.7 = (bf16[4,64,4224]{2,1,0:T(8,128)(2,1)S(1)}, f32[8,128]{1,0:T(8,128)}) custom-call(bf16[4,2,64,2048]{3,2,1,0:T(8,128)(2,1)} %bitcast.8, bf16[2048,8192]{1,0:T(8,128)(2,1)} %w_ref.21), custom_call_target="tpu_custom_call" | custom-call | bytes 720000 | tf_op jit(solution)/shard_map/forward_piece/pallas_call | solution.py:107
  10.7 5.1 %collective-permute-start.3 = (bf16[64,4224]{1,0:T(8,128)(2,1)S(1)}, bf16[64,4224]{1,0:T(8,128)(2,1)S(1)}, u32[]{:S(2)}, u32[]{:S(2)}) collective-permute-start(bf16[64,4224]{1,0:T(8,128)(2,1)S(1)} %first_block.7), channel_id=1, source_target_pairs={{0,4},{13,9},{2,6},{15,11},{16,20},{29,25},{18,22},{31,27}} | collective-permute-start | bytes 1622024 | tf_op jit(solution)/shard_map/ppermute | solution.py:780
  17.2 7.6 %forward_piece.8 = (bf16[4,64,4224]{2,1,0:T(8,128)(2,1)S(1)}, f32[8,128]{1,0:T(8,128)S(1)}) custom-call(bf16[4,2,64,2048]{3,2,1,0:T(8,128)(2,1)S(1)} %bitcast.9, bf16[2048,8192]{1,0:T(8,128)(2,1)} %w_ref.21, bf16[64,4224]{1,0:T(8,128)(2,1)S(1)} %first_block.4.refs_0_), custom_call_target="tpu_custom_call" | custom-call | bytes 720000 | tf_op jit(solution)/shard_map/forward_piece/pallas_call | solution.py:107
  34.5 5.3 %collective-permute-done.1.refs_0_ = bf16[64,4224]{1,0:T(8,128)(2,1)S(1)} collective-permute-done((bf16[64,4224]{1,0:T(8,128)(2,1)S(1)}, bf16[64,4224]{1,0:T(8,128)(2,1)S(1)}, u32[]{:S(2)}, u32[]{:S(2)}) %collective-permute-start.1) | collective-permute-done | bytes 540704 | tf_op jit(solution)/shard_map/ppermute | solution.py:780
  40.5 4.4 %collective-permute-start.9 = (bf16[64,4224]{1,0:T(8,128)(2,1)S(1)}, bf16[64,4224]{1,0:T(8,128)(2,1)S(1)}, u32[]{:S(2)}, u32[]{:S(2)}) collective-permute-start(bf16[64,4224]{1,0:T(8,128)(2,1)S(1)} %relay.30.refs_3_), channel_id=1, source_target_pairs={{0,4},{4,8},{9,5},{13,9},{2,6},{6,10},{11,7},{15,11},{16,20},{20,2... | collective-permute-start | bytes 1622024 | tf_op jit(solution)/shard_map/ppermute | solution.py:780
  52.1 4.4 %collective-permute-start.6 = (bf16[64,4224]{1,0:T(8,128)(2,1)S(1)}, bf16[64,4224]{1,0:T(8,128)(2,1)S(1)}, u32[]{:S(2)}, u32[]{:S(2)}) collective-permute-start(bf16[64,4224]{1,0:T(8,128)(2,1)S(1)} %relay.32.refs_3_), channel_id=1, source_target_pairs={{0,4},{4,8},{8,12},{5,1},{9,5},{13,9},{2,6},{6,10},{10,14},{7,3},{... | collective-permute-start | bytes 1622024 | tf_op jit(solution)/shard_map/ppermute | solution.py:780
  65.6 5.2 %collective-permute-start.10 = (bf16[64,4224]{1,0:T(8,128)(2,1)S(1)}, bf16[64,4224]{1,0:T(8,128)(2,1)S(1)}, u32[]{:S(2)}, u32[]{:S(2)}) collective-permute-start(bf16[64,4224]{1,0:T(8,128)(2,1)S(1)} %relay.34.refs_3_), channel_id=1, source_target_pairs={{0,4},{4,8},{8,12},{5,1},{9,5},{13,9},{2,6},{6,10},{10,14},{7,3},{... | collective-permute-start | bytes 1622024 | tf_op jit(solution)/shard_map/ppermute | solution.py:780
  72.4 7.6 %forward_piece.11 = (bf16[4,64,4224]{2,1,0:T(8,128)(2,1)S(1)}, f32[8,128]{1,0:T(8,128)S(1)}) custom-call(bf16[4,2,64,2048]{3,2,1,0:T(8,128)(2,1)S(1)} %bitcast.13, bf16[2048,8192]{1,0:T(8,128)(2,1)} %w_ref.21, bf16[64,8192]{1,0:T(8,128)(2,1)S(1)} %get-tuple-element.90.refs_0_.refs_3_.refs_9_), custom_call_target="tpu_custom_call" | custom-call | bytes 720000 | tf_op jit(solution)/shard_map/forward_piece/pallas_call | solution.py:107
  81.2 5.0 %collective-permute-done.10.refs_1_.refs_7_ = bf16[64,4224]{1,0:T(8,128)(2,1)S(1)} collective-permute-done((bf16[64,4224]{1,0:T(8,128)(2,1)S(1)}, bf16[64,4224]{1,0:T(8,128)(2,1)S(1)}, u32[]{:S(2)}, u32[]{:S(2)}) %collective-permute-start.10) | collective-permute-done | bytes 540704 | tf_op jit(solution)/shard_map/ppermute | solution.py:780
  89.6 4.4 %collective-permute-start.13 = (bf16[64,4224]{1,0:T(8,128)(2,1)S(1)}, bf16[64,4224]{1,0:T(8,128)(2,1)S(1)}, u32[]{:S(2)}, u32[]{:S(2)}) collective-permute-start(bf16[64,4224]{1,0:T(8,128)(2,1)S(1)} %get-tuple-element.97.refs_1_), channel_id=1, source_target_pairs={{0,4},{4,8},{8,12},{5,1},{9,5},{13,9},{2,6},{6,10},{10,14},{7,3},{... | collective-permute-start | bytes 1622024 | tf_op jit(solution)/shard_map/ppermute | solution.py:780
  99.9 4.6 %collective-permute-start.14 = (bf16[64,4224]{1,0:T(8,128)(2,1)S(1)}, bf16[64,4224]{1,0:T(8,128)(2,1)S(1)}, u32[]{:S(2)}, u32[]{:S(2)}) collective-permute-start(bf16[64,4224]{1,0:T(8,128)(2,1)S(1)} %get-tuple-element.102.refs_4_), channel_id=1, source_target_pairs={{0,4},{4,8},{8,12},{5,1},{9,5},{13,9},{2,6},{6,10},{10,14},{7,3},{... | collective-permute-start | bytes 1622024 | tf_op jit(solution)/shard_map/ppermute | solution.py:780
  106.5 4.5 %collective-permute-start.18 = (bf16[64,4224]{1,0:T(8,128)(2,1)S(1)}, bf16[64,4224]{1,0:T(8,128)(2,1)S(1)}, u32[]{:S(2)}, u32[]{:S(2)}) collective-permute-start(bf16[64,4224]{1,0:T(8,128)(2,1)S(1)} %get-tuple-element.104.refs_4_), channel_id=1, source_target_pairs={{0,4},{4,8},{8,12},{5,1},{9,5},{13,9},{2,6},{6,10},{10,14},{7,3},{... | collective-permute-start | bytes 1622024 | tf_op jit(solution)/shard_map/ppermute | solution.py:780
  135.9 4.5 %collective-permute-done.15.refs_0_ = bf16[64,4224]{1,0:T(8,128)(2,1)S(1)} collective-permute-done((bf16[64,4224]{1,0:T(8,128)(2,1)S(1)}, bf16[64,4224]{1,0:T(8,128)(2,1)S(1)}, u32[]{:S(2)}, u32[]{:S(2)}) %collective-permute-start.15) | collective-permute-done | bytes 540704 | tf_op jit(solution)/shard_map/ppermute | solution.py:780
  153.2 4.6 %collective-permute-start.26 = (bf16[64,4224]{1,0:T(8,128)(2,1)S(1)}, bf16[64,4224]{1,0:T(8,128)(2,1)S(1)}, u32[]{:S(2)}, u32[]{:S(2)}) collective-permute-start(bf16[64,4224]{1,0:T(8,128)(2,1)S(1)} %get-tuple-element.124.refs_4_), channel_id=1, source_target_pairs={{0,4},{4,8},{8,12},{5,1},{9,5},{13,9},{2,6},{6,10},{10,14},{7,3},{... | collective-permute-start | bytes 1622024 | tf_op jit(solution)/shard_map/ppermute | solution.py:780
  169.9 4.6 %collective-permute-start.23 = (bf16[64,4224]{1,0:T(8,128)(2,1)S(1)}, bf16[64,4224]{1,0:T(8,128)(2,1)S(1)}, u32[]{:S(2)}, u32[]{:S(2)}) collective-permute-start(bf16[64,4224]{1,0:T(8,128)(2,1)S(1)} %get-tuple-element.126.refs_4_), channel_id=1, source_target_pairs={{0,4},{4,8},{8,12},{5,1},{9,5},{13,9},{2,6},{6,10},{10,14},{7,3},{... | collective-permute-start | bytes 1622024 | tf_op jit(solution)/shard_map/ppermute | solution.py:780
  181.3 6.4 %load_weights.7.refs_6_.refs_8_.refs_3_.refs_4_ = bf16[512,8192]{1,0:T(8,128)(2,1)S(1)} custom-call(bf16[2048,8192]{1,0:T(8,128)(2,1)} %w_ref.21, bf16[512,8192]{1,0:T(8,128)(2,1)S(1)} %load_weights.6.refs_0_.refs_2_.refs_3_), custom_call_target="tpu_custom_call" | custom-call | bytes 720000 | tf_op jit(solution)/shard_map/load_weights/pallas_call | solution.py:139
  196.3 6.2 %backward_piece.4 = (bf16[4,2,64,2048]{3,2,1,0:T(8,128)(2,1)}, f32[8,128]{1,0:T(8,128)S(1)}) custom-call(bf16[4,64,4224]{2,1,0:T(8,128)(2,1)S(1)} %get-tuple-element.134.refs_0_, bf16[4,64,4224]{2,1,0:T(8,128)(2,1)S(1)} %get-tuple-element.135.refs_1_, bf16[512,8192]{1,0:T(8,128)(2,1)S(1)} %load_weights.4.refs_3_.refs_2_.refs_1_, ...), custom_call_target="tpu_custom_call" | custom-call | bytes 720000 | tf_op jit(solution)/shard_map/backward_piece/pallas_call | solution.py:215
  203.6 4.6 %collective-permute-start.28 = (bf16[64,4224]{1,0:T(8,128)(2,1)S(1)}, bf16[64,4224]{1,0:T(8,128)(2,1)S(1)}, u32[]{:S(2)}, u32[]{:S(2)}) collective-permute-start(bf16[64,4224]{1,0:T(8,128)(2,1)S(1)} %get-tuple-element.138.x_ref.refs_3_), channel_id=1, source_target_pairs={{0,4},{4,8},{8,12},{5,1},{9,5},{13,9},{2,6},{6,10},{10,14},{7,3},{... | collective-permute-start | bytes 1622024 | tf_op jit(solution)/shard_map/ppermute | solution.py:780
  212.8 7.2 %collective-permute-done.28.refs_0_ = bf16[64,4224]{1,0:T(8,128)(2,1)S(1)} collective-permute-done((bf16[64,4224]{1,0:T(8,128)(2,1)S(1)}, bf16[64,4224]{1,0:T(8,128)(2,1)S(1)}, u32[]{:S(2)}, u32[]{:S(2)}) %collective-permute-start.28) | collective-permute-done | bytes 540704 | tf_op jit(solution)/shard_map/ppermute | solution.py:780
  228.8 8.2 %collective-permute-done.33.refs_0_ = bf16[64,4224]{1,0:T(8,128)(2,1)S(1)} collective-permute-done((bf16[64,4224]{1,0:T(8,128)(2,1)S(1)}, bf16[64,4224]{1,0:T(8,128)(2,1)S(1)}, u32[]{:S(2)}, u32[]{:S(2)}) %collective-permute-start.33) | collective-permute-done | bytes 540704 | tf_op jit(solution)/shard_map/ppermute | solution.py:780
  240.3 8.2 %collective-permute-done.36.refs_0_ = bf16[64,4224]{1,0:T(8,128)(2,1)S(1)} collective-permute-done((bf16[64,4224]{1,0:T(8,128)(2,1)S(1)}, bf16[64,4224]{1,0:T(8,128)(2,1)S(1)}, u32[]{:S(2)}, u32[]{:S(2)}) %collective-permute-start.36) | collective-permute-done | bytes 540704 | tf_op jit(solution)/shard_map/ppermute | solution.py:780
  250.5 6.2 %backward_piece.5 = (bf16[4,2,64,2048]{3,2,1,0:T(8,128)(2,1)}, f32[8,128]{1,0:T(8,128)S(1)}) custom-call(bf16[4,64,4224]{2,1,0:T(8,128)(2,1)S(1)} %get-tuple-element.134.refs_0_, bf16[4,64,4224]{2,1,0:T(8,128)(2,1)S(1)} %get-tuple-element.135.refs_1_, bf16[512,8192]{1,0:T(8,128)(2,1)S(1)} %bitcast.7, ...), custom_call_target="tpu_custom_call", output_to_operand_aliasing={{0}: (4, {})} | custom-call | bytes 720000 | tf_op jit(solution)/shard_map/backward_piece/pallas_call | solution.py:215
  262.8 6.1 %backward_piece.6 = (f32[4,64,2048]{2,1,0:T(8,128)S(1)}, f32[8,128]{1,0:T(8,128)S(1)}) custom-call(bf16[4,64,4224]{2,1,0:T(8,128)(2,1)S(1)} %store_last.2.refs_1_.refs_0_, bf16[512,8192]{1,0:T(8,128)(2,1)S(1)} %load_weights.4.refs_3_.refs_2_.refs_1_, bf16[512,8192]{1,0:T(8,128)(2,1)S(1)} %load_weights.5.refs_0_.refs_3_.refs_2_, ...), custom_call_target="tpu_custom_call" | custom-call | bytes 720000 | tf_op jit(solution)/shard_map/backward_piece/pallas_call | solution.py:215
  274.3 7.1 %backward_piece.7 = (bf16[4,2,64,2048]{3,2,1,0:T(8,128)(2,1)}, f32[8,128]{1,0:T(8,128)S(1)}) custom-call(bf16[4,64,4224]{2,1,0:T(8,128)(2,1)S(1)} %store_last.3.refs_0_, bf16[512,8192]{1,0:T(8,128)(2,1)S(1)} %load_weights.4.refs_3_.refs_2_.refs_1_, bf16[512,8192]{1,0:T(8,128)(2,1)S(1)} %load_weights.5.refs_0_.refs_3_.refs_2_, ...), custom_call_target="tpu_custom_call", output_to_operand_aliasing={{0}: (6, {})} | custom-call | bytes 720000 | tf_op jit(solution)/shard_map/backward_piece/pallas_call | solution.py:215
  (159 shorter events, 139.7 us)
Async XLA Ops:
  29.4 22.0 %collective-permute-start.5 = (bf16[64,4224]{1,0:T(8,128)(2,1)S(1)}, bf16[64,4224]{1,0:T(8,128)(2,1)S(1)}, u32[]{:S(2)}, u32[]{:S(2)}) collective-permute-start(bf16[64,4224]{1,0:T(8,128)(2,1)S(1)} %relay.28.refs_3_), channel_id=1, source_target_pairs={{0,4},{4,8},{9,5},{13,9},{2,6},{6,10},{11,7},{15,11},{16,20},{20,2... | collective-permute-start | bytes 1622024 | tf_op jit(solution)/shard_map/ppermute | solution.py:780
  33.8 22.7 %collective-permute-start.4 = (bf16[64,4224]{1,0:T(8,128)(2,1)S(1)}, bf16[64,4224]{1,0:T(8,128)(2,1)S(1)}, u32[]{:S(2)}, u32[]{:S(2)}) collective-permute-start(bf16[64,4224]{1,0:T(8,128)(2,1)S(1)} %relay.29.refs_3_), channel_id=1, source_target_pairs={{8,4},{12,8},{1,5},{5,9},{10,6},{14,10},{3,7},{7,11},{24,20},{28,2... | collective-permute-start | bytes 1622024 | tf_op jit(solution)/shard_map/ppermute | solution.py:780
  40.5 22.5 %collective-permute-start.9 = (bf16[64,4224]{1,0:T(8,128)(2,1)S(1)}, bf16[64,4224]{1,0:T(8,128)(2,1)S(1)}, u32[]{:S(2)}, u32[]{:S(2)}) collective-permute-start(bf16[64,4224]{1,0:T(8,128)(2,1)S(1)} %relay.30.refs_3_), channel_id=1, source_target_pairs={{0,4},{4,8},{9,5},{13,9},{2,6},{6,10},{11,7},{15,11},{16,20},{20,2... | collective-permute-start | bytes 1622024 | tf_op jit(solution)/shard_map/ppermute | solution.py:780
  52.1 27.9 %collective-permute-start.6 = (bf16[64,4224]{1,0:T(8,128)(2,1)S(1)}, bf16[64,4224]{1,0:T(8,128)(2,1)S(1)}, u32[]{:S(2)}, u32[]{:S(2)}) collective-permute-start(bf16[64,4224]{1,0:T(8,128)(2,1)S(1)} %relay.32.refs_3_), channel_id=1, source_target_pairs={{0,4},{4,8},{8,12},{5,1},{9,5},{13,9},{2,6},{6,10},{10,14},{7,3},{... | collective-permute-start | bytes 1622024 | tf_op jit(solution)/shard_map/ppermute | solution.py:780
  57.2 22.9 %collective-permute-start.7 = (bf16[64,4224]{1,0:T(8,128)(2,1)S(1)}, bf16[64,4224]{1,0:T(8,128)(2,1)S(1)}, u32[]{:S(2)}, u32[]{:S(2)}) collective-permute-start(bf16[64,4224]{1,0:T(8,128)(2,1)S(1)} %relay.33.refs_1_.refs_3_), channel_id=1, source_target_pairs={{4,0},{8,4},{12,8},{1,5},{5,9},{9,13},{6,2},{10,6},{14,10},{3,7},{... | collective-permute-start | bytes 1622024 | tf_op jit(solution)/shard_map/ppermute | solution.py:780
  65.6 20.6 %collective-permute-start.10 = (bf16[64,4224]{1,0:T(8,128)(2,1)S(1)}, bf16[64,4224]{1,0:T(8,128)(2,1)S(1)}, u32[]{:S(2)}, u32[]{:S(2)}) collective-permute-start(bf16[64,4224]{1,0:T(8,128)(2,1)S(1)} %relay.34.refs_3_), channel_id=1, source_target_pairs={{0,4},{4,8},{8,12},{5,1},{9,5},{13,9},{2,6},{6,10},{10,14},{7,3},{... | collective-permute-start | bytes 1622024 | tf_op jit(solution)/shard_map/ppermute | solution.py:780
  106.5 22.3 %collective-permute-start.18 = (bf16[64,4224]{1,0:T(8,128)(2,1)S(1)}, bf16[64,4224]{1,0:T(8,128)(2,1)S(1)}, u32[]{:S(2)}, u32[]{:S(2)}) collective-permute-start(bf16[64,4224]{1,0:T(8,128)(2,1)S(1)} %get-tuple-element.104.refs_4_), channel_id=1, source_target_pairs={{0,4},{4,8},{8,12},{5,1},{9,5},{13,9},{2,6},{6,10},{10,14},{7,3},{... | collective-permute-start | bytes 1622024 | tf_op jit(solution)/shard_map/ppermute | solution.py:780
  111.7 22.2 %collective-permute-start.17 = (bf16[64,4224]{1,0:T(8,128)(2,1)S(1)}, bf16[64,4224]{1,0:T(8,128)(2,1)S(1)}, u32[]{:S(2)}, u32[]{:S(2)}) collective-permute-start(bf16[64,4224]{1,0:T(8,128)(2,1)S(1)} %get-tuple-element.105.refs_1_.refs_4_), channel_id=1, source_target_pairs={{4,0},{8,4},{12,8},{1,5},{5,9},{9,13},{6,2},{10,6},{14,10},{3,7},{... | collective-permute-start | bytes 1622024 | tf_op jit(solution)/shard_map/ppermute | solution.py:780
  118.1 22.3 %collective-permute-start.15 = (bf16[64,4224]{1,0:T(8,128)(2,1)S(1)}, bf16[64,4224]{1,0:T(8,128)(2,1)S(1)}, u32[]{:S(2)}, u32[]{:S(2)}) collective-permute-start(bf16[64,4224]{1,0:T(8,128)(2,1)S(1)} %get-tuple-element.109.refs_4_), channel_id=1, source_target_pairs={{0,4},{4,8},{8,12},{5,1},{9,5},{13,9},{2,6},{6,10},{10,14},{7,3},{... | collective-permute-start | bytes 1622024 | tf_op jit(solution)/shard_map/ppermute | solution.py:780
  123.1 22.4 %collective-permute-start.20 = (bf16[64,4224]{1,0:T(8,128)(2,1)S(1)}, bf16[64,4224]{1,0:T(8,128)(2,1)S(1)}, u32[]{:S(2)}, u32[]{:S(2)}) collective-permute-start(bf16[64,4224]{1,0:T(8,128)(2,1)S(1)} %get-tuple-element.113.refs_4_), channel_id=1, source_target_pairs={{4,0},{8,4},{12,8},{1,5},{5,9},{9,13},{6,2},{10,6},{14,10},{3,7},{... | collective-permute-start | bytes 1622024 | tf_op jit(solution)/shard_map/ppermute | solution.py:780
  129.5 23.0 %collective-permute-start.22 = (bf16[64,4224]{1,0:T(8,128)(2,1)S(1)}, bf16[64,4224]{1,0:T(8,128)(2,1)S(1)}, u32[]{:S(2)}, u32[]{:S(2)}) collective-permute-start(bf16[64,4224]{1,0:T(8,128)(2,1)S(1)} %get-tuple-element.115.refs_4_), channel_id=1, source_target_pairs={{0,4},{4,8},{8,12},{5,1},{9,5},{13,9},{2,6},{6,10},{10,14},{7,3},{... | collective-permute-start | bytes 1622024 | tf_op jit(solution)/shard_map/ppermute | solution.py:780
  134.6 23.2 %collective-permute-start.21 = (bf16[64,4224]{1,0:T(8,128)(2,1)S(1)}, bf16[64,4224]{1,0:T(8,128)(2,1)S(1)}, u32[]{:S(2)}, u32[]{:S(2)}) collective-permute-start(bf16[64,4224]{1,0:T(8,128)(2,1)S(1)} %get-tuple-element.116.refs_4_), channel_id=1, source_target_pairs={{4,0},{8,4},{12,8},{1,5},{5,9},{9,13},{6,2},{10,6},{14,10},{3,7},{... | collective-permute-start | bytes 1622024 | tf_op jit(solution)/shard_map/ppermute | solution.py:780
  141.1 22.5 %collective-permute-start.19 = (bf16[64,4224]{1,0:T(8,128)(2,1)S(1)}, bf16[64,4224]{1,0:T(8,128)(2,1)S(1)}, u32[]{:S(2)}, u32[]{:S(2)}) collective-permute-start(bf16[64,4224]{1,0:T(8,128)(2,1)S(1)} %get-tuple-element.117.refs_4_), channel_id=1, source_target_pairs={{0,4},{4,8},{8,12},{5,1},{9,5},{13,9},{2,6},{6,10},{10,14},{7,3},{... | collective-permute-start | bytes 1622024 | tf_op jit(solution)/shard_map/ppermute | solution.py:780
  146.2 21.7 %collective-permute-start.24 = (bf16[64,4224]{1,0:T(8,128)(2,1)S(1)}, bf16[64,4224]{1,0:T(8,128)(2,1)S(1)}, u32[]{:S(2)}, u32[]{:S(2)}) collective-permute-start(bf16[64,4224]{1,0:T(8,128)(2,1)S(1)} %get-tuple-element.120.refs_2_.refs_4_), channel_id=1, source_target_pairs={{4,0},{8,4},{12,8},{1,5},{5,9},{9,13},{6,2},{10,6},{14,10},{3,7},{... | collective-permute-start | bytes 1622024 | tf_op jit(solution)/shard_map/ppermute | solution.py:780
  153.2 34.6 %collective-permute-start.26 = (bf16[64,4224]{1,0:T(8,128)(2,1)S(1)}, bf16[64,4224]{1,0:T(8,128)(2,1)S(1)}, u32[]{:S(2)}, u32[]{:S(2)}) collective-permute-start(bf16[64,4224]{1,0:T(8,128)(2,1)S(1)} %get-tuple-element.124.refs_4_), channel_id=1, source_target_pairs={{0,4},{4,8},{8,12},{5,1},{9,5},{13,9},{2,6},{6,10},{10,14},{7,3},{... | collective-permute-start | bytes 1622024 | tf_op jit(solution)/shard_map/ppermute | solution.py:780
  158.4 29.3 %collective-permute-start.27 = (bf16[64,4224]{1,0:T(8,128)(2,1)S(1)}, bf16[64,4224]{1,0:T(8,128)(2,1)S(1)}, u32[]{:S(2)}, u32[]{:S(2)}) collective-permute-start(bf16[64,4224]{1,0:T(8,128)(2,1)S(1)} %get-tuple-element.125.refs_4_), channel_id=1, source_target_pairs={{4,0},{8,4},{12,8},{1,5},{5,9},{9,13},{6,2},{10,6},{14,10},{3,7},{... | collective-permute-start | bytes 1622024 | tf_op jit(solution)/shard_map/ppermute | solution.py:780
  168.6 20.3 %collective-permute-start.25 = (bf16[64,4224]{1,0:T(8,128)(2,1)S(1)}, bf16[64,4224]{1,0:T(8,128)(2,1)S(1)}, u32[]{:S(2)}, u32[]{:S(2)}) collective-permute-start(bf16[64,4224]{1,0:T(8,128)(2,1)S(1)} %get-tuple-element.128.refs_0_), channel_id=1, source_target_pairs={{4,0},{8,4},{12,8},{1,5},{5,9},{9,13},{6,2},{10,6},{14,10},{3,7},{... | collective-permute-start | bytes 1622024 | tf_op jit(solution)/shard_map/ppermute | solution.py:780
  169.9 19.0 %collective-permute-start.23 = (bf16[64,4224]{1,0:T(8,128)(2,1)S(1)}, bf16[64,4224]{1,0:T(8,128)(2,1)S(1)}, u32[]{:S(2)}, u32[]{:S(2)}) collective-permute-start(bf16[64,4224]{1,0:T(8,128)(2,1)S(1)} %get-tuple-element.126.refs_4_), channel_id=1, source_target_pairs={{0,4},{4,8},{8,12},{5,1},{9,5},{13,9},{2,6},{6,10},{10,14},{7,3},{... | collective-permute-start | bytes 1622024 | tf_op jit(solution)/shard_map/ppermute | solution.py:780
  211.5 25.4 %collective-permute-start.33 = (bf16[64,4224]{1,0:T(8,128)(2,1)S(1)}, bf16[64,4224]{1,0:T(8,128)(2,1)S(1)}, u32[]{:S(2)}, u32[]{:S(2)}) collective-permute-start(bf16[64,4224]{1,0:T(8,128)(2,1)S(1)} %get-tuple-element.143.x_ref.refs_3_), channel_id=1, source_target_pairs={{4,0},{8,4},{5,9},{9,13},{6,2},{10,6},{7,11},{11,15},{20,16},{24,2... | collective-permute-start | bytes 1622024 | tf_op jit(solution)/shard_map/ppermute | solution.py:780
  226.0 22.5 %collective-permute-start.36 = (bf16[64,4224]{1,0:T(8,128)(2,1)S(1)}, bf16[64,4224]{1,0:T(8,128)(2,1)S(1)}, u32[]{:S(2)}, u32[]{:S(2)}) collective-permute-start(bf16[64,4224]{1,0:T(8,128)(2,1)S(1)} %get-tuple-element.148.x_ref.refs_3_), channel_id=1, source_target_pairs={{4,0},{8,4},{5,9},{9,13},{6,2},{10,6},{7,11},{11,15},{20,16},{24,2... | collective-permute-start | bytes 1622024 | tf_op jit(solution)/shard_map/ppermute | solution.py:780
  228.1 28.6 %collective-permute-start.38 = (bf16[64,4224]{1,0:T(8,128)(2,1)S(1)}, bf16[64,4224]{1,0:T(8,128)(2,1)S(1)}, u32[]{:S(2)}, u32[]{:S(2)}) collective-permute-start(bf16[64,4224]{1,0:T(8,128)(2,1)S(1)} %get-tuple-element.150.x_ref.refs_3_), channel_id=1, source_target_pairs={{8,12},{5,1},{10,14},{7,3},{24,28},{21,17},{26,30},{23,19}} | collective-permute-start | bytes 1622024 | tf_op jit(solution)/shard_map/ppermute | solution.py:780
  237.6 22.5 %collective-permute-start.39 = (bf16[64,4224]{1,0:T(8,128)(2,1)S(1)}, bf16[64,4224]{1,0:T(8,128)(2,1)S(1)}, u32[]{:S(2)}, u32[]{:S(2)}) collective-permute-start(bf16[64,4224]{1,0:T(8,128)(2,1)S(1)} %get-tuple-element.151.x_ref.refs_3_), channel_id=1, source_target_pairs={{4,0},{9,13},{6,2},{11,15},{20,16},{25,29},{22,18},{27,31}} | collective-permute-start | bytes 1622024 | tf_op jit(solution)/shard_map/ppermute | solution.py:780
  239.6 29.2 %collective-permute-start.35 = (bf16[64,4224]{1,0:T(8,128)(2,1)S(1)}, bf16[64,4224]{1,0:T(8,128)(2,1)S(1)}, u32[]{:S(2)}, u32[]{:S(2)}) collective-permute-start(bf16[64,4224]{1,0:T(8,128)(2,1)S(1)} %get-tuple-element.152.x_ref.refs_3_), channel_id=1, source_target_pairs={{8,12},{5,1},{10,14},{7,3},{24,28},{21,17},{26,30},{23,19}} | collective-permute-start | bytes 1622024 | tf_op jit(solution)/shard_map/ppermute | solution.py:780
  249.2 24.5 %collective-permute-start.37 = (bf16[64,4224]{1,0:T(8,128)(2,1)S(1)}, bf16[64,4224]{1,0:T(8,128)(2,1)S(1)}, u32[]{:S(2)}, u32[]{:S(2)}) collective-permute-start(bf16[64,4224]{1,0:T(8,128)(2,1)S(1)} %get-tuple-element.154.refs_5_), channel_id=1, source_target_pairs={{4,0},{9,13},{6,2},{11,15},{20,16},{25,29},{22,18},{27,31}} | collective-permute-start | bytes 1622024 | tf_op jit(solution)/shard_map/ppermute | solution.py:780
  (29 other events, 387.3 us)

commit v5 on v4

--- a/solution.py
+++ b/solution.py
@@ -80,7 +80,7 @@
     parts, _, rows, depth = by_share.shape
     half = w_out.shape[1] // halves
     span = half // pieces
-    cols = divisor(span, max(256, span // 4))
+    cols = divisor(span, max(256, span // 8))
     steps = span // cols
     base = half_at * half + piece * span
 

time: 284 us -> 285 us (level)
  no operation moved by 1% of the time
where the time goes in v5:
time: 285 us; the launch traced here: 283 us
  Pallas kernels  123 us (43%)
  starting transfers between devices  97.6 us (34%)
  waiting for transfers between devices  60.8 us (21%)
    ppermute x40, starting transfers between devices, body(): lax.ppermute(x, ('tensor', 'query'), pairs(flow, 0 if reduce_now else k,...  93.7 us
    ppermute x40, waiting for transfers between devices, body(): lax.ppermute(x, ('tensor', 'query'), pairs(flow, 0 if reduce_now else k,...  60.8 us
    pallas_call x7, Pallas kernels, forward_piece(): pl.pallas_call(kernel, grid=(steps,), in_specs=[pl.BlockSpec((parts, None...  38.8 us
    pallas_call x4, Pallas kernels, backward_piece(): pl.pallas_call(kernel, grid=(1,), in_specs=[pl.BlockSpec((parts, rows, ha...  25.5 us
    pallas_call x28, Pallas kernels, relay(): pl.pallas_call(kernel, grid_spec=pltpu.PrefetchScalarGridSpec(num_scalar_...  18.4 us
    pallas_call x4, Pallas kernels, load_weights(): pl.pallas_call(kernel, in_specs=[ANY] * (1 + len(after)), out_specs=pl.Bl...  16.6 us
    pallas_call x4, Pallas kernels, norm_out(): pl.pallas_call(kernel, grid_spec=pltpu.PrefetchScalarGridSpec(num_scalar_...  6.77 us
  transfers between devices with their start and end apart: 44, of which 14 were waited for; matrix products, arithmetic and copies ran while one was open for 0% of the time, Pallas kernels for 37%

profile of v5, /device:TPU:0, one launch (start us, length us, event | category | flops | bytes accessed | tf_op | source)
XLA Modules:
  0.0 283.2 jit_solution(630906827805894852)
XLA Ops:
  0.6 9.7 %forward_piece.7 = (bf16[4,64,4224]{2,1,0:T(8,128)(2,1)S(1)}, f32[8,128]{1,0:T(8,128)}) custom-call(bf16[4,2,64,2048]{3,2,1,0:T(8,128)(2,1)} %bitcast.8, bf16[2048,8192]{1,0:T(8,128)(2,1)} %w_ref.21), custom_call_target="tpu_custom_call" | custom-call | bytes 720000 | tf_op jit(solution)/shard_map/forward_piece/pallas_call | solution.py:107
  11.0 5.1 %collective-permute-start.3 = (bf16[64,4224]{1,0:T(8,128)(2,1)S(1)}, bf16[64,4224]{1,0:T(8,128)(2,1)S(1)}, u32[]{:S(2)}, u32[]{:S(2)}) collective-permute-start(bf16[64,4224]{1,0:T(8,128)(2,1)S(1)} %first_block.7), channel_id=1, source_target_pairs={{0,4},{13,9},{2,6},{15,11},{16,20},{29,25},{18,22},{31,27}} | collective-permute-start | bytes 1622024 | tf_op jit(solution)/shard_map/ppermute | solution.py:780
  17.6 7.9 %forward_piece.8 = (bf16[4,64,4224]{2,1,0:T(8,128)(2,1)S(1)}, f32[8,128]{1,0:T(8,128)S(1)}) custom-call(bf16[4,2,64,2048]{3,2,1,0:T(8,128)(2,1)S(1)} %bitcast.9, bf16[2048,8192]{1,0:T(8,128)(2,1)} %w_ref.21, bf16[64,4224]{1,0:T(8,128)(2,1)S(1)} %first_block.4.refs_0_), custom_call_target="tpu_custom_call" | custom-call | bytes 720000 | tf_op jit(solution)/shard_map/forward_piece/pallas_call | solution.py:107
  34.8 5.6 %collective-permute-done.1.refs_0_ = bf16[64,4224]{1,0:T(8,128)(2,1)S(1)} collective-permute-done((bf16[64,4224]{1,0:T(8,128)(2,1)S(1)}, bf16[64,4224]{1,0:T(8,128)(2,1)S(1)}, u32[]{:S(2)}, u32[]{:S(2)}) %collective-permute-start.1) | collective-permute-done | bytes 540704 | tf_op jit(solution)/shard_map/ppermute | solution.py:780
  52.7 4.4 %collective-permute-start.6 = (bf16[64,4224]{1,0:T(8,128)(2,1)S(1)}, bf16[64,4224]{1,0:T(8,128)(2,1)S(1)}, u32[]{:S(2)}, u32[]{:S(2)}) collective-permute-start(bf16[64,4224]{1,0:T(8,128)(2,1)S(1)} %relay.32.refs_3_), channel_id=1, source_target_pairs={{0,4},{4,8},{8,12},{5,1},{9,5},{13,9},{2,6},{6,10},{10,14},{7,3},{... | collective-permute-start | bytes 1622024 | tf_op jit(solution)/shard_map/ppermute | solution.py:780
  66.2 5.2 %collective-permute-start.10 = (bf16[64,4224]{1,0:T(8,128)(2,1)S(1)}, bf16[64,4224]{1,0:T(8,128)(2,1)S(1)}, u32[]{:S(2)}, u32[]{:S(2)}) collective-permute-start(bf16[64,4224]{1,0:T(8,128)(2,1)S(1)} %relay.34.refs_3_), channel_id=1, source_target_pairs={{0,4},{4,8},{8,12},{5,1},{9,5},{13,9},{2,6},{6,10},{10,14},{7,3},{... | collective-permute-start | bytes 1622024 | tf_op jit(solution)/shard_map/ppermute | solution.py:780
  73.0 7.9 %forward_piece.11 = (bf16[4,64,4224]{2,1,0:T(8,128)(2,1)S(1)}, f32[8,128]{1,0:T(8,128)S(1)}) custom-call(bf16[4,2,64,2048]{3,2,1,0:T(8,128)(2,1)S(1)} %bitcast.13, bf16[2048,8192]{1,0:T(8,128)(2,1)} %w_ref.21, bf16[64,8192]{1,0:T(8,128)(2,1)S(1)} %get-tuple-element.90.refs_0_.refs_3_.refs_9_), custom_call_target="tpu_custom_call" | custom-call | bytes 720000 | tf_op jit(solution)/shard_map/forward_piece/pallas_call | solution.py:107
  82.1 4.7 %collective-permute-done.10.refs_1_.refs_7_ = bf16[64,4224]{1,0:T(8,128)(2,1)S(1)} collective-permute-done((bf16[64,4224]{1,0:T(8,128)(2,1)S(1)}, bf16[64,4224]{1,0:T(8,128)(2,1)S(1)}, u32[]{:S(2)}, u32[]{:S(2)}) %collective-permute-start.10) | collective-permute-done | bytes 540704 | tf_op jit(solution)/shard_map/ppermute | solution.py:780
  90.2 4.4 %collective-permute-start.13 = (bf16[64,4224]{1,0:T(8,128)(2,1)S(1)}, bf16[64,4224]{1,0:T(8,128)(2,1)S(1)}, u32[]{:S(2)}, u32[]{:S(2)}) collective-permute-start(bf16[64,4224]{1,0:T(8,128)(2,1)S(1)} %get-tuple-element.97.refs_1_), channel_id=1, source_target_pairs={{0,4},{4,8},{8,12},{5,1},{9,5},{13,9},{2,6},{6,10},{10,14},{7,3},{... | collective-permute-start | bytes 1622024 | tf_op jit(solution)/shard_map/ppermute | solution.py:780
  100.5 4.6 %collective-permute-start.14 = (bf16[64,4224]{1,0:T(8,128)(2,1)S(1)}, bf16[64,4224]{1,0:T(8,128)(2,1)S(1)}, u32[]{:S(2)}, u32[]{:S(2)}) collective-permute-start(bf16[64,4224]{1,0:T(8,128)(2,1)S(1)} %get-tuple-element.102.refs_4_), channel_id=1, source_target_pairs={{0,4},{4,8},{8,12},{5,1},{9,5},{13,9},{2,6},{6,10},{10,14},{7,3},{... | collective-permute-start | bytes 1622024 | tf_op jit(solution)/shard_map/ppermute | solution.py:780
  107.1 4.5 %collective-permute-start.18 = (bf16[64,4224]{1,0:T(8,128)(2,1)S(1)}, bf16[64,4224]{1,0:T(8,128)(2,1)S(1)}, u32[]{:S(2)}, u32[]{:S(2)}) collective-permute-start(bf16[64,4224]{1,0:T(8,128)(2,1)S(1)} %get-tuple-element.104.refs_4_), channel_id=1, source_target_pairs={{0,4},{4,8},{8,12},{5,1},{9,5},{13,9},{2,6},{6,10},{10,14},{7,3},{... | collective-permute-start | bytes 1622024 | tf_op jit(solution)/shard_map/ppermute | solution.py:780
  124.8 4.5 %collective-permute-done.18.refs_0_ = bf16[64,4224]{1,0:T(8,128)(2,1)S(1)} collective-permute-done((bf16[64,4224]{1,0:T(8,128)(2,1)S(1)}, bf16[64,4224]{1,0:T(8,128)(2,1)S(1)}, u32[]{:S(2)}, u32[]{:S(2)}) %collective-permute-start.18) | collective-permute-done | bytes 540704 | tf_op jit(solution)/shard_map/ppermute | solution.py:780
  136.5 4.5 %collective-permute-done.15.refs_0_ = bf16[64,4224]{1,0:T(8,128)(2,1)S(1)} collective-permute-done((bf16[64,4224]{1,0:T(8,128)(2,1)S(1)}, bf16[64,4224]{1,0:T(8,128)(2,1)S(1)}, u32[]{:S(2)}, u32[]{:S(2)}) %collective-permute-start.15) | collective-permute-done | bytes 540704 | tf_op jit(solution)/shard_map/ppermute | solution.py:780
  153.9 4.6 %collective-permute-start.26 = (bf16[64,4224]{1,0:T(8,128)(2,1)S(1)}, bf16[64,4224]{1,0:T(8,128)(2,1)S(1)}, u32[]{:S(2)}, u32[]{:S(2)}) collective-permute-start(bf16[64,4224]{1,0:T(8,128)(2,1)S(1)} %get-tuple-element.124.refs_4_), channel_id=1, source_target_pairs={{0,4},{4,8},{8,12},{5,1},{9,5},{13,9},{2,6},{6,10},{10,14},{7,3},{... | collective-permute-start | bytes 1622024 | tf_op jit(solution)/shard_map/ppermute | solution.py:780
  170.5 4.6 %collective-permute-start.23 = (bf16[64,4224]{1,0:T(8,128)(2,1)S(1)}, bf16[64,4224]{1,0:T(8,128)(2,1)S(1)}, u32[]{:S(2)}, u32[]{:S(2)}) collective-permute-start(bf16[64,4224]{1,0:T(8,128)(2,1)S(1)} %get-tuple-element.126.refs_4_), channel_id=1, source_target_pairs={{0,4},{4,8},{8,12},{5,1},{9,5},{13,9},{2,6},{6,10},{10,14},{7,3},{... | collective-permute-start | bytes 1622024 | tf_op jit(solution)/shard_map/ppermute | solution.py:780
  181.9 6.4 %load_weights.7.refs_6_.refs_8_.refs_3_.refs_4_ = bf16[512,8192]{1,0:T(8,128)(2,1)S(1)} custom-call(bf16[2048,8192]{1,0:T(8,128)(2,1)} %w_ref.21, bf16[512,8192]{1,0:T(8,128)(2,1)S(1)} %load_weights.6.refs_0_.refs_2_.refs_3_), custom_call_target="tpu_custom_call" | custom-call | bytes 720000 | tf_op jit(solution)/shard_map/load_weights/pallas_call | solution.py:139
  196.9 6.2 %backward_piece.4 = (bf16[4,2,64,2048]{3,2,1,0:T(8,128)(2,1)}, f32[8,128]{1,0:T(8,128)S(1)}) custom-call(bf16[4,64,4224]{2,1,0:T(8,128)(2,1)S(1)} %get-tuple-element.134.refs_0_, bf16[4,64,4224]{2,1,0:T(8,128)(2,1)S(1)} %get-tuple-element.135.refs_1_, bf16[512,8192]{1,0:T(8,128)(2,1)S(1)} %load_weights.4.refs_3_.refs_2_.refs_1_, ...), custom_call_target="tpu_custom_call" | custom-call | bytes 720000 | tf_op jit(solution)/shard_map/backward_piece/pallas_call | solution.py:215
  204.2 4.6 %collective-permute-start.28 = (bf16[64,4224]{1,0:T(8,128)(2,1)S(1)}, bf16[64,4224]{1,0:T(8,128)(2,1)S(1)}, u32[]{:S(2)}, u32[]{:S(2)}) collective-permute-start(bf16[64,4224]{1,0:T(8,128)(2,1)S(1)} %get-tuple-element.138.x_ref.refs_3_), channel_id=1, source_target_pairs={{0,4},{4,8},{8,12},{5,1},{9,5},{13,9},{2,6},{6,10},{10,14},{7,3},{... | collective-permute-start | bytes 1622024 | tf_op jit(solution)/shard_map/ppermute | solution.py:780
  213.4 7.1 %collective-permute-done.28.refs_0_ = bf16[64,4224]{1,0:T(8,128)(2,1)S(1)} collective-permute-done((bf16[64,4224]{1,0:T(8,128)(2,1)S(1)}, bf16[64,4224]{1,0:T(8,128)(2,1)S(1)}, u32[]{:S(2)}, u32[]{:S(2)}) %collective-permute-start.28) | collective-permute-done | bytes 540704 | tf_op jit(solution)/shard_map/ppermute | solution.py:780
  229.4 8.2 %collective-permute-done.33.refs_0_ = bf16[64,4224]{1,0:T(8,128)(2,1)S(1)} collective-permute-done((bf16[64,4224]{1,0:T(8,128)(2,1)S(1)}, bf16[64,4224]{1,0:T(8,128)(2,1)S(1)}, u32[]{:S(2)}, u32[]{:S(2)}) %collective-permute-start.33) | collective-permute-done | bytes 540704 | tf_op jit(solution)/shard_map/ppermute | solution.py:780
  240.9 8.2 %collective-permute-done.36.refs_0_ = bf16[64,4224]{1,0:T(8,128)(2,1)S(1)} collective-permute-done((bf16[64,4224]{1,0:T(8,128)(2,1)S(1)}, bf16[64,4224]{1,0:T(8,128)(2,1)S(1)}, u32[]{:S(2)}, u32[]{:S(2)}) %collective-permute-start.36) | collective-permute-done | bytes 540704 | tf_op jit(solution)/shard_map/ppermute | solution.py:780
  251.1 6.2 %backward_piece.5 = (bf16[4,2,64,2048]{3,2,1,0:T(8,128)(2,1)}, f32[8,128]{1,0:T(8,128)S(1)}) custom-call(bf16[4,64,4224]{2,1,0:T(8,128)(2,1)S(1)} %get-tuple-element.134.refs_0_, bf16[4,64,4224]{2,1,0:T(8,128)(2,1)S(1)} %get-tuple-element.135.refs_1_, bf16[512,8192]{1,0:T(8,128)(2,1)S(1)} %bitcast.7, ...), custom_call_target="tpu_custom_call", output_to_operand_aliasing={{0}: (4, {})} | custom-call | bytes 720000 | tf_op jit(solution)/shard_map/backward_piece/pallas_call | solution.py:215
  263.4 6.1 %backward_piece.6 = (f32[4,64,2048]{2,1,0:T(8,128)S(1)}, f32[8,128]{1,0:T(8,128)S(1)}) custom-call(bf16[4,64,4224]{2,1,0:T(8,128)(2,1)S(1)} %store_last.2.refs_1_.refs_0_, bf16[512,8192]{1,0:T(8,128)(2,1)S(1)} %load_weights.4.refs_3_.refs_2_.refs_1_, bf16[512,8192]{1,0:T(8,128)(2,1)S(1)} %load_weights.5.refs_0_.refs_3_.refs_2_, ...), custom_call_target="tpu_custom_call" | custom-call | bytes 720000 | tf_op jit(solution)/shard_map/backward_piece/pallas_call | solution.py:215
  274.9 7.1 %backward_piece.7 = (bf16[4,2,64,2048]{3,2,1,0:T(8,128)(2,1)}, f32[8,128]{1,0:T(8,128)S(1)}) custom-call(bf16[4,64,4224]{2,1,0:T(8,128)(2,1)S(1)} %store_last.3.refs_0_, bf16[512,8192]{1,0:T(8,128)(2,1)S(1)} %load_weights.4.refs_3_.refs_2_.refs_1_, bf16[512,8192]{1,0:T(8,128)(2,1)S(1)} %load_weights.5.refs_0_.refs_3_.refs_2_, ...), custom_call_target="tpu_custom_call", output_to_operand_aliasing={{0}: (6, {})} | custom-call | bytes 720000 | tf_op jit(solution)/shard_map/backward_piece/pallas_call | solution.py:215
  (159 shorter events, 139.3 us)
Async XLA Ops:
  30.0 22.0 %collective-permute-start.5 = (bf16[64,4224]{1,0:T(8,128)(2,1)S(1)}, bf16[64,4224]{1,0:T(8,128)(2,1)S(1)}, u32[]{:S(2)}, u32[]{:S(2)}) collective-permute-start(bf16[64,4224]{1,0:T(8,128)(2,1)S(1)} %relay.28.refs_3_), channel_id=1, source_target_pairs={{0,4},{4,8},{9,5},{13,9},{2,6},{6,10},{11,7},{15,11},{16,20},{20,2... | collective-permute-start | bytes 1622024 | tf_op jit(solution)/shard_map/ppermute | solution.py:780
  34.1 23.0 %collective-permute-start.4 = (bf16[64,4224]{1,0:T(8,128)(2,1)S(1)}, bf16[64,4224]{1,0:T(8,128)(2,1)S(1)}, u32[]{:S(2)}, u32[]{:S(2)}) collective-permute-start(bf16[64,4224]{1,0:T(8,128)(2,1)S(1)} %relay.29.refs_3_), channel_id=1, source_target_pairs={{8,4},{12,8},{1,5},{5,9},{10,6},{14,10},{3,7},{7,11},{24,20},{28,2... | collective-permute-start | bytes 1622024 | tf_op jit(solution)/shard_map/ppermute | solution.py:780
  41.1 22.5 %collective-permute-start.9 = (bf16[64,4224]{1,0:T(8,128)(2,1)S(1)}, bf16[64,4224]{1,0:T(8,128)(2,1)S(1)}, u32[]{:S(2)}, u32[]{:S(2)}) collective-permute-start(bf16[64,4224]{1,0:T(8,128)(2,1)S(1)} %relay.30.refs_3_), channel_id=1, source_target_pairs={{0,4},{4,8},{9,5},{13,9},{2,6},{6,10},{11,7},{15,11},{16,20},{20,2... | collective-permute-start | bytes 1622024 | tf_op jit(solution)/shard_map/ppermute | solution.py:780
  52.7 28.2 %collective-permute-start.6 = (bf16[64,4224]{1,0:T(8,128)(2,1)S(1)}, bf16[64,4224]{1,0:T(8,128)(2,1)S(1)}, u32[]{:S(2)}, u32[]{:S(2)}) collective-permute-start(bf16[64,4224]{1,0:T(8,128)(2,1)S(1)} %relay.32.refs_3_), channel_id=1, source_target_pairs={{0,4},{4,8},{8,12},{5,1},{9,5},{13,9},{2,6},{6,10},{10,14},{7,3},{... | collective-permute-start | bytes 1622024 | tf_op jit(solution)/shard_map/ppermute | solution.py:780
  57.8 23.2 %collective-permute-start.7 = (bf16[64,4224]{1,0:T(8,128)(2,1)S(1)}, bf16[64,4224]{1,0:T(8,128)(2,1)S(1)}, u32[]{:S(2)}, u32[]{:S(2)}) collective-permute-start(bf16[64,4224]{1,0:T(8,128)(2,1)S(1)} %relay.33.refs_1_.refs_3_), channel_id=1, source_target_pairs={{4,0},{8,4},{12,8},{1,5},{5,9},{9,13},{6,2},{10,6},{14,10},{3,7},{... | collective-permute-start | bytes 1622024 | tf_op jit(solution)/shard_map/ppermute | solution.py:780
  66.2 20.6 %collective-permute-start.10 = (bf16[64,4224]{1,0:T(8,128)(2,1)S(1)}, bf16[64,4224]{1,0:T(8,128)(2,1)S(1)}, u32[]{:S(2)}, u32[]{:S(2)}) collective-permute-start(bf16[64,4224]{1,0:T(8,128)(2,1)S(1)} %relay.34.refs_3_), channel_id=1, source_target_pairs={{0,4},{4,8},{8,12},{5,1},{9,5},{13,9},{2,6},{6,10},{10,14},{7,3},{... | collective-permute-start | bytes 1622024 | tf_op jit(solution)/shard_map/ppermute | solution.py:780
  107.1 22.3 %collective-permute-start.18 = (bf16[64,4224]{1,0:T(8,128)(2,1)S(1)}, bf16[64,4224]{1,0:T(8,128)(2,1)S(1)}, u32[]{:S(2)}, u32[]{:S(2)}) collective-permute-start(bf16[64,4224]{1,0:T(8,128)(2,1)S(1)} %get-tuple-element.104.refs_4_), channel_id=1, source_target_pairs={{0,4},{4,8},{8,12},{5,1},{9,5},{13,9},{2,6},{6,10},{10,14},{7,3},{... | collective-permute-start | bytes 1622024 | tf_op jit(solution)/shard_map/ppermute | solution.py:780
  112.3 22.2 %collective-permute-start.17 = (bf16[64,4224]{1,0:T(8,128)(2,1)S(1)}, bf16[64,4224]{1,0:T(8,128)(2,1)S(1)}, u32[]{:S(2)}, u32[]{:S(2)}) collective-permute-start(bf16[64,4224]{1,0:T(8,128)(2,1)S(1)} %get-tuple-element.105.refs_1_.refs_4_), channel_id=1, source_target_pairs={{4,0},{8,4},{12,8},{1,5},{5,9},{9,13},{6,2},{10,6},{14,10},{3,7},{... | collective-permute-start | bytes 1622024 | tf_op jit(solution)/shard_map/ppermute | solution.py:780
  118.5 22.5 %collective-permute-start.15 = (bf16[64,4224]{1,0:T(8,128)(2,1)S(1)}, bf16[64,4224]{1,0:T(8,128)(2,1)S(1)}, u32[]{:S(2)}, u32[]{:S(2)}) collective-permute-start(bf16[64,4224]{1,0:T(8,128)(2,1)S(1)} %get-tuple-element.109.refs_4_), channel_id=1, source_target_pairs={{0,4},{4,8},{8,12},{5,1},{9,5},{13,9},{2,6},{6,10},{10,14},{7,3},{... | collective-permute-start | bytes 1622024 | tf_op jit(solution)/shard_map/ppermute | solution.py:780
  123.5 22.7 %collective-permute-start.20 = (bf16[64,4224]{1,0:T(8,128)(2,1)S(1)}, bf16[64,4224]{1,0:T(8,128)(2,1)S(1)}, u32[]{:S(2)}, u32[]{:S(2)}) collective-permute-start(bf16[64,4224]{1,0:T(8,128)(2,1)S(1)} %get-tuple-element.113.refs_4_), channel_id=1, source_target_pairs={{4,0},{8,4},{12,8},{1,5},{5,9},{9,13},{6,2},{10,6},{14,10},{3,7},{... | collective-permute-start | bytes 1622024 | tf_op jit(solution)/shard_map/ppermute | solution.py:780
  130.1 23.1 %collective-permute-start.22 = (bf16[64,4224]{1,0:T(8,128)(2,1)S(1)}, bf16[64,4224]{1,0:T(8,128)(2,1)S(1)}, u32[]{:S(2)}, u32[]{:S(2)}) collective-permute-start(bf16[64,4224]{1,0:T(8,128)(2,1)S(1)} %get-tuple-element.115.refs_4_), channel_id=1, source_target_pairs={{0,4},{4,8},{8,12},{5,1},{9,5},{13,9},{2,6},{6,10},{10,14},{7,3},{... | collective-permute-start | bytes 1622024 | tf_op jit(solution)/shard_map/ppermute | solution.py:780
  135.2 23.3 %collective-permute-start.21 = (bf16[64,4224]{1,0:T(8,128)(2,1)S(1)}, bf16[64,4224]{1,0:T(8,128)(2,1)S(1)}, u32[]{:S(2)}, u32[]{:S(2)}) collective-permute-start(bf16[64,4224]{1,0:T(8,128)(2,1)S(1)} %get-tuple-element.116.refs_4_), channel_id=1, source_target_pairs={{4,0},{8,4},{12,8},{1,5},{5,9},{9,13},{6,2},{10,6},{14,10},{3,7},{... | collective-permute-start | bytes 1622024 | tf_op jit(solution)/shard_map/ppermute | solution.py:780
  141.8 22.3 %collective-permute-start.19 = (bf16[64,4224]{1,0:T(8,128)(2,1)S(1)}, bf16[64,4224]{1,0:T(8,128)(2,1)S(1)}, u32[]{:S(2)}, u32[]{:S(2)}) collective-permute-start(bf16[64,4224]{1,0:T(8,128)(2,1)S(1)} %get-tuple-element.117.refs_4_), channel_id=1, source_target_pairs={{0,4},{4,8},{8,12},{5,1},{9,5},{13,9},{2,6},{6,10},{10,14},{7,3},{... | collective-permute-start | bytes 1622024 | tf_op jit(solution)/shard_map/ppermute | solution.py:780
  146.9 21.6 %collective-permute-start.24 = (bf16[64,4224]{1,0:T(8,128)(2,1)S(1)}, bf16[64,4224]{1,0:T(8,128)(2,1)S(1)}, u32[]{:S(2)}, u32[]{:S(2)}) collective-permute-start(bf16[64,4224]{1,0:T(8,128)(2,1)S(1)} %get-tuple-element.120.refs_2_.refs_4_), channel_id=1, source_target_pairs={{4,0},{8,4},{12,8},{1,5},{5,9},{9,13},{6,2},{10,6},{14,10},{3,7},{... | collective-permute-start | bytes 1622024 | tf_op jit(solution)/shard_map/ppermute | solution.py:780
  153.9 34.4 %collective-permute-start.26 = (bf16[64,4224]{1,0:T(8,128)(2,1)S(1)}, bf16[64,4224]{1,0:T(8,128)(2,1)S(1)}, u32[]{:S(2)}, u32[]{:S(2)}) collective-permute-start(bf16[64,4224]{1,0:T(8,128)(2,1)S(1)} %get-tuple-element.124.refs_4_), channel_id=1, source_target_pairs={{0,4},{4,8},{8,12},{5,1},{9,5},{13,9},{2,6},{6,10},{10,14},{7,3},{... | collective-permute-start | bytes 1622024 | tf_op jit(solution)/shard_map/ppermute | solution.py:780
  159.2 29.1 %collective-permute-start.27 = (bf16[64,4224]{1,0:T(8,128)(2,1)S(1)}, bf16[64,4224]{1,0:T(8,128)(2,1)S(1)}, u32[]{:S(2)}, u32[]{:S(2)}) collective-permute-start(bf16[64,4224]{1,0:T(8,128)(2,1)S(1)} %get-tuple-element.125.refs_4_), channel_id=1, source_target_pairs={{4,0},{8,4},{12,8},{1,5},{5,9},{9,13},{6,2},{10,6},{14,10},{3,7},{... | collective-permute-start | bytes 1622024 | tf_op jit(solution)/shard_map/ppermute | solution.py:780
  169.2 20.3 %collective-permute-start.25 = (bf16[64,4224]{1,0:T(8,128)(2,1)S(1)}, bf16[64,4224]{1,0:T(8,128)(2,1)S(1)}, u32[]{:S(2)}, u32[]{:S(2)}) collective-permute-start(bf16[64,4224]{1,0:T(8,128)(2,1)S(1)} %get-tuple-element.128.refs_0_), channel_id=1, source_target_pairs={{4,0},{8,4},{12,8},{1,5},{5,9},{9,13},{6,2},{10,6},{14,10},{3,7},{... | collective-permute-start | bytes 1622024 | tf_op jit(solution)/shard_map/ppermute | solution.py:780
  170.5 19.0 %collective-permute-start.23 = (bf16[64,4224]{1,0:T(8,128)(2,1)S(1)}, bf16[64,4224]{1,0:T(8,128)(2,1)S(1)}, u32[]{:S(2)}, u32[]{:S(2)}) collective-permute-start(bf16[64,4224]{1,0:T(8,128)(2,1)S(1)} %get-tuple-element.126.refs_4_), channel_id=1, source_target_pairs={{0,4},{4,8},{8,12},{5,1},{9,5},{13,9},{2,6},{6,10},{10,14},{7,3},{... | collective-permute-start | bytes 1622024 | tf_op jit(solution)/shard_map/ppermute | solution.py:780
  212.1 25.4 %collective-permute-start.33 = (bf16[64,4224]{1,0:T(8,128)(2,1)S(1)}, bf16[64,4224]{1,0:T(8,128)(2,1)S(1)}, u32[]{:S(2)}, u32[]{:S(2)}) collective-permute-start(bf16[64,4224]{1,0:T(8,128)(2,1)S(1)} %get-tuple-element.143.x_ref.refs_3_), channel_id=1, source_target_pairs={{4,0},{8,4},{5,9},{9,13},{6,2},{10,6},{7,11},{11,15},{20,16},{24,2... | collective-permute-start | bytes 1622024 | tf_op jit(solution)/shard_map/ppermute | solution.py:780
  226.6 22.5 %collective-permute-start.36 = (bf16[64,4224]{1,0:T(8,128)(2,1)S(1)}, bf16[64,4224]{1,0:T(8,128)(2,1)S(1)}, u32[]{:S(2)}, u32[]{:S(2)}) collective-permute-start(bf16[64,4224]{1,0:T(8,128)(2,1)S(1)} %get-tuple-element.148.x_ref.refs_3_), channel_id=1, source_target_pairs={{4,0},{8,4},{5,9},{9,13},{6,2},{10,6},{7,11},{11,15},{20,16},{24,2... | collective-permute-start | bytes 1622024 | tf_op jit(solution)/shard_map/ppermute | solution.py:780
  228.6 28.6 %collective-permute-start.38 = (bf16[64,4224]{1,0:T(8,128)(2,1)S(1)}, bf16[64,4224]{1,0:T(8,128)(2,1)S(1)}, u32[]{:S(2)}, u32[]{:S(2)}) collective-permute-start(bf16[64,4224]{1,0:T(8,128)(2,1)S(1)} %get-tuple-element.150.x_ref.refs_3_), channel_id=1, source_target_pairs={{8,12},{5,1},{10,14},{7,3},{24,28},{21,17},{26,30},{23,19}} | collective-permute-start | bytes 1622024 | tf_op jit(solution)/shard_map/ppermute | solution.py:780
  238.2 22.5 %collective-permute-start.39 = (bf16[64,4224]{1,0:T(8,128)(2,1)S(1)}, bf16[64,4224]{1,0:T(8,128)(2,1)S(1)}, u32[]{:S(2)}, u32[]{:S(2)}) collective-permute-start(bf16[64,4224]{1,0:T(8,128)(2,1)S(1)} %get-tuple-element.151.x_ref.refs_3_), channel_id=1, source_target_pairs={{4,0},{9,13},{6,2},{11,15},{20,16},{25,29},{22,18},{27,31}} | collective-permute-start | bytes 1622024 | tf_op jit(solution)/shard_map/ppermute | solution.py:780
  240.2 29.2 %collective-permute-start.35 = (bf16[64,4224]{1,0:T(8,128)(2,1)S(1)}, bf16[64,4224]{1,0:T(8,128)(2,1)S(1)}, u32[]{:S(2)}, u32[]{:S(2)}) collective-permute-start(bf16[64,4224]{1,0:T(8,128)(2,1)S(1)} %get-tuple-element.152.x_ref.refs_3_), channel_id=1, source_target_pairs={{8,12},{5,1},{10,14},{7,3},{24,28},{21,17},{26,30},{23,19}} | collective-permute-start | bytes 1622024 | tf_op jit(solution)/shard_map/ppermute | solution.py:780
  249.8 24.5 %collective-permute-start.37 = (bf16[64,4224]{1,0:T(8,128)(2,1)S(1)}, bf16[64,4224]{1,0:T(8,128)(2,1)S(1)}, u32[]{:S(2)}, u32[]{:S(2)}) collective-permute-start(bf16[64,4224]{1,0:T(8,128)(2,1)S(1)} %get-tuple-element.154.refs_5_), channel_id=1, source_target_pairs={{4,0},{9,13},{6,2},{11,15},{20,16},{25,29},{22,18},{27,31}} | collective-permute-start | bytes 1622024 | tf_op jit(solution)/shard_map/ppermute | solution.py:780
  (29 other events, 387.9 us)
